TPU v7x, 32 devices: a whole 2x2x4 slice. The times are simulated.
32 devices in a mesh: az: 2 (over y), ax: 16 (over z, x, core).
Axes of the slice: x: 2, y: 2, z: 4, core: 2. Of those that a mesh axis runs over, the one named last changes fastest.
Arguments:
- density: float32 [128, 32, 512], P('ax', 'az'), may hold values from 0.1 to 2
- courant_r: bfloat16 [128, 32, 512], P('ax', 'az'), may hold values from -0.19921875 to 0.19921875
- courant_t: bfloat16 [128, 32, 512], P('ax', 'az'), may hold values from -0.19921875 to 0.19921875
- courant_z: bfloat16 [128, 32, 512], P('ax', 'az'), may hold values from -0.19921875 to 0.19921875
- ionization: bfloat16 [128, 32, 512], P('ax', 'az'), may hold values from 0.0099487305 to 0.19921875
- send_block: int32 [2, 256, 2], P('az', 'ax'), may hold values from 0 to 16, as said below
- recv_slot: int32 [2, 384], P('az', 'ax'), may hold values from 0 to 31, as said below
Outputs:
- evolved: float32 [128, 32, 512], P('ax', 'az')
- fine_patches: float32 [2, 384, 8, 16, 256], P('az', 'ax')
Inputs may be any that keep to these rules, and one draw needn't show every extreme that they name: `send_block`: an entry is the local id (block_z * 8 + block_t * 4 + block_r) of a coarse block of the source device, with block_r 0 or 1, or 16 for an empty slot. Each (source, destination) pair carries 0 or exactly 2 blocks; the sources of one sector lie within 12 cyclically consecutive slabs. `recv_slot`: each owner's 24 patches name distinct non-empty slots of the blocks sent to that owner, as source * 2 + slot; every non-empty slot is named once.
All inputs are finite; a program needn't handle non-finite values.
Results may differ from a plain program's by a relative error of at most 0.0015.
Values may be sent and summed in bfloat16 or wider, within the bound.
No kernel may reach another device: no remote copies, remote signals or barrier semaphores. Data moves between devices by JAX's collectives and lax.ppermute only.
A program may use at most 128 MiB of HBM per device.

v0:
```python
import jax
import jax.numpy as jnp
from jax import lax
from jax.sharding import PartitionSpec as P

BZ = 4
BT = 8
BR = 128
CAP = 2


diffusion_number = 0.05


def passed_along(shard, axis, by):
    peers = lax.axis_size(axis)
    return lax.ppermute(shard, axis, [(i, (i + by) % peers) for i in range(peers)])


def shifted(value, axis, steps):
    count = lax.axis_size(axis)
    leading, last = (max(0, -steps), min(count, count - steps))
    return lax.ppermute(value, axis, [(source, source + steps) for source in range(leading, last)])


def with_halo(block, sides, width):
    for axis, dim in sides:
        count = lax.axis_size(axis)
        forward = [(i, i + 1) for i in range(count - 1)]
        forward.append((count - 1, 0))
        backward = [(target, source) for source, target in forward]
        low = lax.ppermute(
            lax.slice_in_dim(block, block.shape[dim] - width, None, axis=dim), axis, forward
        )
        high = lax.ppermute(lax.slice_in_dim(block, 0, width, axis=dim), axis, backward)
        block = jnp.concatenate([low, block, high], axis=dim)
    return block


def upwind_change(values, courant, axis_dim):
    length = values.shape[axis_dim]
    slopes = 0.5 * (
        lax.slice_in_dim(values, 2, length, axis=axis_dim)
        - lax.slice_in_dim(values, 0, length - 2, axis=axis_dim)
    )
    centre = lax.slice_in_dim(values, 1, length - 1, axis=axis_dim)
    face_count = length - 3
    upwind_left = lax.slice_in_dim(centre, 0, face_count, axis=axis_dim) + 0.5 * lax.slice_in_dim(
        slopes, 0, face_count, axis=axis_dim
    )
    upwind_right = lax.slice_in_dim(
        centre, 1, face_count + 1, axis=axis_dim
    ) - 0.5 * lax.slice_in_dim(slopes, 1, face_count + 1, axis=axis_dim)
    courant_f = courant.astype(jnp.float32)
    face_flux = (
        jnp.maximum(courant_f, 0.0) * upwind_left + jnp.minimum(courant_f, 0.0) * upwind_right
    )
    return lax.slice_in_dim(face_flux, 1, face_count, axis=axis_dim) - lax.slice_in_dim(
        face_flux, 0, face_count - 1, axis=axis_dim
    )


def section_rate(padded, across, radial_c, azim_c, axial_c, source):
    cells = padded[2:-2, 2:-2, :]
    azimuthal = upwind_change(padded[2:-2, :, :], azim_c, 1)
    axial_change = upwind_change(padded[:, 2:-2, :], axial_c, 0)
    axial_lap = padded[3:-1, 2:-2, :] + padded[1:-3, 2:-2, :] - 2.0 * cells
    radial_n = cells.shape[2]
    zero_col = jnp.zeros(cells.shape[:2] + (1,), jnp.float32)
    extended = jnp.concatenate([across[:, :, None], cells, zero_col, zero_col], axis=2)
    slopes = 0.5 * (extended[:, :, 2:] - extended[:, :, :-2])
    upwind_left = cells + 0.5 * slopes[:, :, :-1]
    upwind_right = extended[:, :, 2 : radial_n + 2] - 0.5 * slopes[:, :, 1:]
    courant_f = radial_c.astype(jnp.float32)
    face_flux = (
        jnp.maximum(courant_f, 0.0) * upwind_left + jnp.minimum(courant_f, 0.0) * upwind_right
    )
    radial_index = jnp.arange(radial_n, dtype=jnp.float32)
    face_area = jnp.where(radial_index < radial_n - 1, radial_index + 1.0, 0.0)
    radius = radial_index + 0.5
    carried = face_area * (
        diffusion_number * (extended[:, :, 2 : radial_n + 2] - cells) - face_flux
    )
    before = jnp.concatenate([zero_col, carried[:, :, :-1]], axis=2)
    radial = (carried - before) / radius
    return (
        radial
        - azimuthal
        - axial_change
        + diffusion_number * axial_lap
        + source.astype(jnp.float32) * cells
    )


def interp_matrix(coarse_count):
    fine_index = jnp.arange(2 * coarse_count, dtype=jnp.int32)
    parent = fine_index // 2
    neighbour = jnp.where(
        fine_index % 2 == 0, jnp.maximum(parent - 1, 0), jnp.minimum(parent + 1, coarse_count - 1)
    )
    columns = jnp.arange(coarse_count, dtype=jnp.int32)
    matrix = 0.75 * (parent[:, None] == columns[None, :]).astype(jnp.float32)
    return matrix + 0.25 * (neighbour[:, None] == columns[None, :]).astype(jnp.float32)


def prolong(blocks):
    spread = jnp.einsum(
        "pztr,Rr->pztR", blocks, interp_matrix(blocks.shape[3]), precision=lax.Precision.HIGHEST
    )
    spread = jnp.einsum(
        "pztR,Tt->pzTR", spread, interp_matrix(blocks.shape[2]), precision=lax.Precision.HIGHEST
    )
    return jnp.einsum(
        "pzTR,Zz->pZTR", spread, interp_matrix(blocks.shape[1]), precision=lax.Precision.HIGHEST
    )


def inside(margin, rows_z, ax_count):
    global_row = (
        lax.axis_index("ax") * rows_z - margin + jnp.arange(rows_z + 2 * margin, dtype=jnp.int32)
    )
    keep = (global_row >= 0) & (global_row < rows_z * ax_count)
    return keep.astype(jnp.float32)[:, None, None]


def local(density, courant_r, courant_t, courant_z, ionization, send_block, recv_slot):
    rows_z, cells_t, cells_r = density.shape
    ax_count = lax.axis_size("ax")
    half_cycle = lax.axis_size("az") // 2

    def across_axis(inner_rows):
        return passed_along(inner_rows, "az", half_cycle)

    mask_two = inside(2, rows_z, ax_count)
    prev_col = passed_along(courant_t[:, -1:], "az", 1)
    prev_row = shifted(courant_z[-1:], "ax", 1)
    azim_c = jnp.concatenate([prev_col, courant_t], axis=1)
    axial_c = jnp.concatenate([prev_row, courant_z], axis=0)

    def section_rise(values):
        padded = (
            with_halo(values.astype(jnp.bfloat16), (("az", 1), ("ax", 0)), 2).astype(values.dtype)
            * mask_two
        )
        return section_rate(
            padded, across_axis(values[:, :, 0]), courant_r, azim_c, axial_c, ionization
        )

    section_one = density + section_rise(density)
    evolved = 0.5 * (density + section_one + section_rise(section_one))
    blocks_z = rows_z // BZ
    blocks_t = cells_t // BT
    blocks_r = cells_r // BR
    block_total = blocks_z * blocks_t * blocks_r
    wanted = send_block[0].reshape(-1)

    def take_block(block_id):
        is_valid = (block_id < block_total).astype(jnp.float32)
        clipped = jnp.minimum(block_id, block_total - 1)
        start_z = clipped // (blocks_t * blocks_r) * BZ
        start_t = clipped // blocks_r % blocks_t * BT
        start_r = clipped % blocks_r * BR
        return lax.dynamic_slice(evolved, (start_z, start_t, start_r), (BZ, BT, BR)) * is_valid

    outgoing = jax.vmap(take_block)(wanted)
    fine_out = prolong(outgoing).reshape(ax_count, CAP, 2 * BZ, 2 * BT, 2 * BR)
    arrived = lax.all_to_all(fine_out, "ax", split_axis=0, concat_axis=0, tiled=True)
    patches = arrived.reshape(ax_count * CAP, 2 * BZ, 2 * BT, 2 * BR)[recv_slot[0]]
    return (evolved, patches[None])


def solution(mesh):
    in_specs = (
        P("ax", "az", None),
        P("ax", "az", None),
        P("ax", "az", None),
        P("ax", "az", None),
        P("ax", "az", None),
        P("az", "ax", None),
        P("az", "ax"),
    )
    out_specs = (P("ax", "az", None), P("az", "ax", None, None, None))
    return jax.shard_map(local, mesh=mesh, in_specs=in_specs, out_specs=out_specs, check_vma=False)
```

profile of v0, /device:TPU:11, one launch (start us, length us, event | category | flops | bytes accessed | tf_op | source)
XLA Modules:
  0.0 240.7 jit_solution(16894732649492685706)
XLA Ops:
  7.5 4.8 %collective-permute-start.6 = (bf16[1,16,512]{2,1,0:T(8,128)(2,1)S(1)}, bf16[1,16,512]{2,1,0:T(8,128)(2,1)S(1)}, u32[]{:S(2)}, u32[]{:S(2)}) collective-permute-start(bf16[1,16,512]{2,1,0:T(8,128)(2,1)S(1)} %slice.238), channel_id=1, source_target_pairs={{0,1},{1,2},{2,3},{3,4},{4,5},{5,6},{6,7},{7,8},{8,9},{9,10},{10,1... | collective-permute-start | bytes 49160 | tf_op jit(solution)/shard_map/ppermute | solution.py:23
  15.5 3.2 %collective-permute-done.3 = bf16[2,20,512]{2,0,1:T(2,128)(2,1)S(1)} collective-permute-done((bf16[2,20,512]{2,0,1:T(2,128)(2,1)S(1)}, bf16[2,20,512]{2,0,1:T(2,128)(2,1)S(1)}, u32[]{:S(2)}, u32[]{:S(2)}) %collective-permute-start.3) | collective-permute-done | bytes 40992 | tf_op jit(solution)/shard_map/ppermute | solution.py:35
  24.6 2.6 %collective-permute-start.9 = (bf16[2,20,512]{2,1,0:T(8,128)(2,1)S(1)}, bf16[2,20,512]{2,1,0:T(8,128)(2,1)S(1)}, u32[]{:S(2)}, u32[]{:S(2)}) collective-permute-start(bf16[2,20,512]{2,1,0:T(8,128)(2,1)S(1)} %get-tuple-element.47), channel_id=1, source_target_pairs={{0,1},{1,2},{2,3},{3,4},{4,5},{5,6},{6,7},{7,8},{8,9},{9,10},{10,1... | collective-permute-start | bytes 122888 | tf_op jit(solution)/shard_map/ppermute | solution.py:32
  30.5 87.1 %while.1 = (s32[]{:T(128)}, f32[8,16,512]{2,1,0:T(8,128)S(1)}, s32[32,3]{0,1:T(4,128)S(1)}, f32[32,4,8,128]{3,2,1,0:T(8,128)S(1)}, s32[]{:T(128)}) while((s32[]{:T(128)}, f32[8,16,512]{2,1,0:T(8,128)S(1)}, s32[32,3]{0,1:T(4,128)S(1)}, f32[32,4,8,128]{3,2,1,0:T(8,128)S(1)}, s32[]{:T(128)}) %tuple.42), condition=%wide.while_cond, body=%wide.while_body.sunk | while | flops 2 | bytes 32897 | solution.py:163
  31.2 2.1 bitcast_dynamic-update-slice_fusion.2
  33.9 2.1 bitcast_dynamic-update-slice_fusion.2
  39.3 2.1 bitcast_dynamic-update-slice_fusion.2
  42.1 2.1 bitcast_dynamic-update-slice_fusion.2
  47.5 2.1 bitcast_dynamic-update-slice_fusion.2
  50.2 2.1 bitcast_dynamic-update-slice_fusion.2
  55.7 2.1 bitcast_dynamic-update-slice_fusion.2
  58.4 2.1 bitcast_dynamic-update-slice_fusion.2
  63.8 2.1 bitcast_dynamic-update-slice_fusion.2
  66.5 2.1 bitcast_dynamic-update-slice_fusion.2
  72.0 2.1 bitcast_dynamic-update-slice_fusion.2
  74.7 2.1 bitcast_dynamic-update-slice_fusion.2
  82.9 2.1 bitcast_dynamic-update-slice_fusion.2
  85.6 2.1 bitcast_dynamic-update-slice_fusion.2
  91.0 2.1 bitcast_dynamic-update-slice_fusion.2
  120.5 6.5 %fusion = f32[8,32,16,256]{3,0,2,1:T(8,128)} fusion(f32[32,4,16,256]{3,2,1,0:T(8,128)S(1)} %convolution_bitcast_fusion, s32[8]{0:T(128)S(1)} %get-tuple-element.62, s32[8]{0:T(128)S(1)} %get-tuple-element.63), kind=kOutput, calls=%fused_computation.3 | convolution fusion | flops 50331808 | bytes 6291520 | tf_op jit(solution)/shard_map/pzTR,Zz->pZTR/dot_general | solution.py:113
  127.0 10.7 %all-to-all-start = ((f32[16,2,8,16,256]{4,2,3,1,0:T(8,128)}), f32[16,2,8,16,256]{4,2,3,1,0:T(8,128)}, u32[]{:S(2)}, u32[]{:S(2)}) async-start(f32[16,2,8,16,256]{4,2,3,1,0:T(8,128)} %bitcast.45), calls=%async_computation | async-start | bytes 8388608 | tf_op jit(solution)/shard_map/all_to_all | solution.py:167
  137.7 92.5 %all-to-all-done = f32[16,2,8,16,256]{4,2,3,1,0:T(8,128)} async-done(((f32[16,2,8,16,256]{4,2,3,1,0:T(8,128)}), f32[16,2,8,16,256]{4,2,3,1,0:T(8,128)}, u32[]{:S(2)}, u32[]{:S(2)}) %all-to-all-start) | async-done | bytes 4194336 | tf_op jit(solution)/shard_map/all_to_all | solution.py:167
  230.2 6.0 %copy.136 = f32[16,2,8,16,256]{4,3,2,1,0:T(8,128)} copy(f32[16,2,8,16,256]{4,2,3,1,0:T(8,128)} %all-to-all-done) | data formatting | bytes 8388608 | tf_op jit(solution)/shard_map/all_to_all | solution.py:167
  236.1 4.6 %gather_fusion = f32[24,8,16,256]{3,2,1,0:T(8,128)} fusion(f32[32,8,16,256]{3,2,1,0:T(8,128)} %bitcast.46, s32[1024]{0:T(1024)S(1)} %pad_clamp_fusion), kind=kCustom, calls=%fused_computation | custom fusion | bytes 6291552 | tf_op jit(solution)/shard_map/gather | solution.py:168
  (173 shorter events, 78.1 us)
Async XLA Ops:
  1.7 12.4 %collective-permute-start = (bf16[8,2,512]{2,0,1:T(8,128)(2,1)S(1)}, bf16[8,2,512]{2,0,1:T(8,128)(2,1)S(1)}, u32[]{:S(2)}, u32[]{:S(2)}) collective-permute-start(bf16[8,2,512]{2,0,1:T(8,128)(2,1)S(1)} %get-tuple-element.53), channel_id=1, source_target_pairs={{0,16},{16,0},{1,17},{17,1},{2,18},{18,2},{3,19},{19,3},{4,20},{20... | collective-permute-start | bytes 49160 | tf_op jit(solution)/shard_map/ppermute | solution.py:32
  3.0 11.1 %collective-permute-start.1 = (bf16[8,2,512]{2,0,1:T(8,128)(2,1)S(1)}, bf16[8,2,512]{2,0,1:T(8,128)(2,1)S(1)}, u32[]{:S(2)}, u32[]{:S(2)}) collective-permute-start(bf16[8,2,512]{2,0,1:T(8,128)(2,1)S(1)} %get-tuple-element.54), channel_id=1, source_target_pairs={{16,0},{0,16},{17,1},{1,17},{18,2},{2,18},{19,3},{3,19},{20,4},{4,... | collective-permute-start | bytes 49160 | tf_op jit(solution)/shard_map/ppermute | solution.py:35
  4.2 9.8 %collective-permute-start.4 = (f32[8,16]{1,0:T(8,128)S(1)}, f32[8,16]{1,0:T(8,128)S(1)}, u32[]{:S(2)}, u32[]{:S(2)}) collective-permute-start(f32[8,16]{1,0:T(8,128)S(1)} %bitcast.50), channel_id=1, source_target_pairs={{0,16},{16,0},{1,17},{17,1},{2,18},{18,2},{3,19},{19,3},{4,20},{20... | collective-permute-start | bytes 1544 | tf_op jit(solution)/shard_map/ppermute | solution.py:17
  6.5 8.3 %collective-permute-start.5 = (bf16[8,1,512]{2,0,1:T(8,128)(2,1)S(1)}, bf16[8,1,512]{2,0,1:T(8,128)(2,1)S(1)}, u32[]{:S(2)}, u32[]{:S(2)}) collective-permute-start(bf16[8,1,512]{2,0,1:T(8,128)(2,1)S(1)} %slice.303), channel_id=1, source_target_pairs={{0,16},{16,0},{1,17},{17,1},{2,18},{18,2},{3,19},{19,3},{4,20},{20... | collective-permute-start | bytes 24584 | tf_op jit(solution)/shard_map/ppermute | solution.py:17
  7.5 12.3 %collective-permute-start.6 = (bf16[1,16,512]{2,1,0:T(8,128)(2,1)S(1)}, bf16[1,16,512]{2,1,0:T(8,128)(2,1)S(1)}, u32[]{:S(2)}, u32[]{:S(2)}) collective-permute-start(bf16[1,16,512]{2,1,0:T(8,128)(2,1)S(1)} %slice.238), channel_id=1, source_target_pairs={{0,1},{1,2},{2,3},{3,4},{4,5},{5,6},{6,7},{7,8},{8,9},{9,10},{10,1... | collective-permute-start | bytes 49160 | tf_op jit(solution)/shard_map/ppermute | solution.py:23
  14.3 1.3 collective-permute-start.2
  14.3 5.2 %copy-start.2 = (bf16[8,16,512]{2,1,0:T(8,128)(2,1)S(1)}, bf16[8,16,512]{2,1,0:T(8,128)(2,1)}, u32[]{:S(2)}) copy-start(bf16[8,16,512]{2,1,0:T(8,128)(2,1)} %param.8) | copy-start | bytes 393220
  14.3 4.4 %collective-permute-start.3 = (bf16[2,20,512]{2,0,1:T(2,128)(2,1)S(1)}, bf16[2,20,512]{2,0,1:T(2,128)(2,1)S(1)}, u32[]{:S(2)}, u32[]{:S(2)}) collective-permute-start(bf16[2,20,512]{2,0,1:T(2,128)(2,1)S(1)} %get-tuple-element.50), channel_id=1, source_target_pairs={{1,0},{2,1},{3,2},{4,3},{5,4},{6,5},{7,6},{8,7},{9,8},{10,9},{11,1... | collective-permute-start | bytes 122888 | tf_op jit(solution)/shard_map/ppermute | solution.py:35
  18.9 1.0 copy-start.1
  19.2 1.0 copy-start
  19.2 1.0 copy-start.3
  20.5 3.0 %collective-permute-start.7 = (bf16[8,2,512]{2,0,1:T(8,128)(2,1)S(1)}, bf16[8,2,512]{2,0,1:T(8,128)(2,1)S(1)}, u32[]{:S(2)}, u32[]{:S(2)}) collective-permute-start(bf16[8,2,512]{2,0,1:T(8,128)(2,1)S(1)} %copy.128), channel_id=1, source_target_pairs={{0,16},{16,0},{1,17},{17,1},{2,18},{18,2},{3,19},{19,3},{4,20},{20... | collective-permute-start | bytes 49160 | tf_op jit(solution)/shard_map/ppermute | solution.py:32
  21.8 2.6 %collective-permute-start.8 = (bf16[8,2,512]{2,0,1:T(8,128)(2,1)S(1)}, bf16[8,2,512]{2,0,1:T(8,128)(2,1)S(1)}, u32[]{:S(2)}, u32[]{:S(2)}) collective-permute-start(bf16[8,2,512]{2,0,1:T(8,128)(2,1)S(1)} %copy.129), channel_id=1, source_target_pairs={{16,0},{0,16},{17,1},{1,17},{18,2},{2,18},{19,3},{3,19},{20,4},{4,... | collective-permute-start | bytes 49160 | tf_op jit(solution)/shard_map/ppermute | solution.py:35
  22.2 5.2 %collective-permute-start.11 = (f32[8,16]{1,0:T(8,128)S(1)}, f32[8,16]{1,0:T(8,128)S(1)}, u32[]{:S(2)}, u32[]{:S(2)}) collective-permute-start(f32[8,16]{1,0:T(8,128)S(1)} %slice_reduce_fusion), channel_id=1, source_target_pairs={{0,16},{16,0},{1,17},{17,1},{2,18},{18,2},{3,19},{19,3},{4,20},{20... | collective-permute-start | bytes 1544 | tf_op jit(solution)/shard_map/ppermute | solution.py:17
  24.5 4.5 %collective-permute-start.10 = (bf16[2,20,512]{2,1,0:T(8,128)(2,1)S(1)}, bf16[2,20,512]{2,1,0:T(8,128)(2,1)S(1)}, u32[]{:S(2)}, u32[]{:S(2)}) collective-permute-start(bf16[2,20,512]{2,1,0:T(8,128)(2,1)S(1)} %get-tuple-element.48), channel_id=1, source_target_pairs={{1,0},{2,1},{3,2},{4,3},{5,4},{6,5},{7,6},{8,7},{9,8},{10,9},{11,1... | collective-permute-start | bytes 122888 | tf_op jit(solution)/shard_map/ppermute | solution.py:35
  24.6 4.4 %collective-permute-start.9 = (bf16[2,20,512]{2,1,0:T(8,128)(2,1)S(1)}, bf16[2,20,512]{2,1,0:T(8,128)(2,1)S(1)}, u32[]{:S(2)}, u32[]{:S(2)}) collective-permute-start(bf16[2,20,512]{2,1,0:T(8,128)(2,1)S(1)} %get-tuple-element.47), channel_id=1, source_target_pairs={{0,1},{1,2},{2,3},{3,4},{4,5},{5,6},{6,7},{7,8},{8,9},{9,10},{10,1... | collective-permute-start | bytes 122888 | tf_op jit(solution)/shard_map/ppermute | solution.py:32
  117.6 9.4 %copy-start.4 = (f32[8,16,512]{2,1,0:T(8,128)}, f32[8,16,512]{2,1,0:T(8,128)S(1)}, u32[]{:S(2)}) copy-start(f32[8,16,512]{2,1,0:T(8,128)S(1)} %get-tuple-element.112) | copy-start | bytes 786436
  127.0 10.7 %copy-start.5 = (s32[1,24]{1,0:T(1,128)S(1)}, s32[1,24]{1,0:T(1,128)}, u32[]{:S(2)}) copy-start(s32[1,24]{1,0:T(1,128)} %param.13) | copy-start | bytes 292
  127.0 103.2 %all-to-all-start = ((f32[16,2,8,16,256]{4,2,3,1,0:T(8,128)}), f32[16,2,8,16,256]{4,2,3,1,0:T(8,128)}, u32[]{:S(2)}, u32[]{:S(2)}) async-start(f32[16,2,8,16,256]{4,2,3,1,0:T(8,128)} %bitcast.45), calls=%async_computation | async-start | bytes 8388608 | tf_op jit(solution)/shard_map/all_to_all | solution.py:167
where the time goes:
time: 242 us; the launch traced here: 241 us
  local copies, waits for them, and re-layouts  102 us (42%)
  waiting for transfers between devices  98.7 us (41%)
  starting transfers between devices  24.7 us (10%)
  matrix products  9.43 us (4%)
  other arithmetic  4.39 us (2%)
    all_to_all x1, waiting for transfers between devices, local(): lax.all_to_all(fine_out, 'ax', split_axis=0, concat_axis=0, tiled=True)  92.5 us
    gather x96, local copies, waits for them, and re-layouts  87 us
    all_to_all x1, starting transfers between devices, local(): lax.all_to_all(fine_out, 'ax', split_axis=0, concat_axis=0, tiled=True)  10.7 us
    dot_general x1, matrix products, prolong(): jnp.einsum('pzTR,Zz->pZTR', spread, interp_matrix(blocks.shape[1]), preci...  6.48 us
    all_to_all x1, local copies, waits for them, and re-layouts, local(): lax.all_to_all(fine_out, 'ax', split_axis=0, concat_axis=0, tiled=True)  5.95 us
    ppermute x4, waiting for transfers between devices, with_halo(): lax.ppermute(lax.slice_in_dim(block, 0, width, axis=dim), axis, backward)  5.55 us
    ppermute x4, starting transfers between devices, with_halo(): lax.ppermute(lax.slice_in_dim(block, block.shape[dim] - width, None, axis...  5.31 us
    ppermute x1, starting transfers between devices, shifted(): lax.ppermute(value, axis, [(source, source + steps) for source in range(l...  4.84 us
  transfers between devices with their start and end apart: 13, of which 5 were waited for; matrix products, arithmetic and copies ran while one was open for 3% of the time, Pallas kernels for 0%

commit v1 on v0

v1 whole, which is shorter than its diff:
```python
import functools

import jax
import jax.numpy as jnp
import numpy as np
from jax import lax
from jax.experimental import pallas as pl
from jax.experimental.pallas import tpu as pltpu
from jax.sharding import PartitionSpec as P

BZ = 4
BT = 8
BR = 128
CAP = 2
F32 = jnp.float32
BF16 = jnp.bfloat16
DIFFUSION = 0.05
VMEM_LIMIT = 24 * 1024 * 1024

BLOCK_ROWS = BZ * BT
MEAN_ROW = CAP * BLOCK_ROWS
CHUNK_ROWS = MEAN_ROW + 8


def pack_sector(values, courant_t, out_ref):
    rows_z, cells_t, cells_r = values.shape
    row = lax.broadcasted_iota(jnp.int32, (8, cells_r), 0)
    lane = lax.broadcasted_iota(jnp.int32, (cells_t, 128), 1)
    inner = jnp.zeros((cells_t, 128), F32)
    tiles = []
    for k in range(rows_z):
        tile = jnp.where(row < 2, values[k, 0:8, :], values[k, cells_t - 8 :, :])
        if courant_t is not None:
            face = courant_t[k].astype(F32)[cells_t - 8 :, :]
            tile = jnp.where(row == 5, pltpu.roll(face, 6, 0), tile)
        tiles.append(tile)
        inner = jnp.where(lane == k, values[k, :, 0:1], inner)
    for pair in range(rows_z // 2):
        out_ref[pair] = jnp.concatenate(tiles[2 * pair : 2 * pair + 2], axis=0).astype(BF16)
    rounded = inner.astype(BF16)
    out_ref[rows_z // 2, :, 0:128] = rounded
    out_ref[rows_z // 2, :, 128:256] = (inner - rounded.astype(F32)).astype(BF16)
    out_ref[rows_z // 2, :, 256:] = jnp.zeros((cells_t, cells_r - 256), BF16)


def pack_slab(values, courant_z, even_ref, odd_ref):
    rows_z = values.shape[0]
    parity = lax.rem(lax.axis_index("ax"), 2)
    first_even = jnp.where(parity == 0, rows_z - 2, 0)
    first_odd = jnp.where(parity == 0, 0, rows_z - 2)
    for out_ref, first in ((even_ref, first_even), (odd_ref, first_odd)):
        for r in range(2):
            out_ref[r] = values[first + r].astype(BF16)
        if courant_z is not None:
            out_ref[2] = courant_z[rows_z - 1]


def first_messages(density, courant_t, courant_z, sector_ref, even_ref, odd_ref):
    pack_sector(density, courant_t, sector_ref)
    pack_slab(density, courant_z, even_ref, odd_ref)


def rates(values, sector, slab, faces_below, courants, ionization):
    rows_z, cells_t, cells_r = values.shape
    left, right, across = sector
    even_msg, odd_msg = slab
    left_faces, even_faces, odd_faces = faces_below
    courant_r, courant_t, courant_z = courants
    me = lax.axis_index("ax")
    is_even = lax.rem(me, 2) == 0
    has_below = me > 0
    has_above = me < lax.axis_size("ax") - 1
    zero = jnp.zeros((cells_t, cells_r), F32)

    def below(even, odd):
        return jnp.where(has_below, jnp.where(is_even, odd, even).astype(F32), zero)

    def above(even, odd):
        return jnp.where(has_above, jnp.where(is_even, even, odd).astype(F32), zero)

    def row_at(k):
        if k < 0:
            return below(even_msg[k + 2], odd_msg[k + 2])
        if k >= rows_z:
            return above(even_msg[k - rows_z], odd_msg[k - rows_z])
        return values[k]

    lane = lax.broadcasted_iota(jnp.int32, (cells_t, cells_r), 1)
    index = lane.astype(F32)
    area = jnp.where(lane < cells_r - 1, index + 1.0, 0.0)
    inverse_radius = 1.0 / (index + 0.5)
    inner = across[rows_z // 2, :, 0:128].astype(F32) + across[rows_z // 2, :, 128:256].astype(F32)
    halo_row = lax.broadcasted_iota(jnp.int32, (8, cells_r), 0)

    def tile_of(msg, k):
        return msg[k // 2].astype(F32)[(k % 2) * 8 : (k % 2) * 8 + 8, :]

    def axial_flux(courant, back, here, up, up_two):
        low = here + 0.25 * (up - back)
        high = up - 0.25 * (up_two - here)
        return courant * jnp.where(courant > 0.0, low, high)

    flux_z = axial_flux(
        below(even_faces[2], odd_faces[2]), row_at(-2), row_at(-1), row_at(0), row_at(1)
    )
    for k in range(rows_z):
        here, back, up = row_at(k), row_at(k - 1), row_at(k + 1)
        next_flux = axial_flux(courant_z[k].astype(F32), back, here, up, row_at(k + 2))
        rate = (
            DIFFUSION * (up - 2.0 * here + back)
            + ionization[k].astype(F32) * here
            - (next_flux - flux_z)
        )
        flux_z = next_flux
        halo = tile_of(left, k)
        if right is not left:
            halo = jnp.where(halo_row < 4, tile_of(right, k), halo)
        face_halo = pltpu.roll(tile_of(left_faces, k), 2, 0)
        ring = jnp.concatenate([halo, here], axis=0)
        rows = cells_t + 8
        courant = jnp.concatenate([face_halo, courant_t[k].astype(F32)], axis=0)
        quarter = 0.25 * (pltpu.roll(ring, rows - 1, 0) - pltpu.roll(ring, 1, 0))
        flux = courant * jnp.where(courant > 0.0, ring + quarter, pltpu.roll(ring - quarter, rows - 1, 0))
        rate = rate - (flux - pltpu.roll(flux, 1, 0))[8:, :]
        inward = jnp.where(lane == 0, inner[:, k : k + 1], pltpu.roll(here, 1, 1))
        outward = jnp.where(lane == cells_r - 1, 0.0, pltpu.roll(here, cells_r - 1, 1))
        quarter = 0.25 * (outward - inward)
        courant = courant_r[k].astype(F32)
        flux = courant * jnp.where(
            courant > 0.0, here + quarter, pltpu.roll(here - quarter, cells_r - 1, 1)
        )
        carried = area * (DIFFUSION * (outward - here) - flux)
        yield rate + (carried - pltpu.roll(carried, 1, 1)) * inverse_radius


def first_stage(count, *refs):
    density, courant_r, courant_t, courant_z, ionization, even, odd = refs[:7]
    sector = refs[7 : 7 + count]
    section, sector_out, even_out, odd_out = refs[7 + count :]
    left, right, across = sector if count == 3 else sector * 3
    steps = rates(
        density, (left, right, across), (even, odd), (left, even, odd), (courant_r, courant_t, courant_z), ionization
    )
    for k, rate in enumerate(steps):
        section[k] = density[k] + rate
    pack_sector(section, None, sector_out)
    pack_slab(section, None, even_out, odd_out)


def second_stage(count, *refs):
    wanted, density, section, courant_r, courant_t, courant_z, ionization = refs[:7]
    left_faces, even_faces, odd_faces, even, odd = refs[7:12]
    sector = refs[12 : 12 + count]
    evolved, outgoing, table, means = refs[12 + count :]
    left, right, across = sector if count == 3 else sector * 3
    steps = rates(
        section,
        (left, right, across),
        (even, odd),
        (left_faces, even_faces, odd_faces),
        (courant_r, courant_t, courant_z),
        ionization,
    )
    for k, rate in enumerate(steps):
        evolved[k] = 0.5 * (density[k] + section[k] + rate)
    rows_z, cells_t, cells_r = evolved.shape
    blocks_t, blocks_r = cells_t // BT, cells_r // BR
    total = rows_z // BZ * blocks_t * blocks_r
    for block in range(total):
        z = block // (blocks_t * blocks_r) * BZ
        t = block // blocks_r % blocks_t * BT
        r = block % blocks_r * BR
        tiles = [evolved[z + i, t : t + BT, r : r + BR] for i in range(BZ)]
        mean = jnp.mean(sum(tiles), axis=0, keepdims=True) * (1.0 / BZ)
        mean = jnp.broadcast_to(mean.astype(BF16).astype(F32), (BT, BR))
        means[block] = mean
        table[block] = jnp.concatenate([tile - mean for tile in tiles], axis=0).astype(BF16)
    means[total] = jnp.zeros((BT, BR), F32)
    table[total] = jnp.zeros((BLOCK_ROWS, BR), BF16)
    row = lax.broadcasted_iota(jnp.int32, (8, BR), 0)
    for owner in range(outgoing.shape[0]):
        mean_rows = jnp.zeros((8, BR), F32)
        for slot in range(CAP):
            block = wanted[0, owner, slot]
            outgoing[owner, slot * BLOCK_ROWS : (slot + 1) * BLOCK_ROWS, :] = table[block]
            mean_rows = jnp.where(row == slot, means[block], mean_rows)
        outgoing[owner, MEAN_ROW:, :] = mean_rows.astype(BF16)


def prolong_patches(slots, arrived, radial_matrix, tile_matrix, patches, spread, fine, sems):
    sources = arrived.shape[0]
    for source in range(sources):
        spread[source] = jnp.dot(arrived[source], radial_matrix[...], preferred_element_type=F32)
    copies = []
    for p in range(fine.shape[0]):
        code = slots[0, p]
        source, slot = lax.shift_right_logical(code, 1), lax.bitwise_and(code, 1)
        first = pl.multiple_of(slot * BLOCK_ROWS, BLOCK_ROWS)
        coarse = spread[source, pl.ds(first, BLOCK_ROWS), :] + spread[source, pl.ds(MEAN_ROW + slot, 1), :]
        high = coarse.astype(BF16)
        low = (coarse - high.astype(F32)).astype(BF16)
        fine[p] = jnp.dot(
            tile_matrix[...], jnp.concatenate([high, low], axis=0), preferred_element_type=F32
        )
        copy = pltpu.make_async_copy(fine.at[p], patches.at[p], sems.at[p])
        copy.start()
        copies.append(copy)
    for copy in copies:
        copy.wait()


def interp_matrix(coarse_count):
    matrix = np.zeros((2 * coarse_count, coarse_count), np.float32)
    for m in range(coarse_count):
        matrix[2 * m, m] += 0.75
        matrix[2 * m, max(m - 1, 0)] += 0.25
        matrix[2 * m + 1, m] += 0.75
        matrix[2 * m + 1, min(m + 1, coarse_count - 1)] += 0.25
    return matrix


def in_vmem(count):
    return [pl.BlockSpec(memory_space=pltpu.VMEM)] * count


def in_smem(count):
    return [pl.BlockSpec(memory_space=pltpu.SMEM)] * count


PARAMS = pltpu.CompilerParams(vmem_limit_bytes=VMEM_LIMIT)


def local(density, courant_r, courant_t, courant_z, ionization, send_block, recv_slot):
    rows_z, cells_t, cells_r = density.shape
    ax_count = lax.axis_size("ax")
    az_count = lax.axis_size("az")
    owned = recv_slot.shape[1]

    def flat(a, i):
        return a * ax_count + i

    even_pairs = [(i, i ^ 1) for i in range(ax_count)]
    odd_pairs = []
    for a in range(az_count):
        odd_pairs += [(flat(a, i), flat(a, ((i - 1) ^ 1) + 1)) for i in range(1, ax_count - 1)]
        odd_pairs += [(flat(a, i), flat(a ^ 1, i)) for i in (0, ax_count - 1)]

    def by(steps):
        return [(a, (a + steps) % az_count) for a in range(az_count)]

    def exchange(sector, even, odd):
        if az_count == 2:
            sectors = [lax.ppermute(sector, "az", by(1))]
        else:
            sectors = [lax.ppermute(sector, "az", by(s)) for s in (1, az_count - 1, az_count // 2)]
        return sectors, lax.ppermute(even, "ax", even_pairs), lax.ppermute(odd, ("az", "ax"), odd_pairs)

    sector_shape = jax.ShapeDtypeStruct((rows_z // 2 + 1, cells_t, cells_r), BF16)
    slab_three = jax.ShapeDtypeStruct((3, cells_t, cells_r), BF16)
    slab_two = jax.ShapeDtypeStruct((2, cells_t, cells_r), BF16)
    field = jax.ShapeDtypeStruct(density.shape, F32)

    sector, even, odd = pl.pallas_call(
        first_messages,
        out_shape=(sector_shape, slab_three, slab_three),
        in_specs=in_vmem(3),
        out_specs=tuple(in_vmem(3)),
        compiler_params=PARAMS,
        name="first_messages",
    )(density, courant_t, courant_z)
    sectors, even, odd = exchange(sector, even, odd)
    count = len(sectors)

    section, sector, even_two, odd_two = pl.pallas_call(
        functools.partial(first_stage, count),
        out_shape=(field, sector_shape, slab_two, slab_two),
        in_specs=in_vmem(7 + count),
        out_specs=tuple(in_vmem(4)),
        compiler_params=PARAMS,
        name="first_stage",
    )(density, courant_r, courant_t, courant_z, ionization, even, odd, *sectors)
    sectors_two, even_two, odd_two = exchange(sector, even_two, odd_two)

    blocks = rows_z // BZ * (cells_t // BT) * (cells_r // BR)
    evolved, outgoing = pl.pallas_call(
        functools.partial(second_stage, count),
        out_shape=(field, jax.ShapeDtypeStruct((ax_count, CHUNK_ROWS, BR), BF16)),
        in_specs=in_smem(1) + in_vmem(11 + count),
        out_specs=tuple(in_vmem(2)),
        scratch_shapes=[
            pltpu.VMEM((blocks + 1, BLOCK_ROWS, BR), BF16),
            pltpu.VMEM((blocks + 1, BT, BR), F32),
        ],
        compiler_params=PARAMS,
        name="second_stage",
    )(
        send_block, density, section, courant_r, courant_t, courant_z, ionization,
        sectors[0], even, odd, even_two, odd_two, *sectors_two,
    )

    arrived = lax.all_to_all(outgoing, "ax", split_axis=0, concat_axis=0, tiled=True)

    tile_matrix = np.kron(interp_matrix(BZ), interp_matrix(BT))
    tile_matrix = jnp.asarray(np.concatenate([tile_matrix, tile_matrix], axis=1), BF16)
    radial_matrix = jnp.asarray(interp_matrix(BR).T, BF16)
    fine_rows = 4 * BZ * BT
    patches = pl.pallas_call(
        prolong_patches,
        out_shape=jax.ShapeDtypeStruct((owned, fine_rows, 2 * BR), F32),
        in_specs=in_smem(1) + in_vmem(3),
        out_specs=pl.BlockSpec(memory_space=pl.ANY),
        scratch_shapes=[
            pltpu.VMEM((ax_count, CHUNK_ROWS, 2 * BR), F32),
            pltpu.VMEM((owned, fine_rows, 2 * BR), F32),
            pltpu.SemaphoreType.DMA((owned,)),
        ],
        compiler_params=PARAMS,
        name="prolong_patches",
    )(recv_slot, arrived, radial_matrix, tile_matrix)
    return (evolved, patches.reshape(1, owned, 2 * BZ, 2 * BT, 2 * BR))


def solution(mesh):
    in_specs = (
        P("ax", "az", None),
        P("ax", "az", None),
        P("ax", "az", None),
        P("ax", "az", None),
        P("ax", "az", None),
        P("az", "ax", None),
        P("az", "ax"),
    )
    out_specs = (P("ax", "az", None), P("az", "ax", None, None, None))
    return jax.shard_map(local, mesh=mesh, in_specs=in_specs, out_specs=out_specs, check_vma=False)
```

time: 242 us -> 44.4 us (0.18)
  the two profiles are of different devices: /device:TPU:11 before, /device:TPU:0 now
where the time goes in v1:
time: 44.4 us; the launch traced here: 44 us
  blocking collectives  15.8 us (36%)
  local copies, waits for them, and re-layouts  9.89 us (22%)
  Pallas kernels  6.39 us (14%)
  waiting for transfers between devices  5.97 us (13%)
  starting transfers between devices  5.28 us (12%)
  between operations  0.67 us (2%)
    all_to_all x1, blocking collectives, local(): lax.all_to_all(outgoing, 'ax', split_axis=0, concat_axis=0, tiled=True)  15.8 us
    unnamed x27, local copies, waits for them, and re-layouts  9.89 us
    ppermute x2, waiting for transfers between devices, exchange(): lax.ppermute(odd, ('az', 'ax'), odd_pairs)  4.89 us
    ppermute x2, starting transfers between devices, exchange(): sectors = [lax.ppermute(sector, 'az', by(1))]  3.97 us
    pallas_call x1, Pallas kernels, local(): pl.pallas_call(prolong_patches, out_shape=jax.ShapeDtypeStruct((owned, fi...  2.92 us
    pallas_call x1, Pallas kernels, local(): pl.pallas_call(functools.partial(second_stage, count), out_shape=(field,...  2.35 us
    ppermute x2, starting transfers between devices, exchange(): lax.ppermute(odd, ('az', 'ax'), odd_pairs)  1.31 us
    ppermute x2, waiting for transfers between devices, exchange(): lax.ppermute(even, 'ax', even_pairs)  1.08 us
  transfers between devices with their start and end apart: 6, of which 3 were waited for; matrix products, arithmetic and copies ran while one was open for 2% of the time, Pallas kernels for 0%

profile of v1, /device:TPU:0, one launch (start us, length us, event | category | flops | bytes accessed | tf_op | source)
XLA Modules:
  0.0 44.0 jit_solution(6894389842191883267)
XLA Ops:
  0.6 0.0 copy-start
  0.6 0.9 %copy-done = f32[8,16,512]{2,1,0:T(8,128)S(1)} copy-done((f32[8,16,512]{2,1,0:T(8,128)S(1)}, f32[8,16,512]{2,1,0:T(8,128)}, u32[]{:S(2)}) %copy-start) | copy-done | bytes 262168
  1.6 0.9 %copy-done.2 = bf16[8,16,512]{2,1,0:T(8,128)(2,1)S(1)} copy-done((bf16[8,16,512]{2,1,0:T(8,128)(2,1)S(1)}, bf16[8,16,512]{2,1,0:T(8,128)(2,1)}, u32[]{:S(2)}) %copy-start.2) | copy-done | bytes 131096
  2.5 0.9 %copy-done.4 = bf16[8,16,512]{2,1,0:T(8,128)(2,1)S(1)} copy-done((bf16[8,16,512]{2,1,0:T(8,128)(2,1)S(1)}, bf16[8,16,512]{2,1,0:T(8,128)(2,1)}, u32[]{:S(2)}) %copy-start.4) | copy-done | bytes 131096
  3.4 0.1 first_messages.1
  3.5 3.0 %collective-permute-start.2 = (bf16[5,16,512]{2,1,0:T(8,128)(2,1)S(1)}, bf16[5,16,512]{2,1,0:T(8,128)(2,1)S(1)}, u32[]{:S(2)}, u32[]{:S(2)}) collective-permute-start(bf16[5,16,512]{2,1,0:T(8,128)(2,1)S(1)} %get-tuple-element.13), channel_id=1, source_target_pairs={{0,16},{16,0},{1,17},{17,1},{2,18},{18,2},{3,19},{19,3},{4,20},{20... | collective-permute-start | bytes 245768 | tf_op jit(solution)/shard_map/ppermute | solution.py:253
  6.5 0.2 collective-permute-start.1
  6.7 1.1 %collective-permute-done.refs_5_.refs_8_ = bf16[3,16,512]{2,1,0:T(8,128)(2,1)S(1)} collective-permute-done((bf16[3,16,512]{2,1,0:T(8,128)(2,1)S(1)}, bf16[3,16,512]{2,1,0:T(8,128)(2,1)S(1)}, u32[]{:S(2)}, u32[]{:S(2)}) %collective-permute-start) | collective-permute-done | bytes 49184 | tf_op jit(solution)/shard_map/ppermute | solution.py:256
  7.8 2.9 %collective-permute-done.1.refs_6_.refs_9_ = bf16[3,16,512]{2,1,0:T(8,128)(2,1)S(1)} collective-permute-done((bf16[3,16,512]{2,1,0:T(8,128)(2,1)S(1)}, bf16[3,16,512]{2,1,0:T(8,128)(2,1)S(1)}, u32[]{:S(2)}, u32[]{:S(2)}) %collective-permute-start.1) | collective-permute-done | bytes 49184 | tf_op jit(solution)/shard_map/ppermute | solution.py:256
  10.6 0.9 %copy-done.6 = bf16[8,16,512]{2,1,0:T(8,128)(2,1)S(1)} copy-done((bf16[8,16,512]{2,1,0:T(8,128)(2,1)S(1)}, bf16[8,16,512]{2,1,0:T(8,128)(2,1)}, u32[]{:S(2)}) %copy-start.6) | copy-done | bytes 131096
  11.5 0.9 %copy-done.8 = bf16[8,16,512]{2,1,0:T(8,128)(2,1)S(1)} copy-done((bf16[8,16,512]{2,1,0:T(8,128)(2,1)S(1)}, bf16[8,16,512]{2,1,0:T(8,128)(2,1)}, u32[]{:S(2)}) %copy-start.8) | copy-done | bytes 131096
  12.4 1.0 %first_stage.1 = (f32[8,16,512]{2,1,0:T(8,128)S(1)}, bf16[5,16,512]{2,1,0:T(8,128)(2,1)S(1)}, bf16[2,16,512]{2,1,0:T(8,128)(2,1)S(1)}, bf16[2,16,512]{2,1,0:T(8,128)(2,1)S(1)}) custom-call(f32[8,16,512]{2,1,0:T(8,128)S(1)} %copy-done, bf16[8,16,512]{2,1,0:T(8,128)(2,1)S(1)} %copy-done.6, bf16[8,16,512]{2,1,0:T(8,128)(2,1)S(1)} %copy-done.2, ...), custom_call_target="tpu_custom_call" | custom-call | tf_op jit(solution)/shard_map/first_stage/pallas_call | solution.py:274
  13.5 0.9 %collective-permute-start.5 = (bf16[5,16,512]{2,1,0:T(8,128)(2,1)S(1)}, bf16[5,16,512]{2,1,0:T(8,128)(2,1)S(1)}, u32[]{:S(2)}, u32[]{:S(2)}) collective-permute-start(bf16[5,16,512]{2,1,0:T(8,128)(2,1)S(1)} %get-tuple-element.17), channel_id=1, source_target_pairs={{0,16},{16,0},{1,17},{17,1},{2,18},{18,2},{3,19},{19,3},{4,20},{20... | collective-permute-start | bytes 245768 | tf_op jit(solution)/shard_map/ppermute | solution.py:253
  14.4 1.2 %collective-permute-start.4 = (bf16[2,16,512]{2,1,0:T(8,128)(2,1)S(1)}, bf16[2,16,512]{2,1,0:T(8,128)(2,1)S(1)}, u32[]{:S(2)}, u32[]{:S(2)}) collective-permute-start(bf16[2,16,512]{2,1,0:T(8,128)(2,1)S(1)} %get-tuple-element.16), channel_id=1, source_target_pairs={{1,2},{2,1},{3,4},{4,3},{5,6},{6,5},{7,8},{8,7},{9,10},{10,9},{11,... | collective-permute-start | bytes 98312 | tf_op jit(solution)/shard_map/ppermute | solution.py:256
  15.6 0.8 %copy.11.refs_0_ = s32[1,16,2]{2,1,0:T(8,128)S(1)} copy(s32[1,16,2]{1,2,0:T(2,128)} %param.14) | data formatting | bytes 256 | tf_op args[5]
  16.3 2.0 %collective-permute-done.4.refs_11_ = bf16[2,16,512]{2,1,0:T(8,128)(2,1)S(1)} collective-permute-done((bf16[2,16,512]{2,1,0:T(8,128)(2,1)S(1)}, bf16[2,16,512]{2,1,0:T(8,128)(2,1)S(1)}, u32[]{:S(2)}, u32[]{:S(2)}) %collective-permute-start.4) | collective-permute-done | bytes 32800 | tf_op jit(solution)/shard_map/ppermute | solution.py:256
  18.4 0.9 %copy-done.1 = f32[8,16,512]{2,1,0:T(8,128)S(1)} copy-done((f32[8,16,512]{2,1,0:T(8,128)S(1)}, f32[8,16,512]{2,1,0:T(8,128)}, u32[]{:S(2)}) %copy-start.1) | copy-done | bytes 262168
  19.3 0.9 %copy-done.3 = bf16[8,16,512]{2,1,0:T(8,128)(2,1)S(1)} copy-done((bf16[8,16,512]{2,1,0:T(8,128)(2,1)S(1)}, bf16[8,16,512]{2,1,0:T(8,128)(2,1)}, u32[]{:S(2)}) %copy-start.3) | copy-done | bytes 131096
  20.2 0.9 %copy-done.5 = bf16[8,16,512]{2,1,0:T(8,128)(2,1)S(1)} copy-done((bf16[8,16,512]{2,1,0:T(8,128)(2,1)S(1)}, bf16[8,16,512]{2,1,0:T(8,128)(2,1)}, u32[]{:S(2)}) %copy-start.5) | copy-done | bytes 131096
  21.1 0.9 %copy-done.7 = bf16[8,16,512]{2,1,0:T(8,128)(2,1)S(1)} copy-done((bf16[8,16,512]{2,1,0:T(8,128)(2,1)S(1)}, bf16[8,16,512]{2,1,0:T(8,128)(2,1)}, u32[]{:S(2)}) %copy-start.7) | copy-done | bytes 131096
  22.0 0.9 %copy-done.9 = bf16[8,16,512]{2,1,0:T(8,128)(2,1)S(1)} copy-done((bf16[8,16,512]{2,1,0:T(8,128)(2,1)S(1)}, bf16[8,16,512]{2,1,0:T(8,128)(2,1)}, u32[]{:S(2)}) %copy-start.9) | copy-done | bytes 131096
  22.9 2.4 %second_stage.1 = (f32[8,16,512]{2,1,0:T(8,128)}, bf16[16,72,128]{2,1,0:T(8,128)(2,1)S(1)}) custom-call(s32[1,16,2]{2,1,0:T(8,128)S(1)} %copy.11.refs_0_, f32[8,16,512]{2,1,0:T(8,128)S(1)} %copy-done.1, f32[8,16,512]{2,1,0:T(8,128)S(1)} %get-tuple-element.14.refs_2_, bf16[8,16,512]{2,1,0:T(8,128)(2,1)S(1)} %copy-done.7, bf16[8,16,512]{2,1,0:T(8,128)(2,1)S(1)} %copy-done.3, ...), custom_call_target="tpu_custom_call" | custom-call | tf_op jit(solution)/shard_map/second_stage/pallas_call | solution.py:285
  25.3 15.8 %all_to_all.5.arrived = bf16[16,72,128]{2,1,0:T(8,128)(2,1)S(1)} all-to-all(bf16[16,72,128]{2,1,0:T(8,128)(2,1)S(1)} %get-tuple-element.19), channel_id=1, replica_groups=mesh['az'=2,'ax'=16] {'ax'}, dimensions={0} | all-to-all | bytes 589824 | tf_op jit(solution)/shard_map/all_to_all | solution.py:301
  41.1 2.9 %prolong_patches.1 = f32[24,128,256]{2,1,0:T(8,128)} custom-call(s32[1,24]{1,0:T(1,128)S(1)} %copy-done.12, bf16[16,72,128]{2,1,0:T(8,128)(2,1)S(1)} %all_to_all.5.arrived, bf16[128,256]{1,0:T(8,128)(2,1)S(1)} %copy-done.10, bf16[128,64]{1,0:T(8,128)(2,1)S(1)} %copy-done.11), custom_call_target="tpu_custom_call" | custom-call | tf_op jit(solution)/shard_map/prolong_patches/pallas_call | solution.py:307
  (20 shorter events, 0.0 us)
Async XLA Ops:
  0.6 1.0 %copy-start = (f32[8,16,512]{2,1,0:T(8,128)S(1)}, f32[8,16,512]{2,1,0:T(8,128)}, u32[]{:S(2)}) copy-start(f32[8,16,512]{2,1,0:T(8,128)} %refs_1_.3) | copy-start | bytes 786436
  1.6 0.9 %copy-start.2 = (bf16[8,16,512]{2,1,0:T(8,128)(2,1)S(1)}, bf16[8,16,512]{2,1,0:T(8,128)(2,1)}, u32[]{:S(2)}) copy-start(bf16[8,16,512]{2,1,0:T(8,128)(2,1)} %refs_4_.3) | copy-start | bytes 393220
  2.5 0.9 %copy-start.4 = (bf16[8,16,512]{2,1,0:T(8,128)(2,1)S(1)}, bf16[8,16,512]{2,1,0:T(8,128)(2,1)}, u32[]{:S(2)}) copy-start(bf16[8,16,512]{2,1,0:T(8,128)(2,1)} %refs_5_.1) | copy-start | bytes 393220
  3.4 37.7 %copy-start.10 = (bf16[128,256]{1,0:T(8,128)(2,1)S(1)}, bf16[128,256]{1,0:T(8,128)(2,1)}, u32[]{:S(2)}) copy-start(bf16[128,256]{1,0:T(8,128)(2,1)} %constant.5.clone.radial_matrix) | copy-start | bytes 196612
  3.4 37.7 %copy-start.11 = (bf16[128,64]{1,0:T(8,128)(2,1)S(1)}, bf16[128,64]{1,0:T(8,128)(2,1)}, u32[]{:S(2)}) copy-start(bf16[128,64]{1,0:T(8,128)(2,1)} %constant.4.clone.tile_matrix) | copy-start | bytes 49156
  3.4 37.7 %copy-start.12 = (s32[1,24]{1,0:T(1,128)S(1)}, s32[1,24]{1,0:T(1,128)}, u32[]{:S(2)}) copy-start(s32[1,24]{1,0:T(1,128)} %slots.1) | copy-start | bytes 292
  3.5 7.1 %collective-permute-start.2 = (bf16[5,16,512]{2,1,0:T(8,128)(2,1)S(1)}, bf16[5,16,512]{2,1,0:T(8,128)(2,1)S(1)}, u32[]{:S(2)}, u32[]{:S(2)}) collective-permute-start(bf16[5,16,512]{2,1,0:T(8,128)(2,1)S(1)} %get-tuple-element.13), channel_id=1, source_target_pairs={{0,16},{16,0},{1,17},{17,1},{2,18},{18,2},{3,19},{19,3},{4,20},{20... | collective-permute-start | bytes 245768 | tf_op jit(solution)/shard_map/ppermute | solution.py:253
  6.5 1.2 %collective-permute-start = (bf16[3,16,512]{2,1,0:T(8,128)(2,1)S(1)}, bf16[3,16,512]{2,1,0:T(8,128)(2,1)S(1)}, u32[]{:S(2)}, u32[]{:S(2)}) collective-permute-start(bf16[3,16,512]{2,1,0:T(8,128)(2,1)S(1)} %get-tuple-element.11), channel_id=1, source_target_pairs={{0,1},{1,0},{2,3},{3,2},{4,5},{5,4},{6,7},{7,6},{8,9},{9,8},{10,11... | collective-permute-start | bytes 147464 | tf_op jit(solution)/shard_map/ppermute | solution.py:256
  6.5 4.1 %collective-permute-start.1 = (bf16[3,16,512]{2,1,0:T(8,128)(2,1)S(1)}, bf16[3,16,512]{2,1,0:T(8,128)(2,1)S(1)}, u32[]{:S(2)}, u32[]{:S(2)}) collective-permute-start(bf16[3,16,512]{2,1,0:T(8,128)(2,1)S(1)} %get-tuple-element.12), channel_id=1, source_target_pairs={{1,2},{2,1},{3,4},{4,3},{5,6},{6,5},{7,8},{8,7},{9,10},{10,9},{11,... | collective-permute-start | bytes 147464 | tf_op jit(solution)/shard_map/ppermute | solution.py:256
  10.6 0.9 %copy-start.6 = (bf16[8,16,512]{2,1,0:T(8,128)(2,1)S(1)}, bf16[8,16,512]{2,1,0:T(8,128)(2,1)}, u32[]{:S(2)}) copy-start(bf16[8,16,512]{2,1,0:T(8,128)(2,1)} %refs_3_.3) | copy-start | bytes 393220
  11.5 0.9 %copy-start.8 = (bf16[8,16,512]{2,1,0:T(8,128)(2,1)S(1)}, bf16[8,16,512]{2,1,0:T(8,128)(2,1)}, u32[]{:S(2)}) copy-start(bf16[8,16,512]{2,1,0:T(8,128)(2,1)} %refs_6_.1) | copy-start | bytes 393220
  13.5 4.9 %collective-permute-start.5 = (bf16[5,16,512]{2,1,0:T(8,128)(2,1)S(1)}, bf16[5,16,512]{2,1,0:T(8,128)(2,1)S(1)}, u32[]{:S(2)}, u32[]{:S(2)}) collective-permute-start(bf16[5,16,512]{2,1,0:T(8,128)(2,1)S(1)} %get-tuple-element.17), channel_id=1, source_target_pairs={{0,16},{16,0},{1,17},{17,1},{2,18},{18,2},{3,19},{19,3},{4,20},{20... | collective-permute-start | bytes 245768 | tf_op jit(solution)/shard_map/ppermute | solution.py:253
  14.4 1.9 %collective-permute-start.3 = (bf16[2,16,512]{2,1,0:T(8,128)(2,1)S(1)}, bf16[2,16,512]{2,1,0:T(8,128)(2,1)S(1)}, u32[]{:S(2)}, u32[]{:S(2)}) collective-permute-start(bf16[2,16,512]{2,1,0:T(8,128)(2,1)S(1)} %get-tuple-element.15), channel_id=1, source_target_pairs={{0,1},{1,0},{2,3},{3,2},{4,5},{5,4},{6,7},{7,6},{8,9},{9,8},{10,11... | collective-permute-start | bytes 98312 | tf_op jit(solution)/shard_map/ppermute | solution.py:256
  14.4 3.9 %collective-permute-start.4 = (bf16[2,16,512]{2,1,0:T(8,128)(2,1)S(1)}, bf16[2,16,512]{2,1,0:T(8,128)(2,1)S(1)}, u32[]{:S(2)}, u32[]{:S(2)}) collective-permute-start(bf16[2,16,512]{2,1,0:T(8,128)(2,1)S(1)} %get-tuple-element.16), channel_id=1, source_target_pairs={{1,2},{2,1},{3,4},{4,3},{5,6},{6,5},{7,8},{8,7},{9,10},{10,9},{11,... | collective-permute-start | bytes 98312 | tf_op jit(solution)/shard_map/ppermute | solution.py:256
  18.3 1.0 %copy-start.1 = (f32[8,16,512]{2,1,0:T(8,128)S(1)}, f32[8,16,512]{2,1,0:T(8,128)}, u32[]{:S(2)}) copy-start(f32[8,16,512]{2,1,0:T(8,128)} %refs_1_.3) | copy-start | bytes 786436
  19.3 0.9 %copy-start.3 = (bf16[8,16,512]{2,1,0:T(8,128)(2,1)S(1)}, bf16[8,16,512]{2,1,0:T(8,128)(2,1)}, u32[]{:S(2)}) copy-start(bf16[8,16,512]{2,1,0:T(8,128)(2,1)} %refs_4_.3) | copy-start | bytes 393220
  20.2 0.9 %copy-start.5 = (bf16[8,16,512]{2,1,0:T(8,128)(2,1)S(1)}, bf16[8,16,512]{2,1,0:T(8,128)(2,1)}, u32[]{:S(2)}) copy-start(bf16[8,16,512]{2,1,0:T(8,128)(2,1)} %refs_5_.1) | copy-start | bytes 393220
  21.1 0.9 %copy-start.7 = (bf16[8,16,512]{2,1,0:T(8,128)(2,1)S(1)}, bf16[8,16,512]{2,1,0:T(8,128)(2,1)}, u32[]{:S(2)}) copy-start(bf16[8,16,512]{2,1,0:T(8,128)(2,1)} %refs_3_.3) | copy-start | bytes 393220
  22.0 0.9 %copy-start.9 = (bf16[8,16,512]{2,1,0:T(8,128)(2,1)S(1)}, bf16[8,16,512]{2,1,0:T(8,128)(2,1)}, u32[]{:S(2)}) copy-start(bf16[8,16,512]{2,1,0:T(8,128)(2,1)} %refs_6_.1) | copy-start | bytes 393220

commit v2 on v1

--- a/solution.py
+++ b/solution.py
@@ -12,6 +12,8 @@
 BT = 8
 BR = 128
 CAP = 2
+HEAD_R = 2
+GROUP = 4
 F32 = jnp.float32
 BF16 = jnp.bfloat16
 DIFFUSION = 0.05
@@ -55,9 +57,19 @@
             out_ref[2] = courant_z[rows_z - 1]
 
 
-def first_messages(density, courant_t, courant_z, sector_ref, even_ref, odd_ref):
-    pack_sector(density, courant_t, sector_ref)
-    pack_slab(density, courant_z, even_ref, odd_ref)
+def first_messages(count, *refs):
+    given, held = refs[:count], refs[count : 2 * count]
+    sector_out, even_out, odd_out, sems = refs[2 * count :]
+    copies = [pltpu.make_async_copy(given[i], held[i], sems.at[i]) for i in range(count)]
+    for copy in copies:
+        copy.start()
+    density, courant_t, courant_z = held[:3]
+    for copy in copies[:3]:
+        copy.wait()
+    pack_slab(density, courant_z, even_out, odd_out)
+    pack_sector(density, courant_t, sector_out)
+    for copy in copies[3:]:
+        copy.wait()
 
 
 def rates(values, sector, slab, faces_below, courants, ionization):
@@ -148,10 +160,12 @@
 
 
 def second_stage(count, *refs):
-    wanted, density, section, courant_r, courant_t, courant_z, ionization = refs[:7]
+    wanted_held, density, section, courant_r, courant_t, courant_z, ionization = refs[:7]
     left_faces, even_faces, odd_faces, even, odd = refs[7:12]
     sector = refs[12 : 12 + count]
-    evolved, outgoing, table, means = refs[12 + count :]
+    evolved, outgoing, table, means, wanted, sem = refs[12 + count :]
+    copy = pltpu.make_async_copy(wanted_held, wanted, sem)
+    copy.start()
     left, right, across = sector if count == 3 else sector * 3
     steps = rates(
         section,
@@ -170,6 +184,8 @@
         z = block // (blocks_t * blocks_r) * BZ
         t = block // blocks_r % blocks_t * BT
         r = block % blocks_r * BR
+        if r >= HEAD_R * BR:
+            continue
         tiles = [evolved[z + i, t : t + BT, r : r + BR] for i in range(BZ)]
         mean = jnp.mean(sum(tiles), axis=0, keepdims=True) * (1.0 / BZ)
         mean = jnp.broadcast_to(mean.astype(BF16).astype(F32), (BT, BR))
@@ -178,33 +194,42 @@
     means[total] = jnp.zeros((BT, BR), F32)
     table[total] = jnp.zeros((BLOCK_ROWS, BR), BF16)
     row = lax.broadcasted_iota(jnp.int32, (8, BR), 0)
+    copy.wait()
     for owner in range(outgoing.shape[0]):
         mean_rows = jnp.zeros((8, BR), F32)
         for slot in range(CAP):
-            block = wanted[0, owner, slot]
+            block = wanted[0, slot, owner]
             outgoing[owner, slot * BLOCK_ROWS : (slot + 1) * BLOCK_ROWS, :] = table[block]
             mean_rows = jnp.where(row == slot, means[block], mean_rows)
         outgoing[owner, MEAN_ROW:, :] = mean_rows.astype(BF16)
 
 
-def prolong_patches(slots, arrived, radial_matrix, tile_matrix, patches, spread, fine, sems):
-    sources = arrived.shape[0]
-    for source in range(sources):
+def prolong_patches(
+    slots_held, evolved, arrived, radial_matrix, tile_matrix, evolved_out, patches, spread, fine, slots, sems
+):
+    codes = pltpu.make_async_copy(slots_held, slots, sems.at[0])
+    codes.start()
+    copies = [pltpu.make_async_copy(evolved, evolved_out, sems.at[1])]
+    copies[0].start()
+    for source in range(arrived.shape[0]):
         spread[source] = jnp.dot(arrived[source], radial_matrix[...], preferred_element_type=F32)
-    copies = []
-    for p in range(fine.shape[0]):
-        code = slots[0, p]
-        source, slot = lax.shift_right_logical(code, 1), lax.bitwise_and(code, 1)
-        first = pl.multiple_of(slot * BLOCK_ROWS, BLOCK_ROWS)
-        coarse = spread[source, pl.ds(first, BLOCK_ROWS), :] + spread[source, pl.ds(MEAN_ROW + slot, 1), :]
-        high = coarse.astype(BF16)
-        low = (coarse - high.astype(F32)).astype(BF16)
-        fine[p] = jnp.dot(
-            tile_matrix[...], jnp.concatenate([high, low], axis=0), preferred_element_type=F32
-        )
-        copy = pltpu.make_async_copy(fine.at[p], patches.at[p], sems.at[p])
-        copy.start()
-        copies.append(copy)
+    codes.wait()
+    owned = fine.shape[0]
+    for first in range(0, owned, GROUP):
+        size = min(GROUP, owned - first)
+        for p in range(first, first + size):
+            code = slots[0, p]
+            source, slot = lax.shift_right_logical(code, 1), lax.bitwise_and(code, 1)
+            row = pl.multiple_of(slot * BLOCK_ROWS, BLOCK_ROWS)
+            coarse = spread[source, pl.ds(row, BLOCK_ROWS), :] + spread[source, pl.ds(MEAN_ROW + slot, 1), :]
+            high = coarse.astype(BF16)
+            low = (coarse - high.astype(F32)).astype(BF16)
+            fine[p] = jnp.dot(
+                tile_matrix[...], jnp.concatenate([high, low], axis=0), preferred_element_type=F32
+            )
+        part = pl.ds(first, size)
+        copies.append(pltpu.make_async_copy(fine.at[part], patches.at[part], sems.at[len(copies) + 1]))
+        copies[-1].start()
     for copy in copies:
         copy.wait()
 
@@ -223,10 +248,6 @@
     return [pl.BlockSpec(memory_space=pltpu.VMEM)] * count
 
 
-def in_smem(count):
-    return [pl.BlockSpec(memory_space=pltpu.SMEM)] * count
-
-
 PARAMS = pltpu.CompilerParams(vmem_limit_bytes=VMEM_LIMIT)
 
 
@@ -260,14 +281,21 @@
     slab_two = jax.ShapeDtypeStruct((2, cells_t, cells_r), BF16)
     field = jax.ShapeDtypeStruct(density.shape, F32)
 
-    sector, even, odd = pl.pallas_call(
-        first_messages,
-        out_shape=(sector_shape, slab_three, slab_three),
-        in_specs=in_vmem(3),
-        out_specs=tuple(in_vmem(3)),
+    given = (
+        density, courant_t, courant_z, courant_r, ionization, jnp.transpose(send_block, (0, 2, 1)), recv_slot
+    )
+    given = tuple(pltpu.with_memory_space_constraint(x, pltpu.HBM) for x in given)
+    *held, sector, even, odd = pl.pallas_call(
+        functools.partial(first_messages, len(given)),
+        out_shape=tuple(jax.ShapeDtypeStruct(x.shape, x.dtype) for x in given)
+        + (sector_shape, slab_three, slab_three),
+        in_specs=[pl.BlockSpec(memory_space=pltpu.HBM)] * len(given),
+        out_specs=tuple(in_vmem(len(given) + 3)),
+        scratch_shapes=[pltpu.SemaphoreType.DMA((len(given),))],
         compiler_params=PARAMS,
         name="first_messages",
-    )(density, courant_t, courant_z)
+    )(*given)
+    density, courant_t, courant_z, courant_r, ionization, wanted, slots = held
     sectors, even, odd = exchange(sector, even, odd)
     count = len(sectors)
 
@@ -285,16 +313,18 @@
     evolved, outgoing = pl.pallas_call(
         functools.partial(second_stage, count),
         out_shape=(field, jax.ShapeDtypeStruct((ax_count, CHUNK_ROWS, BR), BF16)),
-        in_specs=in_smem(1) + in_vmem(11 + count),
+        in_specs=in_vmem(12 + count),
         out_specs=tuple(in_vmem(2)),
         scratch_shapes=[
             pltpu.VMEM((blocks + 1, BLOCK_ROWS, BR), BF16),
             pltpu.VMEM((blocks + 1, BT, BR), F32),
+            pltpu.SMEM(wanted.shape, jnp.int32),
+            pltpu.SemaphoreType.DMA,
         ],
         compiler_params=PARAMS,
         name="second_stage",
     )(
-        send_block, density, section, courant_r, courant_t, courant_z, ionization,
+        wanted, density, section, courant_r, courant_t, courant_z, ionization,
         sectors[0], even, odd, even_two, odd_two, *sectors_two,
     )
 
@@ -304,19 +334,20 @@
     tile_matrix = jnp.asarray(np.concatenate([tile_matrix, tile_matrix], axis=1), BF16)
     radial_matrix = jnp.asarray(interp_matrix(BR).T, BF16)
     fine_rows = 4 * BZ * BT
-    patches = pl.pallas_call(
+    evolved, patches = pl.pallas_call(
         prolong_patches,
-        out_shape=jax.ShapeDtypeStruct((owned, fine_rows, 2 * BR), F32),
-        in_specs=in_smem(1) + in_vmem(3),
-        out_specs=pl.BlockSpec(memory_space=pl.ANY),
+        out_shape=(field, jax.ShapeDtypeStruct((owned, fine_rows, 2 * BR), F32)),
+        in_specs=in_vmem(5),
+        out_specs=(pl.BlockSpec(memory_space=pltpu.HBM),) * 2,
         scratch_shapes=[
             pltpu.VMEM((ax_count, CHUNK_ROWS, 2 * BR), F32),
             pltpu.VMEM((owned, fine_rows, 2 * BR), F32),
-            pltpu.SemaphoreType.DMA((owned,)),
+            pltpu.SMEM(slots.shape, jnp.int32),
+            pltpu.SemaphoreType.DMA((-(-owned // GROUP) + 2,)),
         ],
         compiler_params=PARAMS,
         name="prolong_patches",
-    )(recv_slot, arrived, radial_matrix, tile_matrix)
+    )(slots, evolved, arrived, radial_matrix, tile_matrix)
     return (evolved, patches.reshape(1, owned, 2 * BZ, 2 * BT, 2 * BR))
 
 

time: 44.4 us -> 34.6 us (0.78)
  local copies, waits for them, and re-layouts: 9.89 us -> 0.01 us
  waiting for transfers between devices: 5.97 us -> 6.72 us
  Pallas kernels: 6.39 us -> 5.85 us
    unnamed x27 -> x4, local copies, waits for them, and re-layouts: 9.89 us -> 0.01 us
    pallas_call x1, Pallas kernels: 2.35 us -> 1.05 us  [local(): pl.pallas_call(functools.partial(second_stage, count), out_shape=(field,...]
    pallas_call x2, Pallas kernels: 3.01 us -> 3.75 us  [the longest x1 2.49 us: local(): pl.pallas_call(prolong_patches, out_shape=(field, jax.ShapeDtypeStruct((o...]
    ppermute x2, waiting for transfers between devices: 4.89 us -> 5.59 us  [exchange(): lax.ppermute(odd, ('az', 'ax'), odd_pairs)]
  transfers between devices with their start and end apart: 6 -> 6, of which waited for: 3 -> 4; matrix products, arithmetic and copies ran while one was open for 2% -> 0% of each run, Pallas kernels for 0% -> 0%
where the time goes in v2:
time: 34.6 us; the launch traced here: 34.4 us
  blocking collectives  15.8 us (46%)
  waiting for transfers between devices  6.72 us (19%)
  Pallas kernels  5.85 us (17%)
  starting transfers between devices  5.28 us (15%)
  between operations  0.68 us (2%)
    all_to_all x1, blocking collectives, local(): lax.all_to_all(outgoing, 'ax', split_axis=0, concat_axis=0, tiled=True)  15.8 us
    ppermute x2, waiting for transfers between devices, exchange(): lax.ppermute(odd, ('az', 'ax'), odd_pairs)  5.59 us
    ppermute x2, starting transfers between devices, exchange(): sectors = [lax.ppermute(sector, 'az', by(1))]  3.97 us
    pallas_call x1, Pallas kernels, local(): pl.pallas_call(prolong_patches, out_shape=(field, jax.ShapeDtypeStruct((o...  2.49 us
    ppermute x2, starting transfers between devices, exchange(): lax.ppermute(odd, ('az', 'ax'), odd_pairs)  1.31 us
    pallas_call x1, Pallas kernels, local(): pl.pallas_call(functools.partial(first_messages, len(given)), out_shape=t...  1.26 us
    ppermute x2, waiting for transfers between devices, exchange(): lax.ppermute(even, 'ax', even_pairs)  1.13 us
    pallas_call x1, Pallas kernels, local(): pl.pallas_call(functools.partial(second_stage, count), out_shape=(field,...  1.05 us
  transfers between devices with their start and end apart: 6, of which 4 were waited for; matrix products, arithmetic and copies ran while one was open for 0% of the time, Pallas kernels for 0%

profile of v2, /device:TPU:0, one launch (start us, length us, event | category | flops | bytes accessed | tf_op | source)
XLA Modules:
  0.0 34.4 jit_solution(670671191741096687)
XLA Ops:
  0.6 0.0 copy-start
  0.6 0.0 copy-start.1
  0.7 1.3 %first_messages.1 = (f32[8,16,512]{2,1,0:T(8,128)S(1)}, bf16[8,16,512]{2,1,0:T(8,128)(2,1)S(1)}, bf16[8,16,512]{2,1,0:T(8,128)(2,1)S(1)}, bf16[8,16,512]{2,1,0:T...) custom-call(f32[8,16,512]{2,1,0:T(8,128)} %refs_0_.1, ...), custom_call_target="tpu_custom_call" | custom-call | tf_op jit(solution)/shard_map/first_messages/pallas_call | solution.py:288
  1.9 3.0 %collective-permute-start.2 = (bf16[5,16,512]{2,1,0:T(8,128)(2,1)S(1)}, bf16[5,16,512]{2,1,0:T(8,128)(2,1)S(1)}, u32[]{:S(2)}, u32[]{:S(2)}) collective-permute-start(bf16[5,16,512]{2,1,0:T(8,128)(2,1)S(1)} %get-tuple-element.29), channel_id=1, source_target_pairs={{0,16},{16,0},{1,17},{17,1},{2,18},{18,2},{3,19},{19,3},{4,20},{20... | collective-permute-start | bytes 245768 | tf_op jit(solution)/shard_map/ppermute | solution.py:274
  5.0 0.0 collective-permute-start
  5.0 0.2 collective-permute-start.1
  5.1 1.1 %collective-permute-done.refs_5_.refs_8_ = bf16[3,16,512]{2,1,0:T(8,128)(2,1)S(1)} collective-permute-done((bf16[3,16,512]{2,1,0:T(8,128)(2,1)S(1)}, bf16[3,16,512]{2,1,0:T(8,128)(2,1)S(1)}, u32[]{:S(2)}, u32[]{:S(2)}) %collective-permute-start) | collective-permute-done | bytes 49184 | tf_op jit(solution)/shard_map/ppermute | solution.py:277
  6.2 2.9 %collective-permute-done.1.refs_6_.refs_9_ = bf16[3,16,512]{2,1,0:T(8,128)(2,1)S(1)} collective-permute-done((bf16[3,16,512]{2,1,0:T(8,128)(2,1)S(1)}, bf16[3,16,512]{2,1,0:T(8,128)(2,1)S(1)}, u32[]{:S(2)}, u32[]{:S(2)}) %collective-permute-start.1) | collective-permute-done | bytes 49184 | tf_op jit(solution)/shard_map/ppermute | solution.py:277
  9.0 0.0 collective-permute-done.2.refs_7_
  9.1 1.0 %first_stage.1 = (f32[8,16,512]{2,1,0:T(8,128)S(1)}, bf16[5,16,512]{2,1,0:T(8,128)(2,1)S(1)}, bf16[2,16,512]{2,1,0:T(8,128)(2,1)S(1)}, bf16[2,16,512]{2,1,0:T(8,128)(2,1)S(1)}) custom-call(f32[8,16,512]{2,1,0:T(8,128)S(1)} %get-tuple-element.22.refs_0_.refs_1_, bf16[8,16,512]{2,1,0:T(8,128)(2,1)S(1)} %get-tuple-element.23.refs_1_.refs_3_, ...), custom_call_target="tpu_custom_call" | custom-call | tf_op jit(solution)/shard_map/first_stage/pallas_call | solution.py:302
  10.1 0.9 %collective-permute-start.5 = (bf16[5,16,512]{2,1,0:T(8,128)(2,1)S(1)}, bf16[5,16,512]{2,1,0:T(8,128)(2,1)S(1)}, u32[]{:S(2)}, u32[]{:S(2)}) collective-permute-start(bf16[5,16,512]{2,1,0:T(8,128)(2,1)S(1)} %get-tuple-element.33), channel_id=1, source_target_pairs={{0,16},{16,0},{1,17},{17,1},{2,18},{18,2},{3,19},{19,3},{4,20},{20... | collective-permute-start | bytes 245768 | tf_op jit(solution)/shard_map/ppermute | solution.py:274
  11.0 0.0 collective-permute-start.3
  11.0 1.2 %collective-permute-start.4 = (bf16[2,16,512]{2,1,0:T(8,128)(2,1)S(1)}, bf16[2,16,512]{2,1,0:T(8,128)(2,1)S(1)}, u32[]{:S(2)}, u32[]{:S(2)}) collective-permute-start(bf16[2,16,512]{2,1,0:T(8,128)(2,1)S(1)} %get-tuple-element.32), channel_id=1, source_target_pairs={{1,2},{2,1},{3,4},{4,3},{5,6},{6,5},{7,8},{8,7},{9,10},{10,9},{11,... | collective-permute-start | bytes 98312 | tf_op jit(solution)/shard_map/ppermute | solution.py:277
  12.2 0.1 collective-permute-done.3.refs_10_
  12.2 2.7 %collective-permute-done.4.refs_11_ = bf16[2,16,512]{2,1,0:T(8,128)(2,1)S(1)} collective-permute-done((bf16[2,16,512]{2,1,0:T(8,128)(2,1)S(1)}, bf16[2,16,512]{2,1,0:T(8,128)(2,1)S(1)}, u32[]{:S(2)}, u32[]{:S(2)}) %collective-permute-start.4) | collective-permute-done | bytes 32800 | tf_op jit(solution)/shard_map/ppermute | solution.py:277
  15.0 0.0 collective-permute-done.5.refs_12_
  15.0 1.1 %second_stage.1 = (f32[8,16,512]{2,1,0:T(8,128)S(1)}, bf16[16,72,128]{2,1,0:T(8,128)(2,1)S(1)}) custom-call(s32[1,2,16]{2,1,0:T(2,128)S(1)} %get-tuple-element.21.refs_0_, f32[8,16,512]{2,1,0:T(8,128)S(1)} %get-tuple-element.22.refs_0_.refs_1_, f32[8,16,512]{2,1,0:T(8,128)S(1)} %get-tuple-element.30.refs_2_, ...), custom_call_target="tpu_custom_call" | custom-call | tf_op jit(solution)/shard_map/second_stage/pallas_call | solution.py:313
  16.0 15.8 %all_to_all.5.arrived = bf16[16,72,128]{2,1,0:T(8,128)(2,1)S(1)} all-to-all(bf16[16,72,128]{2,1,0:T(8,128)(2,1)S(1)} %get-tuple-element.35), channel_id=1, replica_groups=mesh['az'=2,'ax'=16] {'ax'}, dimensions={0} | all-to-all | bytes 589824 | tf_op jit(solution)/shard_map/all_to_all | solution.py:331
  31.9 0.0 copy-done
  31.9 0.0 copy-done.1
  31.9 2.5 %prolong_patches.1 = (f32[8,16,512]{2,1,0:T(8,128)}, f32[24,128,256]{2,1,0:T(8,128)}) custom-call(s32[1,24]{1,0:T(1,128)S(1)} %get-tuple-element.20.slots_held, f32[8,16,512]{2,1,0:T(8,128)S(1)} %get-tuple-element.34.evolved, bf16[16,72,128]{2,1,0:T(8,128)(2,1)S(1)} %all_to_all.5.arrived, bf16[128,256]{1,0:T(8,128)(2,1)S(1)} %copy-done, ...), custom_call_target="tpu_custom_call" | custom-call | tf_op jit(solution)/shard_map/prolong_patches/pallas_call | solution.py:337
Async XLA Ops:
  0.6 31.2 %copy-start = (bf16[128,256]{1,0:T(8,128)(2,1)S(1)}, bf16[128,256]{1,0:T(8,128)(2,1)}, u32[]{:S(2)}) copy-start(bf16[128,256]{1,0:T(8,128)(2,1)} %constant.5.clone.radial_matrix) | copy-start | bytes 196612
  0.6 31.2 %copy-start.1 = (bf16[128,64]{1,0:T(8,128)(2,1)S(1)}, bf16[128,64]{1,0:T(8,128)(2,1)}, u32[]{:S(2)}) copy-start(bf16[128,64]{1,0:T(8,128)(2,1)} %constant.4.clone.tile_matrix) | copy-start | bytes 49156
  1.9 7.1 %collective-permute-start.2 = (bf16[5,16,512]{2,1,0:T(8,128)(2,1)S(1)}, bf16[5,16,512]{2,1,0:T(8,128)(2,1)S(1)}, u32[]{:S(2)}, u32[]{:S(2)}) collective-permute-start(bf16[5,16,512]{2,1,0:T(8,128)(2,1)S(1)} %get-tuple-element.29), channel_id=1, source_target_pairs={{0,16},{16,0},{1,17},{17,1},{2,18},{18,2},{3,19},{19,3},{4,20},{20... | collective-permute-start | bytes 245768 | tf_op jit(solution)/shard_map/ppermute | solution.py:274
  5.0 1.2 %collective-permute-start = (bf16[3,16,512]{2,1,0:T(8,128)(2,1)S(1)}, bf16[3,16,512]{2,1,0:T(8,128)(2,1)S(1)}, u32[]{:S(2)}, u32[]{:S(2)}) collective-permute-start(bf16[3,16,512]{2,1,0:T(8,128)(2,1)S(1)} %get-tuple-element.27), channel_id=1, source_target_pairs={{0,1},{1,0},{2,3},{3,2},{4,5},{5,4},{6,7},{7,6},{8,9},{9,8},{10,11... | collective-permute-start | bytes 147464 | tf_op jit(solution)/shard_map/ppermute | solution.py:277
  5.0 4.1 %collective-permute-start.1 = (bf16[3,16,512]{2,1,0:T(8,128)(2,1)S(1)}, bf16[3,16,512]{2,1,0:T(8,128)(2,1)S(1)}, u32[]{:S(2)}, u32[]{:S(2)}) collective-permute-start(bf16[3,16,512]{2,1,0:T(8,128)(2,1)S(1)} %get-tuple-element.28), channel_id=1, source_target_pairs={{1,2},{2,1},{3,4},{4,3},{5,6},{6,5},{7,8},{8,7},{9,10},{10,9},{11,... | collective-permute-start | bytes 147464 | tf_op jit(solution)/shard_map/ppermute | solution.py:277
  10.1 4.9 %collective-permute-start.5 = (bf16[5,16,512]{2,1,0:T(8,128)(2,1)S(1)}, bf16[5,16,512]{2,1,0:T(8,128)(2,1)S(1)}, u32[]{:S(2)}, u32[]{:S(2)}) collective-permute-start(bf16[5,16,512]{2,1,0:T(8,128)(2,1)S(1)} %get-tuple-element.33), channel_id=1, source_target_pairs={{0,16},{16,0},{1,17},{17,1},{2,18},{18,2},{3,19},{19,3},{4,20},{20... | collective-permute-start | bytes 245768 | tf_op jit(solution)/shard_map/ppermute | solution.py:274
  11.0 1.2 %collective-permute-start.3 = (bf16[2,16,512]{2,1,0:T(8,128)(2,1)S(1)}, bf16[2,16,512]{2,1,0:T(8,128)(2,1)S(1)}, u32[]{:S(2)}, u32[]{:S(2)}) collective-permute-start(bf16[2,16,512]{2,1,0:T(8,128)(2,1)S(1)} %get-tuple-element.31), channel_id=1, source_target_pairs={{0,1},{1,0},{2,3},{3,2},{4,5},{5,4},{6,7},{7,6},{8,9},{9,8},{10,11... | collective-permute-start | bytes 98312 | tf_op jit(solution)/shard_map/ppermute | solution.py:277
  11.0 3.9 %collective-permute-start.4 = (bf16[2,16,512]{2,1,0:T(8,128)(2,1)S(1)}, bf16[2,16,512]{2,1,0:T(8,128)(2,1)S(1)}, u32[]{:S(2)}, u32[]{:S(2)}) collective-permute-start(bf16[2,16,512]{2,1,0:T(8,128)(2,1)S(1)} %get-tuple-element.32), channel_id=1, source_target_pairs={{1,2},{2,1},{3,4},{4,3},{5,6},{6,5},{7,8},{8,7},{9,10},{10,9},{11,... | collective-permute-start | bytes 98312 | tf_op jit(solution)/shard_map/ppermute | solution.py:277

commit v3 on v2

--- a/solution.py
+++ b/solution.py
@@ -29,20 +29,29 @@
     row = lax.broadcasted_iota(jnp.int32, (8, cells_r), 0)
     lane = lax.broadcasted_iota(jnp.int32, (cells_t, 128), 1)
     inner = jnp.zeros((cells_t, 128), F32)
-    tiles = []
+    ends = []
     for k in range(rows_z):
-        tile = jnp.where(row < 2, values[k, 0:8, :], values[k, cells_t - 8 :, :])
-        if courant_t is not None:
+        ends.append(jnp.where(row < 2, values[k, 0:8, :], values[k, cells_t - 8 :, :]))
+        inner = jnp.where(lane == k, values[k, :, 0:1], inner)
+    outer = (row < 2) | (row > 5)
+    tiles = [
+        jnp.where(outer, ends[k], pltpu.roll(ends[k + 1], 4, 0)) for k in range(0, rows_z, 2)
+    ]
+    faces = jnp.zeros((8, cells_r), F32)
+    if courant_t is not None:
+        for k in range(rows_z):
             face = courant_t[k].astype(F32)[cells_t - 8 :, :]
-            tile = jnp.where(row == 5, pltpu.roll(face, 6, 0), tile)
-        tiles.append(tile)
-        inner = jnp.where(lane == k, values[k, :, 0:1], inner)
-    for pair in range(rows_z // 2):
+            faces = jnp.where(row == k, pltpu.roll(face, (k + 1) % 8, 0), faces)
+    tiles.append(faces)
+    rounded = inner.astype(BF16).astype(F32)
+    rest = inner - rounded
+    tiles.append(jnp.concatenate([rounded[:8], rounded[8:], rest[:8], rest[8:]], axis=1))
+    for pair in range(len(tiles) // 2):
         out_ref[pair] = jnp.concatenate(tiles[2 * pair : 2 * pair + 2], axis=0).astype(BF16)
-    rounded = inner.astype(BF16)
-    out_ref[rows_z // 2, :, 0:128] = rounded
-    out_ref[rows_z // 2, :, 128:256] = (inner - rounded.astype(F32)).astype(BF16)
-    out_ref[rows_z // 2, :, 256:] = jnp.zeros((cells_t, cells_r - 256), BF16)
+
+
+def tile_of(msg, index):
+    return msg[index // 2].astype(F32)[(index % 2) * 8 : (index % 2) * 8 + 8, :]
 
 
 def pack_slab(values, courant_z, even_ref, odd_ref):
@@ -72,7 +81,47 @@
         copy.wait()
 
 
-def rates(values, sector, slab, faces_below, courants, ionization):
+def axial_flux(courant, back, here, up, up_two):
+    low = here + 0.25 * (up - back)
+    high = up - 0.25 * (up_two - here)
+    return courant * jnp.where(courant > 0.0, low, high)
+
+
+def inner_rates(values, courant_r, courant_z, ionization):
+    rows_z, cells_t, cells_r = values.shape
+    zero = jnp.zeros((cells_t, cells_r), F32)
+
+    def row_at(k):
+        return values[k] if 0 <= k < rows_z else zero
+
+    lane = lax.broadcasted_iota(jnp.int32, (cells_t, cells_r), 1)
+    index = lane.astype(F32)
+    area = jnp.where(lane < cells_r - 1, index + 1.0, 0.0)
+    inverse_radius = 1.0 / (index + 0.5)
+    flux_z = zero
+    for k in range(rows_z):
+        here, back, up = row_at(k), row_at(k - 1), row_at(k + 1)
+        next_flux = zero
+        if k < rows_z - 1:
+            next_flux = axial_flux(courant_z[k].astype(F32), back, here, up, row_at(k + 2))
+        rate = (
+            DIFFUSION * (up - 2.0 * here + back)
+            + ionization[k].astype(F32) * here
+            - (next_flux - flux_z)
+        )
+        flux_z = next_flux
+        inward = jnp.where(lane == 0, 0.0, pltpu.roll(here, 1, 1))
+        outward = jnp.where(lane == cells_r - 1, 0.0, pltpu.roll(here, cells_r - 1, 1))
+        quarter = 0.25 * (outward - inward)
+        courant = courant_r[k].astype(F32)
+        flux = courant * jnp.where(
+            courant > 0.0, here + quarter, pltpu.roll(here - quarter, cells_r - 1, 1)
+        )
+        carried = area * (DIFFUSION * (outward - here) - flux)
+        yield rate + (carried - pltpu.roll(carried, 1, 1)) * inverse_radius
+
+
+def outer_rates(values, sector, slab, faces_below, courants):
     rows_z, cells_t, cells_r = values.shape
     left, right, across = sector
     even_msg, odd_msg = slab
@@ -90,93 +139,94 @@
     def above(even, odd):
         return jnp.where(has_above, jnp.where(is_even, even, odd).astype(F32), zero)
 
-    def row_at(k):
-        if k < 0:
-            return below(even_msg[k + 2], odd_msg[k + 2])
-        if k >= rows_z:
-            return above(even_msg[k - rows_z], odd_msg[k - rows_z])
-        return values[k]
-
-    lane = lax.broadcasted_iota(jnp.int32, (cells_t, cells_r), 1)
-    index = lane.astype(F32)
-    area = jnp.where(lane < cells_r - 1, index + 1.0, 0.0)
-    inverse_radius = 1.0 / (index + 0.5)
-    inner = across[rows_z // 2, :, 0:128].astype(F32) + across[rows_z // 2, :, 128:256].astype(F32)
+    top = rows_z - 1
+    below_one, below_two = below(even_msg[1], odd_msg[1]), below(even_msg[0], odd_msg[0])
+    above_one, above_two = above(even_msg[0], odd_msg[0]), above(even_msg[1], odd_msg[1])
+    first_flux = axial_flux(
+        below(even_faces[2], odd_faces[2]), below_two, below_one, values[0], values[1]
+    )
+    last_flux = axial_flux(
+        courant_z[top].astype(F32), values[top - 1], values[top], above_one, above_two
+    )
+    low_change = -0.25 * jnp.maximum(courant_z[0].astype(F32), 0.0) * below_one
+    high_change = -0.25 * jnp.minimum(courant_z[top - 1].astype(F32), 0.0) * above_one
+    axial = {
+        0: first_flux - low_change + DIFFUSION * below_one,
+        1: low_change,
+        top - 1: -high_change,
+        top: high_change - last_flux + DIFFUSION * above_one,
+    }
     halo_row = lax.broadcasted_iota(jnp.int32, (8, cells_r), 0)
-
-    def tile_of(msg, k):
-        return msg[k // 2].astype(F32)[(k % 2) * 8 : (k % 2) * 8 + 8, :]
-
-    def axial_flux(courant, back, here, up, up_two):
-        low = here + 0.25 * (up - back)
-        high = up - 0.25 * (up_two - here)
-        return courant * jnp.where(courant > 0.0, low, high)
-
-    flux_z = axial_flux(
-        below(even_faces[2], odd_faces[2]), row_at(-2), row_at(-1), row_at(0), row_at(1)
-    )
+    lane = lax.broadcasted_iota(jnp.int32, (cells_t, 128), 1)
+    packed = tile_of(across, rows_z // 2 + 1)
+    packed = packed[:, 0:256] + packed[:, 256:512]
+    inner = jnp.concatenate([packed[:, 0:128], packed[:, 128:256]], axis=0)
+    faces = tile_of(left_faces, rows_z // 2)
+    rows = cells_t + 8
     for k in range(rows_z):
-        here, back, up = row_at(k), row_at(k - 1), row_at(k + 1)
-        next_flux = axial_flux(courant_z[k].astype(F32), back, here, up, row_at(k + 2))
-        rate = (
-            DIFFUSION * (up - 2.0 * here + back)
-            + ionization[k].astype(F32) * here
-            - (next_flux - flux_z)
-        )
-        flux_z = next_flux
-        halo = tile_of(left, k)
+        here = values[k]
+        halo = tile_of(left, k // 2)
         if right is not left:
-            halo = jnp.where(halo_row < 4, tile_of(right, k), halo)
-        face_halo = pltpu.roll(tile_of(left_faces, k), 2, 0)
+            beyond = (halo_row < 2) | (halo_row == 4) | (halo_row == 5)
+            halo = jnp.where(beyond, tile_of(right, k // 2), halo)
+        if k % 2:
+            halo = pltpu.roll(halo, 4, 0)
         ring = jnp.concatenate([halo, here], axis=0)
-        rows = cells_t + 8
+        face_halo = pltpu.roll(faces, 7 - k, 0)
         courant = jnp.concatenate([face_halo, courant_t[k].astype(F32)], axis=0)
         quarter = 0.25 * (pltpu.roll(ring, rows - 1, 0) - pltpu.roll(ring, 1, 0))
         flux = courant * jnp.where(courant > 0.0, ring + quarter, pltpu.roll(ring - quarter, rows - 1, 0))
-        rate = rate - (flux - pltpu.roll(flux, 1, 0))[8:, :]
-        inward = jnp.where(lane == 0, inner[:, k : k + 1], pltpu.roll(here, 1, 1))
-        outward = jnp.where(lane == cells_r - 1, 0.0, pltpu.roll(here, cells_r - 1, 1))
-        quarter = 0.25 * (outward - inward)
-        courant = courant_r[k].astype(F32)
-        flux = courant * jnp.where(
-            courant > 0.0, here + quarter, pltpu.roll(here - quarter, cells_r - 1, 1)
-        )
-        carried = area * (DIFFUSION * (outward - here) - flux)
-        yield rate + (carried - pltpu.roll(carried, 1, 1)) * inverse_radius
+        rate = (pltpu.roll(flux, 1, 0) - flux)[8:, :]
+        if k in axial:
+            rate = rate + axial[k]
+        change = 0.25 * jnp.maximum(courant_r[k, :, 0:128].astype(F32), 0.0)
+        change = change * (pltpu.roll(inner, 128 - k, 1) if k else inner)
+        change = jnp.where(lane == 0, change, 0.0)
+        change = 2.0 * change - (1.0 / 1.5) * pltpu.roll(change, 1, 1)
+        yield jnp.concatenate([rate[:, 0:128] + change, rate[:, 128:]], axis=1)
+
+
+def first_inner(density, courant_r, courant_z, ionization, partial):
+    for k, rate in enumerate(inner_rates(density, courant_r, courant_z, ionization)):
+        partial[k] = density[k] + rate
+
+
+def second_inner(density, section, courant_r, courant_z, ionization, partial):
+    for k, rate in enumerate(inner_rates(section, courant_r, courant_z, ionization)):
+        partial[k] = 0.5 * (density[k] + section[k] + rate)
 
 
 def first_stage(count, *refs):
-    density, courant_r, courant_t, courant_z, ionization, even, odd = refs[:7]
-    sector = refs[7 : 7 + count]
-    section, sector_out, even_out, odd_out = refs[7 + count :]
+    odd, sector, refs = refs[0], refs[1 : 1 + count], refs[1:]
+    even, partial, density, courant_r, courant_t, courant_z = refs[count : count + 6]
+    section, sector_out, even_out, odd_out = refs[count + 6 :]
     left, right, across = sector if count == 3 else sector * 3
-    steps = rates(
-        density, (left, right, across), (even, odd), (left, even, odd), (courant_r, courant_t, courant_z), ionization
+    steps = outer_rates(
+        density, (left, right, across), (even, odd), (left, even, odd), (courant_r, courant_t, courant_z)
     )
     for k, rate in enumerate(steps):
-        section[k] = density[k] + rate
+        section[k] = partial[k] + rate
     pack_sector(section, None, sector_out)
     pack_slab(section, None, even_out, odd_out)
 
 
 def second_stage(count, *refs):
-    wanted_held, density, section, courant_r, courant_t, courant_z, ionization = refs[:7]
-    left_faces, even_faces, odd_faces, even, odd = refs[7:12]
-    sector = refs[12 : 12 + count]
-    evolved, outgoing, table, means, wanted, sem = refs[12 + count :]
+    odd, sector, refs = refs[0], refs[1 : 1 + count], refs[1:]
+    even, partial, wanted_held, section, courant_r, courant_t, courant_z = refs[count : count + 7]
+    left_faces, even_faces, odd_faces = refs[count + 7 : count + 10]
+    evolved, outgoing, table, means, wanted, sem = refs[count + 10 :]
     copy = pltpu.make_async_copy(wanted_held, wanted, sem)
     copy.start()
     left, right, across = sector if count == 3 else sector * 3
-    steps = rates(
+    steps = outer_rates(
         section,
         (left, right, across),
         (even, odd),
         (left_faces, even_faces, odd_faces),
         (courant_r, courant_t, courant_z),
-        ionization,
     )
     for k, rate in enumerate(steps):
-        evolved[k] = 0.5 * (density[k] + section[k] + rate)
+        evolved[k] = partial[k] + 0.5 * rate
     rows_z, cells_t, cells_r = evolved.shape
     blocks_t, blocks_r = cells_t // BT, cells_r // BR
     total = rows_z // BZ * blocks_t * blocks_r
@@ -276,9 +326,9 @@
             sectors = [lax.ppermute(sector, "az", by(s)) for s in (1, az_count - 1, az_count // 2)]
         return sectors, lax.ppermute(even, "ax", even_pairs), lax.ppermute(odd, ("az", "ax"), odd_pairs)
 
-    sector_shape = jax.ShapeDtypeStruct((rows_z // 2 + 1, cells_t, cells_r), BF16)
+    sector_shape = jax.ShapeDtypeStruct((rows_z // 4 + 1, cells_t, cells_r), BF16)
     slab_three = jax.ShapeDtypeStruct((3, cells_t, cells_r), BF16)
-    slab_two = jax.ShapeDtypeStruct((2, cells_t, cells_r), BF16)
+    slab_two = jax.ShapeDtypeStruct((3, cells_t, cells_r), BF16)
     field = jax.ShapeDtypeStruct(density.shape, F32)
 
     given = (
@@ -299,6 +349,16 @@
     sectors, even, odd = exchange(sector, even, odd)
     count = len(sectors)
 
+    inner_cost = pl.CostEstimate(flops=40 * density.size, bytes_accessed=16 * density.size, transcendentals=0)
+    partial = pl.pallas_call(
+        first_inner,
+        out_shape=field,
+        in_specs=in_vmem(4),
+        out_specs=in_vmem(1)[0],
+        compiler_params=PARAMS,
+        cost_estimate=inner_cost,
+        name="first_inner",
+    )(density, courant_r, courant_z, ionization)
     section, sector, even_two, odd_two = pl.pallas_call(
         functools.partial(first_stage, count),
         out_shape=(field, sector_shape, slab_two, slab_two),
@@ -306,14 +366,23 @@
         out_specs=tuple(in_vmem(4)),
         compiler_params=PARAMS,
         name="first_stage",
-    )(density, courant_r, courant_t, courant_z, ionization, even, odd, *sectors)
+    )(odd, *sectors, even, partial, density, courant_r, courant_t, courant_z)
     sectors_two, even_two, odd_two = exchange(sector, even_two, odd_two)
 
+    partial = pl.pallas_call(
+        second_inner,
+        out_shape=field,
+        in_specs=in_vmem(5),
+        out_specs=in_vmem(1)[0],
+        compiler_params=PARAMS,
+        cost_estimate=inner_cost,
+        name="second_inner",
+    )(density, section, courant_r, courant_z, ionization)
     blocks = rows_z // BZ * (cells_t // BT) * (cells_r // BR)
     evolved, outgoing = pl.pallas_call(
         functools.partial(second_stage, count),
         out_shape=(field, jax.ShapeDtypeStruct((ax_count, CHUNK_ROWS, BR), BF16)),
-        in_specs=in_vmem(12 + count),
+        in_specs=in_vmem(11 + count),
         out_specs=tuple(in_vmem(2)),
         scratch_shapes=[
             pltpu.VMEM((blocks + 1, BLOCK_ROWS, BR), BF16),
@@ -324,8 +393,8 @@
         compiler_params=PARAMS,
         name="second_stage",
     )(
-        wanted, density, section, courant_r, courant_t, courant_z, ionization,
-        sectors[0], even, odd, even_two, odd_two, *sectors_two,
+        odd_two, *sectors_two, even_two, partial, wanted, section, courant_r, courant_t, courant_z,
+        sectors[0], even, odd,
     )
 
     arrived = lax.all_to_all(outgoing, "ax", split_axis=0, concat_axis=0, tiled=True)

time: 34.6 us -> 32.9 us (0.951)
  waiting for transfers between devices: 6.72 us -> 4.43 us
  starting transfers between devices: 5.28 us -> 6.4 us
  blocking collectives: 15.8 us -> 15 us
    ppermute x2, waiting for transfers between devices: 5.59 us -> 1.41 us  [exchange(): lax.ppermute(odd, ('az', 'ax'), odd_pairs)]
    ppermute x2, waiting for transfers between devices: 0.01 us -> 3.01 us  [exchange(): sectors = [lax.ppermute(sector, 'az', by(1))]]
    ppermute x2, starting transfers between devices: 3.97 us -> 1.11 us  [exchange(): sectors = [lax.ppermute(sector, 'az', by(1))]]
    ppermute x2, starting transfers between devices: 1.31 us -> 4.04 us  [exchange(): lax.ppermute(odd, ('az', 'ax'), odd_pairs)]
    pallas_call x0 -> x2, Pallas kernels: none -> 1.38 us  [the longest x1 0.7 us: local(): pl.pallas_call(second_inner, out_shape=field, in_specs=in_vmem(5), out_sp...]
    ppermute x2, starting transfers between devices: 0.01 us -> 1.25 us  [exchange(): lax.ppermute(even, 'ax', even_pairs)]
    ppermute x2, waiting for transfers between devices: 1.13 us -> 0.01 us  [exchange(): lax.ppermute(even, 'ax', even_pairs)]
    all_to_all x1, blocking collectives: 15.8 us -> 15 us  [local(): lax.all_to_all(outgoing, 'ax', split_axis=0, concat_axis=0, tiled=True)]
  transfers between devices with their start and end apart: 6 -> 6, of which waited for: 4 -> 3; matrix products, arithmetic and copies ran while one was open for 0% -> 0% of each run, Pallas kernels for 0% -> 4%
where the time goes in v3:
time: 32.9 us; the launch traced here: 32.7 us
  blocking collectives  15 us (46%)
  starting transfers between devices  6.4 us (19%)
  Pallas kernels  6.16 us (19%)
  waiting for transfers between devices  4.43 us (13%)
  between operations  0.68 us (2%)
    all_to_all x1, blocking collectives, local(): lax.all_to_all(outgoing, 'ax', split_axis=0, concat_axis=0, tiled=True)  15 us
    ppermute x2, starting transfers between devices, exchange(): lax.ppermute(odd, ('az', 'ax'), odd_pairs)  4.04 us
    ppermute x2, waiting for transfers between devices, exchange(): sectors = [lax.ppermute(sector, 'az', by(1))]  3.01 us
    pallas_call x1, Pallas kernels, local(): pl.pallas_call(prolong_patches, out_shape=(field, jax.ShapeDtypeStruct((o...  2.49 us
    ppermute x2, waiting for transfers between devices, exchange(): lax.ppermute(odd, ('az', 'ax'), odd_pairs)  1.41 us
    pallas_call x1, Pallas kernels, local(): pl.pallas_call(functools.partial(first_messages, len(given)), out_shape=t...  1.25 us
    ppermute x2, starting transfers between devices, exchange(): lax.ppermute(even, 'ax', even_pairs)  1.25 us
    ppermute x2, starting transfers between devices, exchange(): sectors = [lax.ppermute(sector, 'az', by(1))]  1.11 us
  transfers between devices with their start and end apart: 6, of which 3 were waited for; matrix products, arithmetic and copies ran while one was open for 0% of the time, Pallas kernels for 4%

profile of v3, /device:TPU:0, one launch (start us, length us, event | category | flops | bytes accessed | tf_op | source)
XLA Modules:
  0.0 32.7 jit_solution(5697738131268967703)
XLA Ops:
  0.6 0.0 copy-start
  0.6 0.0 copy-start.1
  0.7 1.3 %first_messages.1 = (f32[8,16,512]{2,1,0:T(8,128)S(1)}, bf16[8,16,512]{2,1,0:T(8,128)(2,1)S(1)}, bf16[8,16,512]{2,1,0:T(8,128)(2,1)S(1)}, bf16[8,16,512]{2,1,0:T...) custom-call(f32[8,16,512]{2,1,0:T(8,128)} %refs_0_.1, ...), custom_call_target="tpu_custom_call" | custom-call | tf_op jit(solution)/shard_map/first_messages/pallas_call | solution.py:338
  1.9 3.0 %collective-permute-start = (bf16[3,16,512]{2,1,0:T(8,128)(2,1)S(1)}, bf16[3,16,512]{2,1,0:T(8,128)(2,1)S(1)}, u32[]{:S(2)}, u32[]{:S(2)}) collective-permute-start(bf16[3,16,512]{2,1,0:T(8,128)(2,1)S(1)} %get-tuple-element.21), channel_id=1, source_target_pairs={{1,2},{2,1},{3,4},{4,3},{5,6},{6,5},{7,8},{8,7},{9,10},{10,9},{11,... | collective-permute-start | bytes 147464 | tf_op jit(solution)/shard_map/ppermute | solution.py:327
  5.0 0.1 collective-permute-start.1
  5.0 1.2 %collective-permute-start.2 = (bf16[3,16,512]{2,1,0:T(8,128)(2,1)S(1)}, bf16[3,16,512]{2,1,0:T(8,128)(2,1)S(1)}, u32[]{:S(2)}, u32[]{:S(2)}) collective-permute-start(bf16[3,16,512]{2,1,0:T(8,128)(2,1)S(1)} %get-tuple-element.23), channel_id=1, source_target_pairs={{0,1},{1,0},{2,3},{3,2},{4,5},{5,4},{6,7},{7,6},{8,9},{9,8},{10,11... | collective-permute-start | bytes 147464 | tf_op jit(solution)/shard_map/ppermute | solution.py:327
  6.3 0.7 %first_inner.1.refs_3_ = f32[8,16,512]{2,1,0:T(8,128)S(1)} custom-call(f32[8,16,512]{2,1,0:T(8,128)S(1)} %get-tuple-element.24.density.refs_4_, bf16[8,16,512]{2,1,0:T(8,128)(2,1)S(1)} %get-tuple-element.25.courant_r.refs_5_.refs_6_, bf16[8,16,512]{2,1,0:T(8,128)(2,1)S(1)} %get-tuple-element.26.courant_z.refs_7_.refs_8_, ...), custom_call_target="tpu_custom_call" | custom-call | flops 2621440 | bytes 1048576 | tf_op jit(solution)/shard_map/first_inner/pallas_call | solution.py:353
  7.0 0.1 collective-permute-done.refs_0_.refs_11_
  7.0 2.0 %collective-permute-done.1.refs_1_.refs_9_ = bf16[3,16,512]{2,1,0:T(8,128)(2,1)S(1)} collective-permute-done((bf16[3,16,512]{2,1,0:T(8,128)(2,1)S(1)}, bf16[3,16,512]{2,1,0:T(8,128)(2,1)S(1)}, u32[]{:S(2)}, u32[]{:S(2)}) %collective-permute-start.1) | collective-permute-done | bytes 49184 | tf_op jit(solution)/shard_map/ppermute | solution.py:324
  9.0 0.0 collective-permute-done.2.refs_2_.refs_10_
  9.0 0.4 %first_stage.1 = (f32[8,16,512]{2,1,0:T(8,128)S(1)}, bf16[3,16,512]{2,1,0:T(8,128)(2,1)S(1)}, bf16[3,16,512]{2,1,0:T(8,128)(2,1)S(1)}, bf16[3,16,512]{2,1,0:T(8,128)(2,1)S(1)}) custom-call(bf16[3,16,512]{2,1,0:T(8,128)(2,1)S(1)} %collective-permute-done.refs_0_.refs_11_, bf16[3,16,512]{2,1,0:T(8,128)(2,1)S(1)} %collective-permute-done.1.refs_1_.refs_9_, ...), custom_call_target="tpu_custom_call" | custom-call | tf_op jit(solution)/shard_map/first_stage/pallas_call | solution.py:362
  9.5 1.0 %collective-permute-start.3 = (bf16[3,16,512]{2,1,0:T(8,128)(2,1)S(1)}, bf16[3,16,512]{2,1,0:T(8,128)(2,1)S(1)}, u32[]{:S(2)}, u32[]{:S(2)}) collective-permute-start(bf16[3,16,512]{2,1,0:T(8,128)(2,1)S(1)} %get-tuple-element.29), channel_id=1, source_target_pairs={{1,2},{2,1},{3,4},{4,3},{5,6},{6,5},{7,8},{8,7},{9,10},{10,9},{11,... | collective-permute-start | bytes 147464 | tf_op jit(solution)/shard_map/ppermute | solution.py:327
  10.5 1.0 %collective-permute-start.4 = (bf16[3,16,512]{2,1,0:T(8,128)(2,1)S(1)}, bf16[3,16,512]{2,1,0:T(8,128)(2,1)S(1)}, u32[]{:S(2)}, u32[]{:S(2)}) collective-permute-start(bf16[3,16,512]{2,1,0:T(8,128)(2,1)S(1)} %get-tuple-element.30), channel_id=1, source_target_pairs={{0,16},{16,0},{1,17},{17,1},{2,18},{18,2},{3,19},{19,3},{4,20},{20... | collective-permute-start | bytes 147464 | tf_op jit(solution)/shard_map/ppermute | solution.py:324
  11.5 0.0 collective-permute-start.5
  11.5 0.7 %second_inner.1.refs_3_ = f32[8,16,512]{2,1,0:T(8,128)S(1)} custom-call(f32[8,16,512]{2,1,0:T(8,128)S(1)} %get-tuple-element.24.density.refs_4_, f32[8,16,512]{2,1,0:T(8,128)S(1)} %get-tuple-element.32.section.refs_5_, bf16[8,16,512]{2,1,0:T(8,128)(2,1)S(1)} %get-tuple-element.25.courant_r.refs_5_.refs_6_, ...), custom_call_target="tpu_custom_call" | custom-call | flops 2621440 | bytes 1048576 | tf_op jit(solution)/shard_map/second_inner/pallas_call | solution.py:372
  12.2 1.4 %collective-permute-done.3.refs_0_ = bf16[3,16,512]{2,1,0:T(8,128)(2,1)S(1)} collective-permute-done((bf16[3,16,512]{2,1,0:T(8,128)(2,1)S(1)}, bf16[3,16,512]{2,1,0:T(8,128)(2,1)S(1)}, u32[]{:S(2)}, u32[]{:S(2)}) %collective-permute-start.3) | collective-permute-done | bytes 49184 | tf_op jit(solution)/shard_map/ppermute | solution.py:327
  13.6 1.0 %collective-permute-done.4.refs_1_ = bf16[3,16,512]{2,1,0:T(8,128)(2,1)S(1)} collective-permute-done((bf16[3,16,512]{2,1,0:T(8,128)(2,1)S(1)}, bf16[3,16,512]{2,1,0:T(8,128)(2,1)S(1)}, u32[]{:S(2)}, u32[]{:S(2)}) %collective-permute-start.4) | collective-permute-done | bytes 49184 | tf_op jit(solution)/shard_map/ppermute | solution.py:324
  14.6 0.0 collective-permute-done.5.refs_2_
  14.6 0.6 %second_stage.1 = (f32[8,16,512]{2,1,0:T(8,128)S(1)}, bf16[16,72,128]{2,1,0:T(8,128)(2,1)S(1)}) custom-call(bf16[3,16,512]{2,1,0:T(8,128)(2,1)S(1)} %collective-permute-done.3.refs_0_, bf16[3,16,512]{2,1,0:T(8,128)(2,1)S(1)} %collective-permute-done.4.refs_1_, bf16[3,16,512]{2,1,0:T(8,128)(2,1)S(1)} %collective-permute-done.5.refs_2_, ...), custom_call_target="tpu_custom_call" | custom-call | tf_op jit(solution)/shard_map/second_stage/pallas_call | solution.py:382
  15.2 15.0 %all_to_all.5.arrived = bf16[16,72,128]{2,1,0:T(8,128)(2,1)S(1)} all-to-all(bf16[16,72,128]{2,1,0:T(8,128)(2,1)S(1)} %get-tuple-element.35), channel_id=1, replica_groups=mesh['az'=2,'ax'=16] {'ax'}, dimensions={0} | all-to-all | bytes 589824 | tf_op jit(solution)/shard_map/all_to_all | solution.py:400
  30.2 0.0 copy-done
  30.2 0.0 copy-done.1
  30.2 2.5 %prolong_patches.1 = (f32[8,16,512]{2,1,0:T(8,128)}, f32[24,128,256]{2,1,0:T(8,128)}) custom-call(s32[1,24]{1,0:T(1,128)S(1)} %get-tuple-element.20.slots_held, f32[8,16,512]{2,1,0:T(8,128)S(1)} %get-tuple-element.34.evolved, bf16[16,72,128]{2,1,0:T(8,128)(2,1)S(1)} %all_to_all.5.arrived, bf16[128,256]{1,0:T(8,128)(2,1)S(1)} %copy-done, ...), custom_call_target="tpu_custom_call" | custom-call | tf_op jit(solution)/shard_map/prolong_patches/pallas_call | solution.py:406
Async XLA Ops:
  0.6 29.6 %copy-start = (bf16[128,256]{1,0:T(8,128)(2,1)S(1)}, bf16[128,256]{1,0:T(8,128)(2,1)}, u32[]{:S(2)}) copy-start(bf16[128,256]{1,0:T(8,128)(2,1)} %constant.5.clone.radial_matrix) | copy-start | bytes 196612
  0.6 29.6 %copy-start.1 = (bf16[128,64]{1,0:T(8,128)(2,1)S(1)}, bf16[128,64]{1,0:T(8,128)(2,1)}, u32[]{:S(2)}) copy-start(bf16[128,64]{1,0:T(8,128)(2,1)} %constant.4.clone.tile_matrix) | copy-start | bytes 49156
  1.9 5.1 %collective-permute-start = (bf16[3,16,512]{2,1,0:T(8,128)(2,1)S(1)}, bf16[3,16,512]{2,1,0:T(8,128)(2,1)S(1)}, u32[]{:S(2)}, u32[]{:S(2)}) collective-permute-start(bf16[3,16,512]{2,1,0:T(8,128)(2,1)S(1)} %get-tuple-element.21), channel_id=1, source_target_pairs={{1,2},{2,1},{3,4},{4,3},{5,6},{6,5},{7,8},{8,7},{9,10},{10,9},{11,... | collective-permute-start | bytes 147464 | tf_op jit(solution)/shard_map/ppermute | solution.py:327
  5.0 4.1 %collective-permute-start.1 = (bf16[3,16,512]{2,1,0:T(8,128)(2,1)S(1)}, bf16[3,16,512]{2,1,0:T(8,128)(2,1)S(1)}, u32[]{:S(2)}, u32[]{:S(2)}) collective-permute-start(bf16[3,16,512]{2,1,0:T(8,128)(2,1)S(1)} %get-tuple-element.22), channel_id=1, source_target_pairs={{0,16},{16,0},{1,17},{17,1},{2,18},{18,2},{3,19},{19,3},{4,20},{20... | collective-permute-start | bytes 147464 | tf_op jit(solution)/shard_map/ppermute | solution.py:324
  5.0 4.0 %collective-permute-start.2 = (bf16[3,16,512]{2,1,0:T(8,128)(2,1)S(1)}, bf16[3,16,512]{2,1,0:T(8,128)(2,1)S(1)}, u32[]{:S(2)}, u32[]{:S(2)}) collective-permute-start(bf16[3,16,512]{2,1,0:T(8,128)(2,1)S(1)} %get-tuple-element.23), channel_id=1, source_target_pairs={{0,1},{1,0},{2,3},{3,2},{4,5},{5,4},{6,7},{7,6},{8,9},{9,8},{10,11... | collective-permute-start | bytes 147464 | tf_op jit(solution)/shard_map/ppermute | solution.py:327
  9.5 4.1 %collective-permute-start.3 = (bf16[3,16,512]{2,1,0:T(8,128)(2,1)S(1)}, bf16[3,16,512]{2,1,0:T(8,128)(2,1)S(1)}, u32[]{:S(2)}, u32[]{:S(2)}) collective-permute-start(bf16[3,16,512]{2,1,0:T(8,128)(2,1)S(1)} %get-tuple-element.29), channel_id=1, source_target_pairs={{1,2},{2,1},{3,4},{4,3},{5,6},{6,5},{7,8},{8,7},{9,10},{10,9},{11,... | collective-permute-start | bytes 147464 | tf_op jit(solution)/shard_map/ppermute | solution.py:327
  10.5 4.1 %collective-permute-start.4 = (bf16[3,16,512]{2,1,0:T(8,128)(2,1)S(1)}, bf16[3,16,512]{2,1,0:T(8,128)(2,1)S(1)}, u32[]{:S(2)}, u32[]{:S(2)}) collective-permute-start(bf16[3,16,512]{2,1,0:T(8,128)(2,1)S(1)} %get-tuple-element.30), channel_id=1, source_target_pairs={{0,16},{16,0},{1,17},{17,1},{2,18},{18,2},{3,19},{19,3},{4,20},{20... | collective-permute-start | bytes 147464 | tf_op jit(solution)/shard_map/ppermute | solution.py:324
  11.5 3.1 %collective-permute-start.5 = (bf16[3,16,512]{2,1,0:T(8,128)(2,1)S(1)}, bf16[3,16,512]{2,1,0:T(8,128)(2,1)S(1)}, u32[]{:S(2)}, u32[]{:S(2)}) collective-permute-start(bf16[3,16,512]{2,1,0:T(8,128)(2,1)S(1)} %get-tuple-element.31), channel_id=1, source_target_pairs={{0,1},{1,0},{2,3},{3,2},{4,5},{5,4},{6,7},{7,6},{8,9},{9,8},{10,11... | collective-permute-start | bytes 147464 | tf_op jit(solution)/shard_map/ppermute | solution.py:327

commit v4 on v3

--- a/solution.py
+++ b/solution.py
@@ -211,12 +211,10 @@
 
 
 def second_stage(count, *refs):
-    odd, sector, refs = refs[0], refs[1 : 1 + count], refs[1:]
-    even, partial, wanted_held, section, courant_r, courant_t, courant_z = refs[count : count + 7]
-    left_faces, even_faces, odd_faces = refs[count + 7 : count + 10]
-    evolved, outgoing, table, means, wanted, sem = refs[count + 10 :]
-    copy = pltpu.make_async_copy(wanted_held, wanted, sem)
-    copy.start()
+    wanted, odd, sector, refs = refs[0], refs[1], refs[2 : 2 + count], refs[2:]
+    even, partial, section, courant_r, courant_t, courant_z = refs[count : count + 6]
+    left_faces, even_faces, odd_faces = refs[count + 6 : count + 9]
+    evolved, outgoing, table, means = refs[count + 9 :]
     left, right, across = sector if count == 3 else sector * 3
     steps = outer_rates(
         section,
@@ -244,7 +242,6 @@
     means[total] = jnp.zeros((BT, BR), F32)
     table[total] = jnp.zeros((BLOCK_ROWS, BR), BF16)
     row = lax.broadcasted_iota(jnp.int32, (8, BR), 0)
-    copy.wait()
     for owner in range(outgoing.shape[0]):
         mean_rows = jnp.zeros((8, BR), F32)
         for slot in range(CAP):
@@ -254,31 +251,41 @@
         outgoing[owner, MEAN_ROW:, :] = mean_rows.astype(BF16)
 
 
-def prolong_patches(
-    slots_held, evolved, arrived, radial_matrix, tile_matrix, evolved_out, patches, spread, fine, slots, sems
-):
-    codes = pltpu.make_async_copy(slots_held, slots, sems.at[0])
-    codes.start()
-    copies = [pltpu.make_async_copy(evolved, evolved_out, sems.at[1])]
+def prolong_patches(slots, evolved, arrived, radial_matrix, tile_matrix, evolved_out, patches, fine, sems):
+    copies = [pltpu.make_async_copy(evolved, evolved_out, sems.at[0])]
     copies[0].start()
-    for source in range(arrived.shape[0]):
-        spread[source] = jnp.dot(arrived[source], radial_matrix[...], preferred_element_type=F32)
-    codes.wait()
     owned = fine.shape[0]
-    for first in range(0, owned, GROUP):
-        size = min(GROUP, owned - first)
-        for p in range(first, first + size):
-            code = slots[0, p]
-            source, slot = lax.shift_right_logical(code, 1), lax.bitwise_and(code, 1)
+
+    def radial(group):
+        blocks, chosen = [], []
+        for p in group:
+            source = lax.shift_right_logical(slots[0, p], 1)
+            slot = lax.bitwise_and(slots[0, p], 1)
             row = pl.multiple_of(slot * BLOCK_ROWS, BLOCK_ROWS)
-            coarse = spread[source, pl.ds(row, BLOCK_ROWS), :] + spread[source, pl.ds(MEAN_ROW + slot, 1), :]
+            blocks += [arrived[source, pl.ds(row, BLOCK_ROWS), :], arrived[source, MEAN_ROW:, :]]
+            chosen.append(slot)
+        spread = jnp.dot(jnp.concatenate(blocks, axis=0), radial_matrix[...], preferred_element_type=F32)
+        pairs = []
+        for i, slot in enumerate(chosen):
+            first = i * (BLOCK_ROWS + 8)
+            after = first + BLOCK_ROWS
+            mean = jnp.where(slot == 0, spread[after : after + 1], spread[after + 1 : after + 2])
+            coarse = spread[first:after] + mean
             high = coarse.astype(BF16)
             low = (coarse - high.astype(F32)).astype(BF16)
-            fine[p] = jnp.dot(
-                tile_matrix[...], jnp.concatenate([high, low], axis=0), preferred_element_type=F32
-            )
-        part = pl.ds(first, size)
-        copies.append(pltpu.make_async_copy(fine.at[part], patches.at[part], sems.at[len(copies) + 1]))
+            pairs.append(jnp.concatenate([high, low], axis=0))
+        return pairs
+
+    groups = [range(p, min(p + GROUP, owned)) for p in range(0, owned, GROUP)]
+    following = radial(groups[0])
+    for g, group in enumerate(groups):
+        pairs = following
+        if g + 1 < len(groups):
+            following = radial(groups[g + 1])
+        for p, pair in zip(group, pairs):
+            fine[p] = jnp.dot(tile_matrix[...], pair, preferred_element_type=F32)
+        part = pl.ds(group[0], len(group))
+        copies.append(pltpu.make_async_copy(fine.at[part], patches.at[part], sems.at[g + 1]))
         copies[-1].start()
     for copy in copies:
         copy.wait()
@@ -298,6 +305,10 @@
     return [pl.BlockSpec(memory_space=pltpu.VMEM)] * count
 
 
+def in_smem(count):
+    return [pl.BlockSpec(memory_space=pltpu.SMEM)] * count
+
+
 PARAMS = pltpu.CompilerParams(vmem_limit_bytes=VMEM_LIMIT)
 
 
@@ -337,10 +348,13 @@
     given = tuple(pltpu.with_memory_space_constraint(x, pltpu.HBM) for x in given)
     *held, sector, even, odd = pl.pallas_call(
         functools.partial(first_messages, len(given)),
-        out_shape=tuple(jax.ShapeDtypeStruct(x.shape, x.dtype) for x in given)
+        out_shape=tuple(
+            pltpu.SMEM(x.shape, x.dtype) if x.dtype == jnp.int32 else jax.ShapeDtypeStruct(x.shape, x.dtype)
+            for x in given
+        )
         + (sector_shape, slab_three, slab_three),
         in_specs=[pl.BlockSpec(memory_space=pltpu.HBM)] * len(given),
-        out_specs=tuple(in_vmem(len(given) + 3)),
+        out_specs=tuple(in_vmem(len(given) - 2) + in_smem(2) + in_vmem(3)),
         scratch_shapes=[pltpu.SemaphoreType.DMA((len(given),))],
         compiler_params=PARAMS,
         name="first_messages",
@@ -382,18 +396,16 @@
     evolved, outgoing = pl.pallas_call(
         functools.partial(second_stage, count),
         out_shape=(field, jax.ShapeDtypeStruct((ax_count, CHUNK_ROWS, BR), BF16)),
-        in_specs=in_vmem(11 + count),
+        in_specs=in_smem(1) + in_vmem(10 + count),
         out_specs=tuple(in_vmem(2)),
         scratch_shapes=[
             pltpu.VMEM((blocks + 1, BLOCK_ROWS, BR), BF16),
             pltpu.VMEM((blocks + 1, BT, BR), F32),
-            pltpu.SMEM(wanted.shape, jnp.int32),
-            pltpu.SemaphoreType.DMA,
         ],
         compiler_params=PARAMS,
         name="second_stage",
     )(
-        odd_two, *sectors_two, even_two, partial, wanted, section, courant_r, courant_t, courant_z,
+        wanted, odd_two, *sectors_two, even_two, partial, section, courant_r, courant_t, courant_z,
         sectors[0], even, odd,
     )
 
@@ -406,13 +418,11 @@
     evolved, patches = pl.pallas_call(
         prolong_patches,
         out_shape=(field, jax.ShapeDtypeStruct((owned, fine_rows, 2 * BR), F32)),
-        in_specs=in_vmem(5),
+        in_specs=in_smem(1) + in_vmem(4),
         out_specs=(pl.BlockSpec(memory_space=pltpu.HBM),) * 2,
         scratch_shapes=[
-            pltpu.VMEM((ax_count, CHUNK_ROWS, 2 * BR), F32),
             pltpu.VMEM((owned, fine_rows, 2 * BR), F32),
-            pltpu.SMEM(slots.shape, jnp.int32),
-            pltpu.SemaphoreType.DMA((-(-owned // GROUP) + 2,)),
+            pltpu.SemaphoreType.DMA((-(-owned // GROUP) + 1,)),
         ],
         compiler_params=PARAMS,
         name="prolong_patches",

time: 32.9 us -> 32.3 us (0.982)
  Pallas kernels: 6.16 us -> 5.53 us
    pallas_call x1, Pallas kernels: 2.49 us -> 2.09 us  [local(): pl.pallas_call(prolong_patches, out_shape=(field, jax.ShapeDtypeStruct((o...]
  transfers between devices with their start and end apart: 6 -> 6, of which waited for: 3 -> 4; matrix products, arithmetic and copies ran while one was open for 0% -> 0% of each run, Pallas kernels for 4% -> 4%
where the time goes in v4:
time: 32.3 us; the launch traced here: 32.1 us
  blocking collectives  15 us (46%)
  starting transfers between devices  6.4 us (20%)
  Pallas kernels  5.53 us (17%)
  waiting for transfers between devices  4.45 us (14%)
  between operations  0.68 us (2%)
    all_to_all x1, blocking collectives, local(): lax.all_to_all(outgoing, 'ax', split_axis=0, concat_axis=0, tiled=True)  15 us
    ppermute x2, starting transfers between devices, exchange(): lax.ppermute(odd, ('az', 'ax'), odd_pairs)  4.04 us
    ppermute x2, waiting for transfers between devices, exchange(): sectors = [lax.ppermute(sector, 'az', by(1))]  3.01 us
    pallas_call x1, Pallas kernels, local(): pl.pallas_call(prolong_patches, out_shape=(field, jax.ShapeDtypeStruct((o...  2.09 us
    ppermute x2, waiting for transfers between devices, exchange(): lax.ppermute(odd, ('az', 'ax'), odd_pairs)  1.43 us
    pallas_call x1, Pallas kernels, local(): pl.pallas_call(functools.partial(first_messages, len(given)), out_shape=t...  1.27 us
    ppermute x2, starting transfers between devices, exchange(): lax.ppermute(even, 'ax', even_pairs)  1.25 us
    ppermute x2, starting transfers between devices, exchange(): sectors = [lax.ppermute(sector, 'az', by(1))]  1.11 us
  transfers between devices with their start and end apart: 6, of which 4 were waited for; matrix products, arithmetic and copies ran while one was open for 0% of the time, Pallas kernels for 4%

profile of v4, /device:TPU:0, one launch (start us, length us, event | category | flops | bytes accessed | tf_op | source)
XLA Modules:
  0.0 32.1 jit_solution(8050536360238961944)
XLA Ops:
  0.6 0.0 copy-start
  0.6 0.0 copy-start.1
  0.7 1.3 %first_messages.1 = (f32[8,16,512]{2,1,0:T(8,128)S(1)}, bf16[8,16,512]{2,1,0:T(8,128)(2,1)S(1)}, bf16[8,16,512]{2,1,0:T(8,128)(2,1)S(1)}, bf16[8,16,512]{2,1,0:T...) custom-call(f32[8,16,512]{2,1,0:T(8,128)} %refs_0_.1, ...), custom_call_target="tpu_custom_call" | custom-call | tf_op jit(solution)/shard_map/first_messages/pallas_call | solution.py:349
  1.9 3.0 %collective-permute-start = (bf16[3,16,512]{2,1,0:T(8,128)(2,1)S(1)}, bf16[3,16,512]{2,1,0:T(8,128)(2,1)S(1)}, u32[]{:S(2)}, u32[]{:S(2)}) collective-permute-start(bf16[3,16,512]{2,1,0:T(8,128)(2,1)S(1)} %get-tuple-element.22), channel_id=1, source_target_pairs={{1,2},{2,1},{3,4},{4,3},{5,6},{6,5},{7,8},{8,7},{9,10},{10,9},{11,... | collective-permute-start | bytes 147464 | tf_op jit(solution)/shard_map/ppermute | solution.py:338
  5.0 0.1 collective-permute-start.1
  5.0 1.2 %collective-permute-start.2 = (bf16[3,16,512]{2,1,0:T(8,128)(2,1)S(1)}, bf16[3,16,512]{2,1,0:T(8,128)(2,1)S(1)}, u32[]{:S(2)}, u32[]{:S(2)}) collective-permute-start(bf16[3,16,512]{2,1,0:T(8,128)(2,1)S(1)} %get-tuple-element.24), channel_id=1, source_target_pairs={{0,1},{1,0},{2,3},{3,2},{4,5},{5,4},{6,7},{7,6},{8,9},{9,8},{10,11... | collective-permute-start | bytes 147464 | tf_op jit(solution)/shard_map/ppermute | solution.py:338
  6.3 0.7 %first_inner.1.refs_3_ = f32[8,16,512]{2,1,0:T(8,128)S(1)} custom-call(f32[8,16,512]{2,1,0:T(8,128)S(1)} %get-tuple-element.25.density.refs_4_, bf16[8,16,512]{2,1,0:T(8,128)(2,1)S(1)} %get-tuple-element.26.courant_r.refs_5_.refs_6_, bf16[8,16,512]{2,1,0:T(8,128)(2,1)S(1)} %get-tuple-element.27.courant_z.refs_7_.refs_8_, ...), custom_call_target="tpu_custom_call" | custom-call | flops 2621440 | bytes 1048576 | tf_op jit(solution)/shard_map/first_inner/pallas_call | solution.py:367
  7.0 0.1 collective-permute-done.refs_0_.refs_11_
  7.0 2.0 %collective-permute-done.1.refs_1_.refs_9_ = bf16[3,16,512]{2,1,0:T(8,128)(2,1)S(1)} collective-permute-done((bf16[3,16,512]{2,1,0:T(8,128)(2,1)S(1)}, bf16[3,16,512]{2,1,0:T(8,128)(2,1)S(1)}, u32[]{:S(2)}, u32[]{:S(2)}) %collective-permute-start.1) | collective-permute-done | bytes 49184 | tf_op jit(solution)/shard_map/ppermute | solution.py:335
  9.1 0.0 collective-permute-done.2.refs_2_.refs_10_
  9.1 0.4 %first_stage.1 = (f32[8,16,512]{2,1,0:T(8,128)S(1)}, bf16[3,16,512]{2,1,0:T(8,128)(2,1)S(1)}, bf16[3,16,512]{2,1,0:T(8,128)(2,1)S(1)}, bf16[3,16,512]{2,1,0:T(8,128)(2,1)S(1)}) custom-call(bf16[3,16,512]{2,1,0:T(8,128)(2,1)S(1)} %collective-permute-done.refs_0_.refs_11_, bf16[3,16,512]{2,1,0:T(8,128)(2,1)S(1)} %collective-permute-done.1.refs_1_.refs_9_, ...), custom_call_target="tpu_custom_call" | custom-call | tf_op jit(solution)/shard_map/first_stage/pallas_call | solution.py:376
  9.5 1.0 %collective-permute-start.3 = (bf16[3,16,512]{2,1,0:T(8,128)(2,1)S(1)}, bf16[3,16,512]{2,1,0:T(8,128)(2,1)S(1)}, u32[]{:S(2)}, u32[]{:S(2)}) collective-permute-start(bf16[3,16,512]{2,1,0:T(8,128)(2,1)S(1)} %get-tuple-element.30), channel_id=1, source_target_pairs={{1,2},{2,1},{3,4},{4,3},{5,6},{6,5},{7,8},{8,7},{9,10},{10,9},{11,... | collective-permute-start | bytes 147464 | tf_op jit(solution)/shard_map/ppermute | solution.py:338
  10.5 1.0 %collective-permute-start.4 = (bf16[3,16,512]{2,1,0:T(8,128)(2,1)S(1)}, bf16[3,16,512]{2,1,0:T(8,128)(2,1)S(1)}, u32[]{:S(2)}, u32[]{:S(2)}) collective-permute-start(bf16[3,16,512]{2,1,0:T(8,128)(2,1)S(1)} %get-tuple-element.31), channel_id=1, source_target_pairs={{0,16},{16,0},{1,17},{17,1},{2,18},{18,2},{3,19},{19,3},{4,20},{20... | collective-permute-start | bytes 147464 | tf_op jit(solution)/shard_map/ppermute | solution.py:335
  11.5 0.0 collective-permute-start.5
  11.5 0.7 %second_inner.1.refs_4_ = f32[8,16,512]{2,1,0:T(8,128)S(1)} custom-call(f32[8,16,512]{2,1,0:T(8,128)S(1)} %get-tuple-element.25.density.refs_4_, f32[8,16,512]{2,1,0:T(8,128)S(1)} %get-tuple-element.33.section.refs_5_, bf16[8,16,512]{2,1,0:T(8,128)(2,1)S(1)} %get-tuple-element.26.courant_r.refs_5_.refs_6_, ...), custom_call_target="tpu_custom_call" | custom-call | flops 2621440 | bytes 1048576 | tf_op jit(solution)/shard_map/second_inner/pallas_call | solution.py:386
  12.2 1.4 %collective-permute-done.3.refs_1_ = bf16[3,16,512]{2,1,0:T(8,128)(2,1)S(1)} collective-permute-done((bf16[3,16,512]{2,1,0:T(8,128)(2,1)S(1)}, bf16[3,16,512]{2,1,0:T(8,128)(2,1)S(1)}, u32[]{:S(2)}, u32[]{:S(2)}) %collective-permute-start.3) | collective-permute-done | bytes 49184 | tf_op jit(solution)/shard_map/ppermute | solution.py:338
  13.6 1.0 %collective-permute-done.4.refs_2_ = bf16[3,16,512]{2,1,0:T(8,128)(2,1)S(1)} collective-permute-done((bf16[3,16,512]{2,1,0:T(8,128)(2,1)S(1)}, bf16[3,16,512]{2,1,0:T(8,128)(2,1)S(1)}, u32[]{:S(2)}, u32[]{:S(2)}) %collective-permute-start.4) | collective-permute-done | bytes 49184 | tf_op jit(solution)/shard_map/ppermute | solution.py:335
  14.6 0.0 collective-permute-done.5.refs_3_
  14.6 0.4 %second_stage.1 = (f32[8,16,512]{2,1,0:T(8,128)S(1)}, bf16[16,72,128]{2,1,0:T(8,128)(2,1)S(1)}) custom-call(s32[1,2,16]{2,1,0:T(2,128)S(4)} %get-tuple-element.21.refs_0_, bf16[3,16,512]{2,1,0:T(8,128)(2,1)S(1)} %collective-permute-done.3.refs_1_, bf16[3,16,512]{2,1,0:T(8,128)(2,1)S(1)} %collective-permute-done.4.refs_2_, ...), custom_call_target="tpu_custom_call" | custom-call | tf_op jit(solution)/shard_map/second_stage/pallas_call | solution.py:396
  15.0 15.0 %all_to_all.5.arrived = bf16[16,72,128]{2,1,0:T(8,128)(2,1)S(1)} all-to-all(bf16[16,72,128]{2,1,0:T(8,128)(2,1)S(1)} %get-tuple-element.35), channel_id=1, replica_groups=mesh['az'=2,'ax'=16] {'ax'}, dimensions={0} | all-to-all | bytes 589824 | tf_op jit(solution)/shard_map/all_to_all | solution.py:412
  30.0 0.0 copy-done
  30.0 0.0 copy-done.1
  30.0 2.1 %prolong_patches.1 = (f32[8,16,512]{2,1,0:T(8,128)}, f32[24,128,256]{2,1,0:T(8,128)}) custom-call(s32[1,24]{1,0:T(1,128)S(4)} %get-tuple-element.20.slots, f32[8,16,512]{2,1,0:T(8,128)S(1)} %get-tuple-element.34.evolved, bf16[16,72,128]{2,1,0:T(8,128)(2,1)S(1)} %all_to_all.5.arrived, bf16[128,256]{1,0:T(8,128)(2,1)S(1)} %copy-done, bf16[128,64]{1,0:T(8,128)(2,1)S(1)} %copy-done.1), custom_call_target="tpu_custom_call" | custom-call | tf_op jit(solution)/shard_map/prolong_patches/pallas_call | solution.py:418
Async XLA Ops:
  0.6 29.4 %copy-start = (bf16[128,256]{1,0:T(8,128)(2,1)S(1)}, bf16[128,256]{1,0:T(8,128)(2,1)}, u32[]{:S(2)}) copy-start(bf16[128,256]{1,0:T(8,128)(2,1)} %constant.5.clone.radial_matrix) | copy-start | bytes 196612
  0.6 29.3 %copy-start.1 = (bf16[128,64]{1,0:T(8,128)(2,1)S(1)}, bf16[128,64]{1,0:T(8,128)(2,1)}, u32[]{:S(2)}) copy-start(bf16[128,64]{1,0:T(8,128)(2,1)} %constant.4.clone.tile_matrix) | copy-start | bytes 49156
  1.9 5.1 %collective-permute-start = (bf16[3,16,512]{2,1,0:T(8,128)(2,1)S(1)}, bf16[3,16,512]{2,1,0:T(8,128)(2,1)S(1)}, u32[]{:S(2)}, u32[]{:S(2)}) collective-permute-start(bf16[3,16,512]{2,1,0:T(8,128)(2,1)S(1)} %get-tuple-element.22), channel_id=1, source_target_pairs={{1,2},{2,1},{3,4},{4,3},{5,6},{6,5},{7,8},{8,7},{9,10},{10,9},{11,... | collective-permute-start | bytes 147464 | tf_op jit(solution)/shard_map/ppermute | solution.py:338
  5.0 4.1 %collective-permute-start.1 = (bf16[3,16,512]{2,1,0:T(8,128)(2,1)S(1)}, bf16[3,16,512]{2,1,0:T(8,128)(2,1)S(1)}, u32[]{:S(2)}, u32[]{:S(2)}) collective-permute-start(bf16[3,16,512]{2,1,0:T(8,128)(2,1)S(1)} %get-tuple-element.23), channel_id=1, source_target_pairs={{0,16},{16,0},{1,17},{17,1},{2,18},{18,2},{3,19},{19,3},{4,20},{20... | collective-permute-start | bytes 147464 | tf_op jit(solution)/shard_map/ppermute | solution.py:335
  5.0 4.0 %collective-permute-start.2 = (bf16[3,16,512]{2,1,0:T(8,128)(2,1)S(1)}, bf16[3,16,512]{2,1,0:T(8,128)(2,1)S(1)}, u32[]{:S(2)}, u32[]{:S(2)}) collective-permute-start(bf16[3,16,512]{2,1,0:T(8,128)(2,1)S(1)} %get-tuple-element.24), channel_id=1, source_target_pairs={{0,1},{1,0},{2,3},{3,2},{4,5},{5,4},{6,7},{7,6},{8,9},{9,8},{10,11... | collective-permute-start | bytes 147464 | tf_op jit(solution)/shard_map/ppermute | solution.py:338
  9.5 4.1 %collective-permute-start.3 = (bf16[3,16,512]{2,1,0:T(8,128)(2,1)S(1)}, bf16[3,16,512]{2,1,0:T(8,128)(2,1)S(1)}, u32[]{:S(2)}, u32[]{:S(2)}) collective-permute-start(bf16[3,16,512]{2,1,0:T(8,128)(2,1)S(1)} %get-tuple-element.30), channel_id=1, source_target_pairs={{1,2},{2,1},{3,4},{4,3},{5,6},{6,5},{7,8},{8,7},{9,10},{10,9},{11,... | collective-permute-start | bytes 147464 | tf_op jit(solution)/shard_map/ppermute | solution.py:338
  10.5 4.1 %collective-permute-start.4 = (bf16[3,16,512]{2,1,0:T(8,128)(2,1)S(1)}, bf16[3,16,512]{2,1,0:T(8,128)(2,1)S(1)}, u32[]{:S(2)}, u32[]{:S(2)}) collective-permute-start(bf16[3,16,512]{2,1,0:T(8,128)(2,1)S(1)} %get-tuple-element.31), channel_id=1, source_target_pairs={{0,16},{16,0},{1,17},{17,1},{2,18},{18,2},{3,19},{19,3},{4,20},{20... | collective-permute-start | bytes 147464 | tf_op jit(solution)/shard_map/ppermute | solution.py:335
  11.5 3.1 %collective-permute-start.5 = (bf16[3,16,512]{2,1,0:T(8,128)(2,1)S(1)}, bf16[3,16,512]{2,1,0:T(8,128)(2,1)S(1)}, u32[]{:S(2)}, u32[]{:S(2)}) collective-permute-start(bf16[3,16,512]{2,1,0:T(8,128)(2,1)S(1)} %get-tuple-element.32), channel_id=1, source_target_pairs={{0,1},{1,0},{2,3},{3,2},{4,5},{5,4},{6,7},{7,6},{8,9},{9,8},{10,11... | collective-permute-start | bytes 147464 | tf_op jit(solution)/shard_map/ppermute | solution.py:338

commit v5 on v4

--- a/solution.py
+++ b/solution.py
@@ -20,8 +20,6 @@
 VMEM_LIMIT = 24 * 1024 * 1024
 
 BLOCK_ROWS = BZ * BT
-MEAN_ROW = CAP * BLOCK_ROWS
-CHUNK_ROWS = MEAN_ROW + 8
 
 
 def pack_sector(values, courant_t, out_ref):
@@ -79,6 +77,16 @@
     pack_sector(density, courant_t, sector_out)
     for copy in copies[3:]:
         copy.wait()
+
+
+def stretched(x):
+    square = x * x
+    return jnp.where(x < 0.0, -square * square, square * square)
+
+
+def unstretched(y):
+    root = jnp.sqrt(jnp.sqrt(jnp.abs(y)))
+    return jnp.where(y < 0.0, -root, root)
 
 
 def axial_flux(courant, back, here, up, up_two):
@@ -214,7 +222,7 @@
     wanted, odd, sector, refs = refs[0], refs[1], refs[2 : 2 + count], refs[2:]
     even, partial, section, courant_r, courant_t, courant_z = refs[count : count + 6]
     left_faces, even_faces, odd_faces = refs[count + 6 : count + 9]
-    evolved, outgoing, table, means = refs[count + 9 :]
+    evolved, outgoing, table = refs[count + 9 :]
     left, right, across = sector if count == 3 else sector * 3
     steps = outer_rates(
         section,
@@ -234,21 +242,17 @@
         r = block % blocks_r * BR
         if r >= HEAD_R * BR:
             continue
-        tiles = [evolved[z + i, t : t + BT, r : r + BR] for i in range(BZ)]
-        mean = jnp.mean(sum(tiles), axis=0, keepdims=True) * (1.0 / BZ)
-        mean = jnp.broadcast_to(mean.astype(BF16).astype(F32), (BT, BR))
-        means[block] = mean
-        table[block] = jnp.concatenate([tile - mean for tile in tiles], axis=0).astype(BF16)
-    means[total] = jnp.zeros((BT, BR), F32)
+        tiles = [stretched(evolved[z + i, t : t + BT, r : r + BR]) for i in range(BZ)]
+        table[block] = jnp.concatenate(tiles, axis=0).astype(BF16)
     table[total] = jnp.zeros((BLOCK_ROWS, BR), BF16)
-    row = lax.broadcasted_iota(jnp.int32, (8, BR), 0)
     for owner in range(outgoing.shape[0]):
-        mean_rows = jnp.zeros((8, BR), F32)
         for slot in range(CAP):
-            block = wanted[0, slot, owner]
-            outgoing[owner, slot * BLOCK_ROWS : (slot + 1) * BLOCK_ROWS, :] = table[block]
-            mean_rows = jnp.where(row == slot, means[block], mean_rows)
-        outgoing[owner, MEAN_ROW:, :] = mean_rows.astype(BF16)
+            outgoing[owner, slot * BLOCK_ROWS : (slot + 1) * BLOCK_ROWS, :] = table[wanted[0, slot, owner]]
+
+
+def halves(x):
+    high = x.astype(BF16)
+    return jnp.concatenate([high, (x - high.astype(F32)).astype(BF16)], axis=0)
 
 
 def prolong_patches(slots, evolved, arrived, radial_matrix, tile_matrix, evolved_out, patches, fine, sems):
@@ -257,24 +261,14 @@
     owned = fine.shape[0]
 
     def radial(group):
-        blocks, chosen = [], []
+        blocks = []
         for p in group:
             source = lax.shift_right_logical(slots[0, p], 1)
-            slot = lax.bitwise_and(slots[0, p], 1)
-            row = pl.multiple_of(slot * BLOCK_ROWS, BLOCK_ROWS)
-            blocks += [arrived[source, pl.ds(row, BLOCK_ROWS), :], arrived[source, MEAN_ROW:, :]]
-            chosen.append(slot)
+            row = pl.multiple_of(lax.bitwise_and(slots[0, p], 1) * BLOCK_ROWS, BLOCK_ROWS)
+            blocks.append(halves(unstretched(arrived[source, pl.ds(row, BLOCK_ROWS), :].astype(F32))))
         spread = jnp.dot(jnp.concatenate(blocks, axis=0), radial_matrix[...], preferred_element_type=F32)
-        pairs = []
-        for i, slot in enumerate(chosen):
-            first = i * (BLOCK_ROWS + 8)
-            after = first + BLOCK_ROWS
-            mean = jnp.where(slot == 0, spread[after : after + 1], spread[after + 1 : after + 2])
-            coarse = spread[first:after] + mean
-            high = coarse.astype(BF16)
-            low = (coarse - high.astype(F32)).astype(BF16)
-            pairs.append(jnp.concatenate([high, low], axis=0))
-        return pairs
+        firsts = [2 * BLOCK_ROWS * i for i in range(len(blocks))]
+        return [halves(spread[f : f + BLOCK_ROWS] + spread[f + BLOCK_ROWS : f + 2 * BLOCK_ROWS]) for f in firsts]
 
     groups = [range(p, min(p + GROUP, owned)) for p in range(0, owned, GROUP)]
     following = radial(groups[0])
@@ -395,12 +389,11 @@
     blocks = rows_z // BZ * (cells_t // BT) * (cells_r // BR)
     evolved, outgoing = pl.pallas_call(
         functools.partial(second_stage, count),
-        out_shape=(field, jax.ShapeDtypeStruct((ax_count, CHUNK_ROWS, BR), BF16)),
+        out_shape=(field, jax.ShapeDtypeStruct((ax_count, CAP * BLOCK_ROWS, BR), BF16)),
         in_specs=in_smem(1) + in_vmem(10 + count),
         out_specs=tuple(in_vmem(2)),
         scratch_shapes=[
             pltpu.VMEM((blocks + 1, BLOCK_ROWS, BR), BF16),
-            pltpu.VMEM((blocks + 1, BT, BR), F32),
         ],
         compiler_params=PARAMS,
         name="second_stage",

time: 32.3 us -> 31.7 us (0.981)
  blocking collectives: 15 us -> 14.5 us
    all_to_all x1, blocking collectives: 15 us -> 14.5 us  [local(): lax.all_to_all(outgoing, 'ax', split_axis=0, concat_axis=0, tiled=True)]
where the time goes in v5:
time: 31.7 us; the launch traced here: 31.5 us
  blocking collectives  14.5 us (46%)
  starting transfers between devices  6.4 us (20%)
  Pallas kernels  5.53 us (17%)
  waiting for transfers between devices  4.45 us (14%)
  between operations  0.68 us (2%)
    all_to_all x1, blocking collectives, local(): lax.all_to_all(outgoing, 'ax', split_axis=0, concat_axis=0, tiled=True)  14.5 us
    ppermute x2, starting transfers between devices, exchange(): lax.ppermute(odd, ('az', 'ax'), odd_pairs)  4.04 us
    ppermute x2, waiting for transfers between devices, exchange(): sectors = [lax.ppermute(sector, 'az', by(1))]  3.01 us
    pallas_call x1, Pallas kernels, local(): pl.pallas_call(prolong_patches, out_shape=(field, jax.ShapeDtypeStruct((o...  2.1 us
    ppermute x2, waiting for transfers between devices, exchange(): lax.ppermute(odd, ('az', 'ax'), odd_pairs)  1.43 us
    pallas_call x1, Pallas kernels, local(): pl.pallas_call(functools.partial(first_messages, len(given)), out_shape=t...  1.27 us
    ppermute x2, starting transfers between devices, exchange(): lax.ppermute(even, 'ax', even_pairs)  1.25 us
    ppermute x2, starting transfers between devices, exchange(): sectors = [lax.ppermute(sector, 'az', by(1))]  1.11 us
  transfers between devices with their start and end apart: 6, of which 4 were waited for; matrix products, arithmetic and copies ran while one was open for 0% of the time, Pallas kernels for 4%

profile of v5, /device:TPU:0, one launch (start us, length us, event | category | flops | bytes accessed | tf_op | source)
XLA Modules:
  0.0 31.5 jit_solution(9873090569246931676)
XLA Ops:
  0.6 0.0 copy-start
  0.6 0.0 copy-start.1
  0.7 1.3 %first_messages.1 = (f32[8,16,512]{2,1,0:T(8,128)S(1)}, bf16[8,16,512]{2,1,0:T(8,128)(2,1)S(1)}, bf16[8,16,512]{2,1,0:T(8,128)(2,1)S(1)}, bf16[8,16,512]{2,1,0:T...) custom-call(f32[8,16,512]{2,1,0:T(8,128)} %refs_0_.1, ...), custom_call_target="tpu_custom_call" | custom-call | tf_op jit(solution)/shard_map/first_messages/pallas_call | solution.py:343
  1.9 3.0 %collective-permute-start = (bf16[3,16,512]{2,1,0:T(8,128)(2,1)S(1)}, bf16[3,16,512]{2,1,0:T(8,128)(2,1)S(1)}, u32[]{:S(2)}, u32[]{:S(2)}) collective-permute-start(bf16[3,16,512]{2,1,0:T(8,128)(2,1)S(1)} %get-tuple-element.22), channel_id=1, source_target_pairs={{1,2},{2,1},{3,4},{4,3},{5,6},{6,5},{7,8},{8,7},{9,10},{10,9},{11,... | collective-permute-start | bytes 147464 | tf_op jit(solution)/shard_map/ppermute | solution.py:332
  5.0 0.1 collective-permute-start.1
  5.0 1.2 %collective-permute-start.2 = (bf16[3,16,512]{2,1,0:T(8,128)(2,1)S(1)}, bf16[3,16,512]{2,1,0:T(8,128)(2,1)S(1)}, u32[]{:S(2)}, u32[]{:S(2)}) collective-permute-start(bf16[3,16,512]{2,1,0:T(8,128)(2,1)S(1)} %get-tuple-element.24), channel_id=1, source_target_pairs={{0,1},{1,0},{2,3},{3,2},{4,5},{5,4},{6,7},{7,6},{8,9},{9,8},{10,11... | collective-permute-start | bytes 147464 | tf_op jit(solution)/shard_map/ppermute | solution.py:332
  6.3 0.7 %first_inner.1.refs_3_ = f32[8,16,512]{2,1,0:T(8,128)S(1)} custom-call(f32[8,16,512]{2,1,0:T(8,128)S(1)} %get-tuple-element.25.density.refs_4_, bf16[8,16,512]{2,1,0:T(8,128)(2,1)S(1)} %get-tuple-element.26.courant_r.refs_5_.refs_6_, bf16[8,16,512]{2,1,0:T(8,128)(2,1)S(1)} %get-tuple-element.27.courant_z.refs_7_.refs_8_, ...), custom_call_target="tpu_custom_call" | custom-call | flops 2621440 | bytes 1048576 | tf_op jit(solution)/shard_map/first_inner/pallas_call | solution.py:361
  7.0 0.1 collective-permute-done.refs_0_.refs_11_
  7.0 2.0 %collective-permute-done.1.refs_1_.refs_9_ = bf16[3,16,512]{2,1,0:T(8,128)(2,1)S(1)} collective-permute-done((bf16[3,16,512]{2,1,0:T(8,128)(2,1)S(1)}, bf16[3,16,512]{2,1,0:T(8,128)(2,1)S(1)}, u32[]{:S(2)}, u32[]{:S(2)}) %collective-permute-start.1) | collective-permute-done | bytes 49184 | tf_op jit(solution)/shard_map/ppermute | solution.py:329
  9.1 0.0 collective-permute-done.2.refs_2_.refs_10_
  9.1 0.4 %first_stage.1 = (f32[8,16,512]{2,1,0:T(8,128)S(1)}, bf16[3,16,512]{2,1,0:T(8,128)(2,1)S(1)}, bf16[3,16,512]{2,1,0:T(8,128)(2,1)S(1)}, bf16[3,16,512]{2,1,0:T(8,128)(2,1)S(1)}) custom-call(bf16[3,16,512]{2,1,0:T(8,128)(2,1)S(1)} %collective-permute-done.refs_0_.refs_11_, bf16[3,16,512]{2,1,0:T(8,128)(2,1)S(1)} %collective-permute-done.1.refs_1_.refs_9_, ...), custom_call_target="tpu_custom_call" | custom-call | tf_op jit(solution)/shard_map/first_stage/pallas_call | solution.py:370
  9.5 1.0 %collective-permute-start.3 = (bf16[3,16,512]{2,1,0:T(8,128)(2,1)S(1)}, bf16[3,16,512]{2,1,0:T(8,128)(2,1)S(1)}, u32[]{:S(2)}, u32[]{:S(2)}) collective-permute-start(bf16[3,16,512]{2,1,0:T(8,128)(2,1)S(1)} %get-tuple-element.30), channel_id=1, source_target_pairs={{1,2},{2,1},{3,4},{4,3},{5,6},{6,5},{7,8},{8,7},{9,10},{10,9},{11,... | collective-permute-start | bytes 147464 | tf_op jit(solution)/shard_map/ppermute | solution.py:332
  10.5 1.0 %collective-permute-start.4 = (bf16[3,16,512]{2,1,0:T(8,128)(2,1)S(1)}, bf16[3,16,512]{2,1,0:T(8,128)(2,1)S(1)}, u32[]{:S(2)}, u32[]{:S(2)}) collective-permute-start(bf16[3,16,512]{2,1,0:T(8,128)(2,1)S(1)} %get-tuple-element.31), channel_id=1, source_target_pairs={{0,16},{16,0},{1,17},{17,1},{2,18},{18,2},{3,19},{19,3},{4,20},{20... | collective-permute-start | bytes 147464 | tf_op jit(solution)/shard_map/ppermute | solution.py:329
  11.5 0.0 collective-permute-start.5
  11.5 0.7 %second_inner.1.refs_4_ = f32[8,16,512]{2,1,0:T(8,128)S(1)} custom-call(f32[8,16,512]{2,1,0:T(8,128)S(1)} %get-tuple-element.25.density.refs_4_, f32[8,16,512]{2,1,0:T(8,128)S(1)} %get-tuple-element.33.section.refs_5_, bf16[8,16,512]{2,1,0:T(8,128)(2,1)S(1)} %get-tuple-element.26.courant_r.refs_5_.refs_6_, ...), custom_call_target="tpu_custom_call" | custom-call | flops 2621440 | bytes 1048576 | tf_op jit(solution)/shard_map/second_inner/pallas_call | solution.py:380
  12.2 1.4 %collective-permute-done.3.refs_1_ = bf16[3,16,512]{2,1,0:T(8,128)(2,1)S(1)} collective-permute-done((bf16[3,16,512]{2,1,0:T(8,128)(2,1)S(1)}, bf16[3,16,512]{2,1,0:T(8,128)(2,1)S(1)}, u32[]{:S(2)}, u32[]{:S(2)}) %collective-permute-start.3) | collective-permute-done | bytes 49184 | tf_op jit(solution)/shard_map/ppermute | solution.py:332
  13.6 1.0 %collective-permute-done.4.refs_2_ = bf16[3,16,512]{2,1,0:T(8,128)(2,1)S(1)} collective-permute-done((bf16[3,16,512]{2,1,0:T(8,128)(2,1)S(1)}, bf16[3,16,512]{2,1,0:T(8,128)(2,1)S(1)}, u32[]{:S(2)}, u32[]{:S(2)}) %collective-permute-start.4) | collective-permute-done | bytes 49184 | tf_op jit(solution)/shard_map/ppermute | solution.py:329
  14.6 0.0 collective-permute-done.5.refs_3_
  14.6 0.4 %second_stage.1 = (f32[8,16,512]{2,1,0:T(8,128)S(1)}, bf16[16,64,128]{2,1,0:T(8,128)(2,1)S(1)}) custom-call(s32[1,2,16]{2,1,0:T(2,128)S(4)} %get-tuple-element.21.refs_0_, bf16[3,16,512]{2,1,0:T(8,128)(2,1)S(1)} %collective-permute-done.3.refs_1_, bf16[3,16,512]{2,1,0:T(8,128)(2,1)S(1)} %collective-permute-done.4.refs_2_, ...), custom_call_target="tpu_custom_call" | custom-call | tf_op jit(solution)/shard_map/second_stage/pallas_call | solution.py:390
  15.0 14.5 %all_to_all.5.arrived = bf16[16,64,128]{2,1,0:T(8,128)(2,1)S(1)} all-to-all(bf16[16,64,128]{2,1,0:T(8,128)(2,1)S(1)} %get-tuple-element.35), channel_id=1, replica_groups=mesh['az'=2,'ax'=16] {'ax'}, dimensions={0} | all-to-all | bytes 524288 | tf_op jit(solution)/shard_map/all_to_all | solution.py:405
  29.4 0.0 copy-done
  29.4 0.0 copy-done.1
  29.4 2.1 %prolong_patches.1 = (f32[8,16,512]{2,1,0:T(8,128)}, f32[24,128,256]{2,1,0:T(8,128)}) custom-call(s32[1,24]{1,0:T(1,128)S(4)} %get-tuple-element.20.slots, f32[8,16,512]{2,1,0:T(8,128)S(1)} %get-tuple-element.34.evolved, bf16[16,64,128]{2,1,0:T(8,128)(2,1)S(1)} %all_to_all.5.arrived, bf16[128,256]{1,0:T(8,128)(2,1)S(1)} %copy-done, bf16[128,64]{1,0:T(8,128)(2,1)S(1)} %copy-done.1), custom_call_target="tpu_custom_call" | custom-call | tf_op jit(solution)/shard_map/prolong_patches/pallas_call | solution.py:411
Async XLA Ops:
  0.6 28.8 %copy-start = (bf16[128,256]{1,0:T(8,128)(2,1)S(1)}, bf16[128,256]{1,0:T(8,128)(2,1)}, u32[]{:S(2)}) copy-start(bf16[128,256]{1,0:T(8,128)(2,1)} %constant.5.clone.radial_matrix) | copy-start | bytes 196612
  0.6 28.8 %copy-start.1 = (bf16[128,64]{1,0:T(8,128)(2,1)S(1)}, bf16[128,64]{1,0:T(8,128)(2,1)}, u32[]{:S(2)}) copy-start(bf16[128,64]{1,0:T(8,128)(2,1)} %constant.4.clone.tile_matrix) | copy-start | bytes 49156
  1.9 5.1 %collective-permute-start = (bf16[3,16,512]{2,1,0:T(8,128)(2,1)S(1)}, bf16[3,16,512]{2,1,0:T(8,128)(2,1)S(1)}, u32[]{:S(2)}, u32[]{:S(2)}) collective-permute-start(bf16[3,16,512]{2,1,0:T(8,128)(2,1)S(1)} %get-tuple-element.22), channel_id=1, source_target_pairs={{1,2},{2,1},{3,4},{4,3},{5,6},{6,5},{7,8},{8,7},{9,10},{10,9},{11,... | collective-permute-start | bytes 147464 | tf_op jit(solution)/shard_map/ppermute | solution.py:332
  5.0 4.1 %collective-permute-start.1 = (bf16[3,16,512]{2,1,0:T(8,128)(2,1)S(1)}, bf16[3,16,512]{2,1,0:T(8,128)(2,1)S(1)}, u32[]{:S(2)}, u32[]{:S(2)}) collective-permute-start(bf16[3,16,512]{2,1,0:T(8,128)(2,1)S(1)} %get-tuple-element.23), channel_id=1, source_target_pairs={{0,16},{16,0},{1,17},{17,1},{2,18},{18,2},{3,19},{19,3},{4,20},{20... | collective-permute-start | bytes 147464 | tf_op jit(solution)/shard_map/ppermute | solution.py:329
  5.0 4.0 %collective-permute-start.2 = (bf16[3,16,512]{2,1,0:T(8,128)(2,1)S(1)}, bf16[3,16,512]{2,1,0:T(8,128)(2,1)S(1)}, u32[]{:S(2)}, u32[]{:S(2)}) collective-permute-start(bf16[3,16,512]{2,1,0:T(8,128)(2,1)S(1)} %get-tuple-element.24), channel_id=1, source_target_pairs={{0,1},{1,0},{2,3},{3,2},{4,5},{5,4},{6,7},{7,6},{8,9},{9,8},{10,11... | collective-permute-start | bytes 147464 | tf_op jit(solution)/shard_map/ppermute | solution.py:332
  9.5 4.1 %collective-permute-start.3 = (bf16[3,16,512]{2,1,0:T(8,128)(2,1)S(1)}, bf16[3,16,512]{2,1,0:T(8,128)(2,1)S(1)}, u32[]{:S(2)}, u32[]{:S(2)}) collective-permute-start(bf16[3,16,512]{2,1,0:T(8,128)(2,1)S(1)} %get-tuple-element.30), channel_id=1, source_target_pairs={{1,2},{2,1},{3,4},{4,3},{5,6},{6,5},{7,8},{8,7},{9,10},{10,9},{11,... | collective-permute-start | bytes 147464 | tf_op jit(solution)/shard_map/ppermute | solution.py:332
  10.5 4.1 %collective-permute-start.4 = (bf16[3,16,512]{2,1,0:T(8,128)(2,1)S(1)}, bf16[3,16,512]{2,1,0:T(8,128)(2,1)S(1)}, u32[]{:S(2)}, u32[]{:S(2)}) collective-permute-start(bf16[3,16,512]{2,1,0:T(8,128)(2,1)S(1)} %get-tuple-element.31), channel_id=1, source_target_pairs={{0,16},{16,0},{1,17},{17,1},{2,18},{18,2},{3,19},{19,3},{4,20},{20... | collective-permute-start | bytes 147464 | tf_op jit(solution)/shard_map/ppermute | solution.py:329
  11.5 3.1 %collective-permute-start.5 = (bf16[3,16,512]{2,1,0:T(8,128)(2,1)S(1)}, bf16[3,16,512]{2,1,0:T(8,128)(2,1)S(1)}, u32[]{:S(2)}, u32[]{:S(2)}) collective-permute-start(bf16[3,16,512]{2,1,0:T(8,128)(2,1)S(1)} %get-tuple-element.32), channel_id=1, source_target_pairs={{0,1},{1,0},{2,3},{3,2},{4,5},{5,4},{6,7},{7,6},{8,9},{9,8},{10,11... | collective-permute-start | bytes 147464 | tf_op jit(solution)/shard_map/ppermute | solution.py:332

commit v6 on v5

--- a/solution.py
+++ b/solution.py
@@ -35,33 +35,58 @@
     tiles = [
         jnp.where(outer, ends[k], pltpu.roll(ends[k + 1], 4, 0)) for k in range(0, rows_z, 2)
     ]
-    faces = jnp.zeros((8, cells_r), F32)
     if courant_t is not None:
+        faces = jnp.zeros((8, cells_r), F32)
         for k in range(rows_z):
             face = courant_t[k].astype(F32)[cells_t - 8 :, :]
             faces = jnp.where(row == k, pltpu.roll(face, (k + 1) % 8, 0), faces)
-    tiles.append(faces)
+        tiles.append(faces)
     rounded = inner.astype(BF16).astype(F32)
     rest = inner - rounded
     tiles.append(jnp.concatenate([rounded[:8], rounded[8:], rest[:8], rest[8:]], axis=1))
-    for pair in range(len(tiles) // 2):
-        out_ref[pair] = jnp.concatenate(tiles[2 * pair : 2 * pair + 2], axis=0).astype(BF16)
-
-
-def tile_of(msg, index):
-    return msg[index // 2].astype(F32)[(index % 2) * 8 : (index % 2) * 8 + 8, :]
+    write_tiles(out_ref, 0, tiles)
+
+
+def unpack_inner(msg, index):
+    parts = tile_of(msg, index, (0, 512))
+    parts = parts[:, 0:256] + parts[:, 256:512]
+    return jnp.concatenate([parts[:, 0:128], parts[:, 128:256]], axis=0)
+
+
+def write_tiles(out_ref, first, tiles):
+    if out_ref.shape[1] == 8:
+        for index, tile in enumerate(tiles):
+            out_ref[first + index] = tile.astype(BF16)
+    else:
+        for index in range(0, len(tiles), 2):
+            out_ref[(first + index) // 2] = jnp.concatenate(tiles[index : index + 2], axis=0).astype(BF16)
+
+
+def tile_of(msg, index, lanes):
+    if msg.shape[1] == 8:
+        return msg[index, :, lanes[0] : lanes[1]].astype(F32)
+    return msg[index // 2, :, lanes[0] : lanes[1]].astype(F32)[(index % 2) * 8 : (index % 2) * 8 + 8, :]
+
+
+def row_of(msg, r, rows, lanes):
+    if msg.shape[1] == 8:
+        parts = rows // 8
+        return jnp.concatenate([tile_of(msg, parts * r + part, lanes) for part in range(parts)], axis=0)
+    return msg[r, :, lanes[0] : lanes[1]].astype(F32)
 
 
 def pack_slab(values, courant_z, even_ref, odd_ref):
-    rows_z = values.shape[0]
+    rows_z, cells_t, _ = values.shape
     parity = lax.rem(lax.axis_index("ax"), 2)
     first_even = jnp.where(parity == 0, rows_z - 2, 0)
     first_odd = jnp.where(parity == 0, 0, rows_z - 2)
+    parts = cells_t // 8
     for out_ref, first in ((even_ref, first_even), (odd_ref, first_odd)):
-        for r in range(2):
-            out_ref[r] = values[first + r].astype(BF16)
+        rows = [values[first + r] for r in range(2)]
         if courant_z is not None:
-            out_ref[2] = courant_z[rows_z - 1]
+            rows.append(courant_z[rows_z - 1].astype(F32))
+        for r, row in enumerate(rows):
+            write_tiles(out_ref, parts * r, [row[8 * part : 8 * part + 8, :] for part in range(parts)])
 
 
 def first_messages(count, *refs):
@@ -129,9 +154,11 @@
         yield rate + (carried - pltpu.roll(carried, 1, 1)) * inverse_radius
 
 
-def outer_rates(values, sector, slab, faces_below, courants):
-    rows_z, cells_t, cells_r = values.shape
-    left, right, across = sector
+def outer_rates(values, lanes, sector, inner, slab, faces_below, courants):
+    rows_z, cells_t = values.shape[:2]
+    low, high = lanes
+    width = high - low
+    left, right = sector
     even_msg, odd_msg = slab
     left_faces, even_faces, odd_faces = faces_below
     courant_r, courant_t, courant_z = courants
@@ -139,54 +166,59 @@
     is_even = lax.rem(me, 2) == 0
     has_below = me > 0
     has_above = me < lax.axis_size("ax") - 1
-    zero = jnp.zeros((cells_t, cells_r), F32)
-
-    def below(even, odd):
-        return jnp.where(has_below, jnp.where(is_even, odd, even).astype(F32), zero)
-
-    def above(even, odd):
-        return jnp.where(has_above, jnp.where(is_even, even, odd).astype(F32), zero)
+    zero = jnp.zeros((cells_t, width), F32)
+
+    def below(even, odd, r):
+        even, odd = row_of(even, r, cells_t, lanes), row_of(odd, r, cells_t, lanes)
+        return jnp.where(has_below, jnp.where(is_even, odd, even), zero)
+
+    def above(even, odd, r):
+        even, odd = row_of(even, r, cells_t, lanes), row_of(odd, r, cells_t, lanes)
+        return jnp.where(has_above, jnp.where(is_even, even, odd), zero)
+
+    def axial_courant(k):
+        return courant_z[k, :, low:high].astype(F32)
+
+    def at(k):
+        return values[k, :, low:high]
 
     top = rows_z - 1
-    below_one, below_two = below(even_msg[1], odd_msg[1]), below(even_msg[0], odd_msg[0])
-    above_one, above_two = above(even_msg[0], odd_msg[0]), above(even_msg[1], odd_msg[1])
-    first_flux = axial_flux(
-        below(even_faces[2], odd_faces[2]), below_two, below_one, values[0], values[1]
-    )
-    last_flux = axial_flux(
-        courant_z[top].astype(F32), values[top - 1], values[top], above_one, above_two
-    )
-    low_change = -0.25 * jnp.maximum(courant_z[0].astype(F32), 0.0) * below_one
-    high_change = -0.25 * jnp.minimum(courant_z[top - 1].astype(F32), 0.0) * above_one
+    below_one, below_two = below(even_msg, odd_msg, 1), below(even_msg, odd_msg, 0)
+    above_one, above_two = above(even_msg, odd_msg, 0), above(even_msg, odd_msg, 1)
+    below_courant = below(even_faces, odd_faces, 2)
+    first_flux = axial_flux(below_courant, below_two, below_one, at(0), at(1))
+    last_flux = axial_flux(axial_courant(top), at(top - 1), at(top), above_one, above_two)
+    low_change = -0.25 * jnp.maximum(axial_courant(0), 0.0) * below_one
+    high_change = -0.25 * jnp.minimum(axial_courant(top - 1), 0.0) * above_one
     axial = {
         0: first_flux - low_change + DIFFUSION * below_one,
         1: low_change,
         top - 1: -high_change,
         top: high_change - last_flux + DIFFUSION * above_one,
     }
-    halo_row = lax.broadcasted_iota(jnp.int32, (8, cells_r), 0)
+    halo_row = lax.broadcasted_iota(jnp.int32, (8, width), 0)
     lane = lax.broadcasted_iota(jnp.int32, (cells_t, 128), 1)
-    packed = tile_of(across, rows_z // 2 + 1)
-    packed = packed[:, 0:256] + packed[:, 256:512]
-    inner = jnp.concatenate([packed[:, 0:128], packed[:, 128:256]], axis=0)
-    faces = tile_of(left_faces, rows_z // 2)
+    faces = tile_of(left_faces, rows_z // 2, lanes)
     rows = cells_t + 8
     for k in range(rows_z):
-        here = values[k]
-        halo = tile_of(left, k // 2)
+        here = at(k)
+        halo = tile_of(left, k // 2, lanes)
         if right is not left:
             beyond = (halo_row < 2) | (halo_row == 4) | (halo_row == 5)
-            halo = jnp.where(beyond, tile_of(right, k // 2), halo)
+            halo = jnp.where(beyond, tile_of(right, k // 2, lanes), halo)
         if k % 2:
             halo = pltpu.roll(halo, 4, 0)
         ring = jnp.concatenate([halo, here], axis=0)
         face_halo = pltpu.roll(faces, 7 - k, 0)
-        courant = jnp.concatenate([face_halo, courant_t[k].astype(F32)], axis=0)
+        courant = jnp.concatenate([face_halo, courant_t[k, :, low:high].astype(F32)], axis=0)
         quarter = 0.25 * (pltpu.roll(ring, rows - 1, 0) - pltpu.roll(ring, 1, 0))
         flux = courant * jnp.where(courant > 0.0, ring + quarter, pltpu.roll(ring - quarter, rows - 1, 0))
         rate = (pltpu.roll(flux, 1, 0) - flux)[8:, :]
         if k in axial:
             rate = rate + axial[k]
+        if inner is None:
+            yield rate
+            continue
         change = 0.25 * jnp.maximum(courant_r[k, :, 0:128].astype(F32), 0.0)
         change = change * (pltpu.roll(inner, 128 - k, 1) if k else inner)
         change = jnp.where(lane == 0, change, 0.0)
@@ -209,8 +241,15 @@
     even, partial, density, courant_r, courant_t, courant_z = refs[count : count + 6]
     section, sector_out, even_out, odd_out = refs[count + 6 :]
     left, right, across = sector if count == 3 else sector * 3
+    inner = unpack_inner(across, density.shape[0] // 2 + 1)
     steps = outer_rates(
-        density, (left, right, across), (even, odd), (left, even, odd), (courant_r, courant_t, courant_z)
+        density,
+        (0, density.shape[2]),
+        (left, right),
+        inner,
+        (even, odd),
+        (left, even, odd),
+        (courant_r, courant_t, courant_z),
     )
     for k, rate in enumerate(steps):
         section[k] = partial[k] + rate
@@ -218,29 +257,31 @@
     pack_slab(section, None, even_out, odd_out)
 
 
-def second_stage(count, *refs):
+def second_head(count, *refs):
     wanted, odd, sector, refs = refs[0], refs[1], refs[2 : 2 + count], refs[2:]
     even, partial, section, courant_r, courant_t, courant_z = refs[count : count + 6]
     left_faces, even_faces, odd_faces = refs[count + 6 : count + 9]
     evolved, outgoing, table = refs[count + 9 :]
+    rows_z, cells_t, lanes = evolved.shape
     left, right, across = sector if count == 3 else sector * 3
     steps = outer_rates(
         section,
-        (left, right, across),
+        (0, lanes),
+        (left, right),
+        unpack_inner(across, rows_z // 2),
         (even, odd),
         (left_faces, even_faces, odd_faces),
         (courant_r, courant_t, courant_z),
     )
     for k, rate in enumerate(steps):
-        evolved[k] = partial[k] + 0.5 * rate
-    rows_z, cells_t, cells_r = evolved.shape
-    blocks_t, blocks_r = cells_t // BT, cells_r // BR
+        evolved[k] = partial[k, :, 0:lanes] + 0.5 * rate
+    blocks_t, blocks_r = cells_t // BT, section.shape[2] // BR
     total = rows_z // BZ * blocks_t * blocks_r
     for block in range(total):
         z = block // (blocks_t * blocks_r) * BZ
         t = block // blocks_r % blocks_t * BT
         r = block % blocks_r * BR
-        if r >= HEAD_R * BR:
+        if r >= lanes:
             continue
         tiles = [stretched(evolved[z + i, t : t + BT, r : r + BR]) for i in range(BZ)]
         table[block] = jnp.concatenate(tiles, axis=0).astype(BF16)
@@ -250,13 +291,33 @@
             outgoing[owner, slot * BLOCK_ROWS : (slot + 1) * BLOCK_ROWS, :] = table[wanted[0, slot, owner]]
 
 
+def second_tail(count, refs, evolved):
+    odd, sector, refs = refs[0], refs[1 : 1 + count], refs[1:]
+    even, partial, section, courant_t, courant_z, left_faces, even_faces, odd_faces = refs[count:]
+    left, right, _ = sector if count == 3 else sector * 3
+    low, high = section.shape[2] - evolved.shape[2], section.shape[2]
+    steps = outer_rates(
+        section,
+        (low, high),
+        (left, right),
+        None,
+        (even, odd),
+        (left_faces, even_faces, odd_faces),
+        (None, courant_t, courant_z),
+    )
+    for k, rate in enumerate(steps):
+        evolved[k] = partial[k, :, low:high] + 0.5 * rate
+
+
 def halves(x):
     high = x.astype(BF16)
     return jnp.concatenate([high, (x - high.astype(F32)).astype(BF16)], axis=0)
 
 
-def prolong_patches(slots, evolved, arrived, radial_matrix, tile_matrix, evolved_out, patches, fine, sems):
-    copies = [pltpu.make_async_copy(evolved, evolved_out, sems.at[0])]
+def prolong_patches(count, slots, head, arrived, radial_matrix, tile_matrix, *refs):
+    for_tail, (evolved, patches, tail, fine, sems) = refs[: count + 9], refs[count + 9 :]
+    lanes = head.shape[2]
+    copies = [pltpu.make_async_copy(head, evolved.at[:, :, pl.ds(0, lanes)], sems.at[0])]
     copies[0].start()
     owned = fine.shape[0]
 
@@ -281,6 +342,12 @@
         part = pl.ds(group[0], len(group))
         copies.append(pltpu.make_async_copy(fine.at[part], patches.at[part], sems.at[g + 1]))
         copies[-1].start()
+        if g == min(1, len(groups) - 1):
+            second_tail(count, for_tail, tail)
+            copies.append(
+                pltpu.make_async_copy(tail, evolved.at[:, :, pl.ds(lanes, tail.shape[2])], sems.at[len(groups) + 1])
+            )
+            copies[-1].start()
     for copy in copies:
         copy.wait()
 
@@ -324,16 +391,16 @@
     def by(steps):
         return [(a, (a + steps) % az_count) for a in range(az_count)]
 
-    def exchange(sector, even, odd):
-        if az_count == 2:
-            sectors = [lax.ppermute(sector, "az", by(1))]
-        else:
-            sectors = [lax.ppermute(sector, "az", by(s)) for s in (1, az_count - 1, az_count // 2)]
+    beside = (1,) if az_count == 2 else (1, az_count - 1)
+    all_steps = beside if az_count == 2 else beside + (az_count // 2,)
+
+    def exchange(sector, even, odd, steps):
+        sectors = [lax.ppermute(sector, "az", by(s)) for s in steps]
         return sectors, lax.ppermute(even, "ax", even_pairs), lax.ppermute(odd, ("az", "ax"), odd_pairs)
 
-    sector_shape = jax.ShapeDtypeStruct((rows_z // 4 + 1, cells_t, cells_r), BF16)
-    slab_three = jax.ShapeDtypeStruct((3, cells_t, cells_r), BF16)
-    slab_two = jax.ShapeDtypeStruct((3, cells_t, cells_r), BF16)
+    lanes = HEAD_R * BR
+    message = jax.ShapeDtypeStruct((rows_z // 4 + 1, cells_t, cells_r), BF16)
+    second_message = jax.ShapeDtypeStruct((rows_z // 2 + 1, 8, cells_r), BF16)
     field = jax.ShapeDtypeStruct(density.shape, F32)
 
     given = (
@@ -346,7 +413,7 @@
             pltpu.SMEM(x.shape, x.dtype) if x.dtype == jnp.int32 else jax.ShapeDtypeStruct(x.shape, x.dtype)
             for x in given
         )
-        + (sector_shape, slab_three, slab_three),
+        + (message,) * 3,
         in_specs=[pl.BlockSpec(memory_space=pltpu.HBM)] * len(given),
         out_specs=tuple(in_vmem(len(given) - 2) + in_smem(2) + in_vmem(3)),
         scratch_shapes=[pltpu.SemaphoreType.DMA((len(given),))],
@@ -354,7 +421,7 @@
         name="first_messages",
     )(*given)
     density, courant_t, courant_z, courant_r, ionization, wanted, slots = held
-    sectors, even, odd = exchange(sector, even, odd)
+    sectors, even, odd = exchange(sector, even, odd, all_steps)
     count = len(sectors)
 
     inner_cost = pl.CostEstimate(flops=40 * density.size, bytes_accessed=16 * density.size, transcendentals=0)
@@ -369,13 +436,13 @@
     )(density, courant_r, courant_z, ionization)
     section, sector, even_two, odd_two = pl.pallas_call(
         functools.partial(first_stage, count),
-        out_shape=(field, sector_shape, slab_two, slab_two),
+        out_shape=(field,) + (second_message,) * 3,
         in_specs=in_vmem(7 + count),
         out_specs=tuple(in_vmem(4)),
         compiler_params=PARAMS,
         name="first_stage",
     )(odd, *sectors, even, partial, density, courant_r, courant_t, courant_z)
-    sectors_two, even_two, odd_two = exchange(sector, even_two, odd_two)
+    sectors_two, even_two, odd_two = exchange(sector, even_two, odd_two, all_steps)
 
     partial = pl.pallas_call(
         second_inner,
@@ -387,16 +454,17 @@
         name="second_inner",
     )(density, section, courant_r, courant_z, ionization)
     blocks = rows_z // BZ * (cells_t // BT) * (cells_r // BR)
-    evolved, outgoing = pl.pallas_call(
-        functools.partial(second_stage, count),
-        out_shape=(field, jax.ShapeDtypeStruct((ax_count, CAP * BLOCK_ROWS, BR), BF16)),
+    head, outgoing = pl.pallas_call(
+        functools.partial(second_head, count),
+        out_shape=(
+            jax.ShapeDtypeStruct((rows_z, cells_t, lanes), F32),
+            jax.ShapeDtypeStruct((ax_count, CAP * BLOCK_ROWS, BR), BF16),
+        ),
         in_specs=in_smem(1) + in_vmem(10 + count),
         out_specs=tuple(in_vmem(2)),
-        scratch_shapes=[
-            pltpu.VMEM((blocks + 1, BLOCK_ROWS, BR), BF16),
-        ],
+        scratch_shapes=[pltpu.VMEM((blocks + 1, BLOCK_ROWS, BR), BF16)],
         compiler_params=PARAMS,
-        name="second_stage",
+        name="second_head",
     )(
         wanted, odd_two, *sectors_two, even_two, partial, section, courant_r, courant_t, courant_z,
         sectors[0], even, odd,
@@ -409,17 +477,21 @@
     radial_matrix = jnp.asarray(interp_matrix(BR).T, BF16)
     fine_rows = 4 * BZ * BT
     evolved, patches = pl.pallas_call(
-        prolong_patches,
+        functools.partial(prolong_patches, count),
         out_shape=(field, jax.ShapeDtypeStruct((owned, fine_rows, 2 * BR), F32)),
-        in_specs=in_smem(1) + in_vmem(4),
+        in_specs=in_smem(1) + in_vmem(13 + count),
         out_specs=(pl.BlockSpec(memory_space=pltpu.HBM),) * 2,
         scratch_shapes=[
+            pltpu.VMEM((rows_z, cells_t, cells_r - lanes), F32),
             pltpu.VMEM((owned, fine_rows, 2 * BR), F32),
-            pltpu.SemaphoreType.DMA((-(-owned // GROUP) + 1,)),
+            pltpu.SemaphoreType.DMA((-(-owned // GROUP) + 2,)),
         ],
         compiler_params=PARAMS,
         name="prolong_patches",
-    )(slots, evolved, arrived, radial_matrix, tile_matrix)
+    )(
+        slots, head, arrived, radial_matrix, tile_matrix,
+        odd_two, *sectors_two, even_two, partial, section, courant_t, courant_z, sectors[0], even, odd,
+    )
     return (evolved, patches.reshape(1, owned, 2 * BZ, 2 * BT, 2 * BR))
 
 

time: 31.7 us -> 31.6 us (level)
  transfers between devices with their start and end apart: 6 -> 6, of which waited for: 4 -> 3; matrix products, arithmetic and copies ran while one was open for 0% -> 0% of each run, Pallas kernels for 4% -> 4%
where the time goes in v6:
time: 31.6 us; the launch traced here: 31.4 us
  blocking collectives  14.5 us (46%)
  starting transfers between devices  6.4 us (20%)
  Pallas kernels  5.49 us (17%)
  waiting for transfers between devices  4.33 us (14%)
  between operations  0.68 us (2%)
    all_to_all x1, blocking collectives, local(): lax.all_to_all(outgoing, 'ax', split_axis=0, concat_axis=0, tiled=True)  14.5 us
    ppermute x2, starting transfers between devices, exchange(): lax.ppermute(odd, ('az', 'ax'), odd_pairs)  4.04 us
    ppermute x2, waiting for transfers between devices, exchange(): sectors = [lax.ppermute(sector, 'az', by(s)) for s in steps]  3.01 us
    pallas_call x1, Pallas kernels, local(): pl.pallas_call(functools.partial(prolong_patches, count), out_shape=(fiel...  2.16 us
    ppermute x2, waiting for transfers between devices, exchange(): lax.ppermute(odd, ('az', 'ax'), odd_pairs)  1.31 us
    pallas_call x1, Pallas kernels, local(): pl.pallas_call(functools.partial(first_messages, len(given)), out_shape=t...  1.27 us
    ppermute x2, starting transfers between devices, exchange(): lax.ppermute(even, 'ax', even_pairs)  1.25 us
    ppermute x2, starting transfers between devices, exchange(): sectors = [lax.ppermute(sector, 'az', by(s)) for s in steps]  1.11 us
  transfers between devices with their start and end apart: 6, of which 3 were waited for; matrix products, arithmetic and copies ran while one was open for 0% of the time, Pallas kernels for 4%

profile of v6, /device:TPU:0, one launch (start us, length us, event | category | flops | bytes accessed | tf_op | source)
XLA Modules:
  0.0 31.4 jit_solution(4166133636536886315)
XLA Ops:
  0.6 0.0 copy-start
  0.6 0.0 copy-start.1
  0.7 1.3 %first_messages.1 = (f32[8,16,512]{2,1,0:T(8,128)S(1)}, bf16[8,16,512]{2,1,0:T(8,128)(2,1)S(1)}, bf16[8,16,512]{2,1,0:T(8,128)(2,1)S(1)}, bf16[8,16,512]{2,1,0:T...) custom-call(f32[8,16,512]{2,1,0:T(8,128)} %refs_0_.1, ...), custom_call_target="tpu_custom_call" | custom-call | tf_op jit(solution)/shard_map/first_messages/pallas_call | solution.py:410
  1.9 3.0 %collective-permute-start = (bf16[3,16,512]{2,1,0:T(8,128)(2,1)S(1)}, bf16[3,16,512]{2,1,0:T(8,128)(2,1)S(1)}, u32[]{:S(2)}, u32[]{:S(2)}) collective-permute-start(bf16[3,16,512]{2,1,0:T(8,128)(2,1)S(1)} %get-tuple-element.22), channel_id=1, source_target_pairs={{1,2},{2,1},{3,4},{4,3},{5,6},{6,5},{7,8},{8,7},{9,10},{10,9},{11,... | collective-permute-start | bytes 147464 | tf_op jit(solution)/shard_map/ppermute | solution.py:399
  5.0 0.1 collective-permute-start.1
  5.0 1.2 %collective-permute-start.2 = (bf16[3,16,512]{2,1,0:T(8,128)(2,1)S(1)}, bf16[3,16,512]{2,1,0:T(8,128)(2,1)S(1)}, u32[]{:S(2)}, u32[]{:S(2)}) collective-permute-start(bf16[3,16,512]{2,1,0:T(8,128)(2,1)S(1)} %get-tuple-element.24), channel_id=1, source_target_pairs={{0,1},{1,0},{2,3},{3,2},{4,5},{5,4},{6,7},{7,6},{8,9},{9,8},{10,11... | collective-permute-start | bytes 147464 | tf_op jit(solution)/shard_map/ppermute | solution.py:399
  6.3 0.7 %first_inner.1.refs_3_ = f32[8,16,512]{2,1,0:T(8,128)S(1)} custom-call(f32[8,16,512]{2,1,0:T(8,128)S(1)} %get-tuple-element.25.density.refs_4_, bf16[8,16,512]{2,1,0:T(8,128)(2,1)S(1)} %get-tuple-element.26.courant_r.refs_5_.refs_6_, bf16[8,16,512]{2,1,0:T(8,128)(2,1)S(1)} %get-tuple-element.27.courant_z.refs_7_.refs_8_.refs_6_, ...), custom_call_target="tpu_custom_call" | custom-call | flops 2621440 | bytes 1048576 | tf_op jit(solution)/shard_map/first_inner/pallas_call | solution.py:428
  7.0 0.0 collective-permute-done.refs_0_.refs_11_.refs_9_
  7.0 2.0 %collective-permute-done.1.refs_1_.refs_9_.refs_7_ = bf16[3,16,512]{2,1,0:T(8,128)(2,1)S(1)} collective-permute-done((bf16[3,16,512]{2,1,0:T(8,128)(2,1)S(1)}, bf16[3,16,512]{2,1,0:T(8,128)(2,1)S(1)}, u32[]{:S(2)}, u32[]{:S(2)}) %collective-permute-start.1) | collective-permute-done | bytes 49184 | tf_op jit(solution)/shard_map/ppermute | solution.py:398
  9.1 0.0 collective-permute-done.2.refs_2_.refs_10_.refs_8_
  9.1 0.4 %first_stage.1 = (f32[8,16,512]{2,1,0:T(8,128)S(1)}, bf16[5,8,512]{2,1,0:T(8,128)(2,1)S(1)}, bf16[5,8,512]{2,1,0:T(8,128)(2,1)S(1)}, bf16[5,8,512]{2,1,0:T(8,128)(2,1)S(1)}) custom-call(bf16[3,16,512]{2,1,0:T(8,128)(2,1)S(1)} %collective-permute-done.refs_0_.refs_11_.refs_9_, bf16[3,16,512]{2,1,0:T(8,128)(2,1)S(1)} %collective-permute-done.1.refs_1_.refs_9_.refs_7_, ...), custom_call_target="tpu_custom_call" | custom-call | tf_op jit(solution)/shard_map/first_stage/pallas_call | solution.py:437
  9.5 1.0 %collective-permute-start.3 = (bf16[5,8,512]{2,1,0:T(8,128)(2,1)S(1)}, bf16[5,8,512]{2,1,0:T(8,128)(2,1)S(1)}, u32[]{:S(2)}, u32[]{:S(2)}) collective-permute-start(bf16[5,8,512]{2,1,0:T(8,128)(2,1)S(1)} %get-tuple-element.30), channel_id=1, source_target_pairs={{1,2},{2,1},{3,4},{4,3},{5,6},{6,5},{7,8},{8,7},{9,10},{10,9},{11,... | collective-permute-start | bytes 122888 | tf_op jit(solution)/shard_map/ppermute | solution.py:399
  10.5 1.0 %collective-permute-start.4 = (bf16[5,8,512]{2,1,0:T(8,128)(2,1)S(1)}, bf16[5,8,512]{2,1,0:T(8,128)(2,1)S(1)}, u32[]{:S(2)}, u32[]{:S(2)}) collective-permute-start(bf16[5,8,512]{2,1,0:T(8,128)(2,1)S(1)} %get-tuple-element.31), channel_id=1, source_target_pairs={{0,16},{16,0},{1,17},{17,1},{2,18},{18,2},{3,19},{19,3},{4,20},{20... | collective-permute-start | bytes 122888 | tf_op jit(solution)/shard_map/ppermute | solution.py:398
  11.5 0.0 collective-permute-start.5
  11.5 0.7 %second_inner.1.refs_4_.refs_3_ = f32[8,16,512]{2,1,0:T(8,128)S(1)} custom-call(f32[8,16,512]{2,1,0:T(8,128)S(1)} %get-tuple-element.25.density.refs_4_, f32[8,16,512]{2,1,0:T(8,128)S(1)} %get-tuple-element.33.section.refs_5_.refs_4_, bf16[8,16,512]{2,1,0:T(8,128)(2,1)S(1)} %get-tuple-element.26.courant_r.refs_5_.refs_6_, ...), custom_call_target="tpu_custom_call" | custom-call | flops 2621440 | bytes 1048576 | tf_op jit(solution)/shard_map/second_inner/pallas_call | solution.py:447
  12.2 1.3 %collective-permute-done.3.refs_1_.refs_0_ = bf16[5,8,512]{2,1,0:T(8,128)(2,1)S(1)} collective-permute-done((bf16[5,8,512]{2,1,0:T(8,128)(2,1)S(1)}, bf16[5,8,512]{2,1,0:T(8,128)(2,1)S(1)}, u32[]{:S(2)}, u32[]{:S(2)}) %collective-permute-start.3) | collective-permute-done | bytes 40992 | tf_op jit(solution)/shard_map/ppermute | solution.py:399
  13.5 1.0 %collective-permute-done.4.refs_2_.refs_1_ = bf16[5,8,512]{2,1,0:T(8,128)(2,1)S(1)} collective-permute-done((bf16[5,8,512]{2,1,0:T(8,128)(2,1)S(1)}, bf16[5,8,512]{2,1,0:T(8,128)(2,1)S(1)}, u32[]{:S(2)}, u32[]{:S(2)}) %collective-permute-start.4) | collective-permute-done | bytes 40992 | tf_op jit(solution)/shard_map/ppermute | solution.py:398
  14.5 0.0 collective-permute-done.5.refs_3_.refs_2_
  14.5 0.2 second_head.1
  14.7 14.5 %all_to_all.5.arrived = bf16[16,64,128]{2,1,0:T(8,128)(2,1)S(1)} all-to-all(bf16[16,64,128]{2,1,0:T(8,128)(2,1)S(1)} %get-tuple-element.35), channel_id=1, replica_groups=mesh['az'=2,'ax'=16] {'ax'}, dimensions={0} | all-to-all | bytes 524288 | tf_op jit(solution)/shard_map/all_to_all | solution.py:473
  29.2 0.0 copy-done
  29.2 0.0 copy-done.1
  29.2 2.2 %prolong_patches.1 = (f32[8,16,512]{2,1,0:T(8,128)}, f32[24,128,256]{2,1,0:T(8,128)}) custom-call(s32[1,24]{1,0:T(1,128)S(4)} %get-tuple-element.20.slots, f32[8,16,256]{2,1,0:T(8,128)S(1)} %get-tuple-element.34.head, bf16[16,64,128]{2,1,0:T(8,128)(2,1)S(1)} %all_to_all.5.arrived, bf16[128,256]{1,0:T(8,128)(2,1)S(1)} %copy-done, ...), custom_call_target="tpu_custom_call" | custom-call | tf_op jit(solution)/shard_map/prolong_patches/pallas_call | solution.py:479
Async XLA Ops:
  0.6 28.6 %copy-start = (bf16[128,256]{1,0:T(8,128)(2,1)S(1)}, bf16[128,256]{1,0:T(8,128)(2,1)}, u32[]{:S(2)}) copy-start(bf16[128,256]{1,0:T(8,128)(2,1)} %constant.5.clone.radial_matrix) | copy-start | bytes 196612
  0.6 28.6 %copy-start.1 = (bf16[128,64]{1,0:T(8,128)(2,1)S(1)}, bf16[128,64]{1,0:T(8,128)(2,1)}, u32[]{:S(2)}) copy-start(bf16[128,64]{1,0:T(8,128)(2,1)} %constant.4.clone.tile_matrix) | copy-start | bytes 49156
  1.9 5.1 %collective-permute-start = (bf16[3,16,512]{2,1,0:T(8,128)(2,1)S(1)}, bf16[3,16,512]{2,1,0:T(8,128)(2,1)S(1)}, u32[]{:S(2)}, u32[]{:S(2)}) collective-permute-start(bf16[3,16,512]{2,1,0:T(8,128)(2,1)S(1)} %get-tuple-element.22), channel_id=1, source_target_pairs={{1,2},{2,1},{3,4},{4,3},{5,6},{6,5},{7,8},{8,7},{9,10},{10,9},{11,... | collective-permute-start | bytes 147464 | tf_op jit(solution)/shard_map/ppermute | solution.py:399
  5.0 4.1 %collective-permute-start.1 = (bf16[3,16,512]{2,1,0:T(8,128)(2,1)S(1)}, bf16[3,16,512]{2,1,0:T(8,128)(2,1)S(1)}, u32[]{:S(2)}, u32[]{:S(2)}) collective-permute-start(bf16[3,16,512]{2,1,0:T(8,128)(2,1)S(1)} %get-tuple-element.23), channel_id=1, source_target_pairs={{0,16},{16,0},{1,17},{17,1},{2,18},{18,2},{3,19},{19,3},{4,20},{20... | collective-permute-start | bytes 147464 | tf_op jit(solution)/shard_map/ppermute | solution.py:398
  5.0 4.0 %collective-permute-start.2 = (bf16[3,16,512]{2,1,0:T(8,128)(2,1)S(1)}, bf16[3,16,512]{2,1,0:T(8,128)(2,1)S(1)}, u32[]{:S(2)}, u32[]{:S(2)}) collective-permute-start(bf16[3,16,512]{2,1,0:T(8,128)(2,1)S(1)} %get-tuple-element.24), channel_id=1, source_target_pairs={{0,1},{1,0},{2,3},{3,2},{4,5},{5,4},{6,7},{7,6},{8,9},{9,8},{10,11... | collective-permute-start | bytes 147464 | tf_op jit(solution)/shard_map/ppermute | solution.py:399
  9.5 4.0 %collective-permute-start.3 = (bf16[5,8,512]{2,1,0:T(8,128)(2,1)S(1)}, bf16[5,8,512]{2,1,0:T(8,128)(2,1)S(1)}, u32[]{:S(2)}, u32[]{:S(2)}) collective-permute-start(bf16[5,8,512]{2,1,0:T(8,128)(2,1)S(1)} %get-tuple-element.30), channel_id=1, source_target_pairs={{1,2},{2,1},{3,4},{4,3},{5,6},{6,5},{7,8},{8,7},{9,10},{10,9},{11,... | collective-permute-start | bytes 122888 | tf_op jit(solution)/shard_map/ppermute | solution.py:399
  10.5 4.0 %collective-permute-start.4 = (bf16[5,8,512]{2,1,0:T(8,128)(2,1)S(1)}, bf16[5,8,512]{2,1,0:T(8,128)(2,1)S(1)}, u32[]{:S(2)}, u32[]{:S(2)}) collective-permute-start(bf16[5,8,512]{2,1,0:T(8,128)(2,1)S(1)} %get-tuple-element.31), channel_id=1, source_target_pairs={{0,16},{16,0},{1,17},{17,1},{2,18},{18,2},{3,19},{19,3},{4,20},{20... | collective-permute-start | bytes 122888 | tf_op jit(solution)/shard_map/ppermute | solution.py:398
  11.5 3.0 %collective-permute-start.5 = (bf16[5,8,512]{2,1,0:T(8,128)(2,1)S(1)}, bf16[5,8,512]{2,1,0:T(8,128)(2,1)S(1)}, u32[]{:S(2)}, u32[]{:S(2)}) collective-permute-start(bf16[5,8,512]{2,1,0:T(8,128)(2,1)S(1)} %get-tuple-element.32), channel_id=1, source_target_pairs={{0,1},{1,0},{2,3},{3,2},{4,5},{5,4},{6,7},{7,6},{8,9},{9,8},{10,11... | collective-permute-start | bytes 122888 | tf_op jit(solution)/shard_map/ppermute | solution.py:399

commit v7 on v6

--- a/solution.py
+++ b/solution.py
@@ -22,29 +22,25 @@
 BLOCK_ROWS = BZ * BT
 
 
-def pack_sector(values, courant_t, out_ref):
-    rows_z, cells_t, cells_r = values.shape
+def gathered(values, j):
+    rows_z, _, cells_r = values.shape
     row = lax.broadcasted_iota(jnp.int32, (8, cells_r), 0)
+    tile = jnp.zeros((8, cells_r), F32)
+    for k in range(rows_z):
+        part = values[k].astype(F32)[j // 8 * 8 : j // 8 * 8 + 8, :]
+        tile = jnp.where(row == k, pltpu.roll(part, (k - j) % 8, 0), tile)
+    return tile
+
+
+def pack_sector(tiles, values, out_ref):
+    rows_z, cells_t, _ = values.shape
     lane = lax.broadcasted_iota(jnp.int32, (cells_t, 128), 1)
     inner = jnp.zeros((cells_t, 128), F32)
-    ends = []
     for k in range(rows_z):
-        ends.append(jnp.where(row < 2, values[k, 0:8, :], values[k, cells_t - 8 :, :]))
         inner = jnp.where(lane == k, values[k, :, 0:1], inner)
-    outer = (row < 2) | (row > 5)
-    tiles = [
-        jnp.where(outer, ends[k], pltpu.roll(ends[k + 1], 4, 0)) for k in range(0, rows_z, 2)
-    ]
-    if courant_t is not None:
-        faces = jnp.zeros((8, cells_r), F32)
-        for k in range(rows_z):
-            face = courant_t[k].astype(F32)[cells_t - 8 :, :]
-            faces = jnp.where(row == k, pltpu.roll(face, (k + 1) % 8, 0), faces)
-        tiles.append(faces)
     rounded = inner.astype(BF16).astype(F32)
     rest = inner - rounded
-    tiles.append(jnp.concatenate([rounded[:8], rounded[8:], rest[:8], rest[8:]], axis=1))
-    write_tiles(out_ref, 0, tiles)
+    write_tiles(out_ref, 0, tiles + [jnp.concatenate([rounded[:8], rounded[8:], rest[:8], rest[8:]], axis=1)])
 
 
 def unpack_inner(msg, index):
@@ -91,7 +87,7 @@
 
 def first_messages(count, *refs):
     given, held = refs[:count], refs[count : 2 * count]
-    sector_out, even_out, odd_out, sems = refs[2 * count :]
+    edges, sector_out, even_out, odd_out, sems = refs[2 * count :]
     copies = [pltpu.make_async_copy(given[i], held[i], sems.at[i]) for i in range(count)]
     for copy in copies:
         copy.start()
@@ -99,7 +95,11 @@
     for copy in copies[:3]:
         copy.wait()
     pack_slab(density, courant_z, even_out, odd_out)
-    pack_sector(density, courant_t, sector_out)
+    cells_t = density.shape[1]
+    tiles = [gathered(density, j) for j in (0, 1, cells_t - 2, cells_t - 1)]
+    for index, tile in enumerate(tiles):
+        edges[index] = tile
+    pack_sector(tiles + [gathered(courant_t, cells_t - 1)], density, sector_out)
     for copy in copies[3:]:
         copy.wait()
 
@@ -120,7 +120,7 @@
     return courant * jnp.where(courant > 0.0, low, high)
 
 
-def inner_rates(values, courant_r, courant_z, ionization):
+def inner_rates(values, courant_r, courant_t, courant_z, ionization):
     rows_z, cells_t, cells_r = values.shape
     zero = jnp.zeros((cells_t, cells_r), F32)
 
@@ -131,6 +131,7 @@
     index = lane.astype(F32)
     area = jnp.where(lane < cells_r - 1, index + 1.0, 0.0)
     inverse_radius = 1.0 / (index + 0.5)
+    last_row = lax.broadcasted_iota(jnp.int32, (cells_t, cells_r), 0) == cells_t - 1
     flux_z = zero
     for k in range(rows_z):
         here, back, up = row_at(k), row_at(k - 1), row_at(k + 1)
@@ -143,6 +144,12 @@
             - (next_flux - flux_z)
         )
         flux_z = next_flux
+        courant = jnp.where(last_row, 0.0, courant_t[k].astype(F32))
+        quarter = 0.25 * (pltpu.roll(here, cells_t - 1, 0) - pltpu.roll(here, 1, 0))
+        flux = courant * jnp.where(
+            courant > 0.0, here + quarter, pltpu.roll(here - quarter, cells_t - 1, 0)
+        )
+        rate = rate + (pltpu.roll(flux, 1, 0) - flux)
         inward = jnp.where(lane == 0, 0.0, pltpu.roll(here, 1, 1))
         outward = jnp.where(lane == cells_r - 1, 0.0, pltpu.roll(here, cells_r - 1, 1))
         quarter = 0.25 * (outward - inward)
@@ -154,14 +161,14 @@
         yield rate + (carried - pltpu.roll(carried, 1, 1)) * inverse_radius
 
 
-def outer_rates(values, lanes, sector, inner, slab, faces_below, courants):
+def finish(out, partial, scale, values, edges, lanes, sector, inner, slab, faces_below, faces, courants):
     rows_z, cells_t = values.shape[:2]
     low, high = lanes
     width = high - low
     left, right = sector
     even_msg, odd_msg = slab
     left_faces, even_faces, odd_faces = faces_below
-    courant_r, courant_t, courant_z = courants
+    courant_r, courant_z = courants
     me = lax.axis_index("ax")
     is_even = lax.rem(me, 2) == 0
     has_below = me > 0
@@ -196,85 +203,98 @@
         top - 1: -high_change,
         top: high_change - last_flux + DIFFUSION * above_one,
     }
-    halo_row = lax.broadcasted_iota(jnp.int32, (8, width), 0)
     lane = lax.broadcasted_iota(jnp.int32, (cells_t, 128), 1)
-    faces = tile_of(left_faces, rows_z // 2, lanes)
-    rows = cells_t + 8
     for k in range(rows_z):
-        here = at(k)
-        halo = tile_of(left, k // 2, lanes)
-        if right is not left:
-            beyond = (halo_row < 2) | (halo_row == 4) | (halo_row == 5)
-            halo = jnp.where(beyond, tile_of(right, k // 2, lanes), halo)
-        if k % 2:
-            halo = pltpu.roll(halo, 4, 0)
-        ring = jnp.concatenate([halo, here], axis=0)
-        face_halo = pltpu.roll(faces, 7 - k, 0)
-        courant = jnp.concatenate([face_halo, courant_t[k, :, low:high].astype(F32)], axis=0)
-        quarter = 0.25 * (pltpu.roll(ring, rows - 1, 0) - pltpu.roll(ring, 1, 0))
-        flux = courant * jnp.where(courant > 0.0, ring + quarter, pltpu.roll(ring - quarter, rows - 1, 0))
-        rate = (pltpu.roll(flux, 1, 0) - flux)[8:, :]
+        row = partial[k, :, low:high]
         if k in axial:
-            rate = rate + axial[k]
-        if inner is None:
-            yield rate
-            continue
-        change = 0.25 * jnp.maximum(courant_r[k, :, 0:128].astype(F32), 0.0)
-        change = change * (pltpu.roll(inner, 128 - k, 1) if k else inner)
-        change = jnp.where(lane == 0, change, 0.0)
-        change = 2.0 * change - (1.0 / 1.5) * pltpu.roll(change, 1, 1)
-        yield jnp.concatenate([rate[:, 0:128] + change, rate[:, 128:]], axis=1)
-
-
-def first_inner(density, courant_r, courant_z, ionization, partial):
-    for k, rate in enumerate(inner_rates(density, courant_r, courant_z, ionization)):
+            row = row + scale * axial[k]
+        if inner is not None:
+            change = 0.25 * scale * jnp.maximum(courant_r[k, :, 0:128].astype(F32), 0.0)
+            change = change * (pltpu.roll(inner, 128 - k, 1) if k else inner)
+            change = jnp.where(lane == 0, change, 0.0)
+            change = 2.0 * change - (1.0 / 1.5) * pltpu.roll(change, 1, 1)
+            row = jnp.concatenate([row[:, 0:128] + change, row[:, 128:]], axis=1)
+        out[k] = row
+    first, second, last_but_one, last = [edges[index, :, low:high] for index in range(4)]
+    first_face, next_face, last_face = [faces[index, :, low:high] for index in range(3)]
+    before_two, before_one = tile_of(left, 2, lanes), tile_of(left, 3, lanes)
+    after_one, after_two = tile_of(right, 0, lanes), tile_of(right, 1, lanes)
+    low_flux = axial_flux(tile_of(left_faces, 4, lanes), before_two, before_one, first, second)
+    high_flux = axial_flux(last_face, last_but_one, last, after_one, after_two)
+    low_change = -0.25 * jnp.maximum(first_face, 0.0) * (before_one - last)
+    high_change = -0.25 * jnp.minimum(next_face, 0.0) * (after_one - first)
+    changes = {
+        0: low_flux - low_change,
+        1: low_change,
+        cells_t - 2: -high_change,
+        cells_t - 1: high_change - high_flux,
+    }
+    tiles = []
+    for j, change in changes.items():
+        tiles.append(out[:, j, :] + scale * change)
+        out[:, j, :] = tiles[-1]
+    return tiles
+
+
+def first_inner(density, courant_r, courant_t, courant_z, ionization, partial, faces):
+    for k, rate in enumerate(inner_rates(density, courant_r, courant_t, courant_z, ionization)):
         partial[k] = density[k] + rate
-
-
-def second_inner(density, section, courant_r, courant_z, ionization, partial):
-    for k, rate in enumerate(inner_rates(section, courant_r, courant_z, ionization)):
+    cells_t = density.shape[1]
+    for index, j in enumerate((0, cells_t - 2, cells_t - 1)):
+        faces[index] = gathered(courant_t, j)
+
+
+def second_inner(density, section, courant_r, courant_t, courant_z, ionization, partial):
+    for k, rate in enumerate(inner_rates(section, courant_r, courant_t, courant_z, ionization)):
         partial[k] = 0.5 * (density[k] + section[k] + rate)
 
 
 def first_stage(count, *refs):
     odd, sector, refs = refs[0], refs[1 : 1 + count], refs[1:]
-    even, partial, density, courant_r, courant_t, courant_z = refs[count : count + 6]
-    section, sector_out, even_out, odd_out = refs[count + 6 :]
+    even, partial, density, edges, faces, courant_r, courant_z = refs[count : count + 7]
+    section, section_edges, sector_out, even_out, odd_out = refs[count + 7 :]
     left, right, across = sector if count == 3 else sector * 3
-    inner = unpack_inner(across, density.shape[0] // 2 + 1)
-    steps = outer_rates(
+    tiles = finish(
+        section,
+        partial,
+        1.0,
         density,
+        edges,
         (0, density.shape[2]),
         (left, right),
-        inner,
+        unpack_inner(across, 5),
         (even, odd),
         (left, even, odd),
-        (courant_r, courant_t, courant_z),
-    )
-    for k, rate in enumerate(steps):
-        section[k] = partial[k] + rate
-    pack_sector(section, None, sector_out)
+        faces,
+        (courant_r, courant_z),
+    )
+    for index, tile in enumerate(tiles):
+        section_edges[index] = tile
+    pack_sector(tiles, section, sector_out)
     pack_slab(section, None, even_out, odd_out)
 
 
 def second_head(count, *refs):
     wanted, odd, sector, refs = refs[0], refs[1], refs[2 : 2 + count], refs[2:]
-    even, partial, section, courant_r, courant_t, courant_z = refs[count : count + 6]
-    left_faces, even_faces, odd_faces = refs[count + 6 : count + 9]
-    evolved, outgoing, table = refs[count + 9 :]
+    even, partial, section, edges, faces, courant_r, courant_z = refs[count : count + 7]
+    left_faces, even_faces, odd_faces = refs[count + 7 : count + 10]
+    evolved, outgoing, table = refs[count + 10 :]
     rows_z, cells_t, lanes = evolved.shape
     left, right, across = sector if count == 3 else sector * 3
-    steps = outer_rates(
+    finish(
+        evolved,
+        partial,
+        0.5,
         section,
+        edges,
         (0, lanes),
         (left, right),
-        unpack_inner(across, rows_z // 2),
+        unpack_inner(across, 4),
         (even, odd),
         (left_faces, even_faces, odd_faces),
-        (courant_r, courant_t, courant_z),
-    )
-    for k, rate in enumerate(steps):
-        evolved[k] = partial[k, :, 0:lanes] + 0.5 * rate
+        faces,
+        (courant_r, courant_z),
+    )
     blocks_t, blocks_r = cells_t // BT, section.shape[2] // BR
     total = rows_z // BZ * blocks_t * blocks_r
     for block in range(total):
@@ -293,20 +313,22 @@
 
 def second_tail(count, refs, evolved):
     odd, sector, refs = refs[0], refs[1 : 1 + count], refs[1:]
-    even, partial, section, courant_t, courant_z, left_faces, even_faces, odd_faces = refs[count:]
+    even, partial, section, edges, faces, courant_z, left_faces, even_faces, odd_faces = refs[count:]
     left, right, _ = sector if count == 3 else sector * 3
-    low, high = section.shape[2] - evolved.shape[2], section.shape[2]
-    steps = outer_rates(
+    finish(
+        evolved,
+        partial,
+        0.5,
         section,
-        (low, high),
+        edges,
+        (section.shape[2] - evolved.shape[2], section.shape[2]),
         (left, right),
         None,
         (even, odd),
         (left_faces, even_faces, odd_faces),
-        (None, courant_t, courant_z),
-    )
-    for k, rate in enumerate(steps):
-        evolved[k] = partial[k, :, low:high] + 0.5 * rate
+        faces,
+        (None, courant_z),
+    )
 
 
 def halves(x):
@@ -315,7 +337,7 @@
 
 
 def prolong_patches(count, slots, head, arrived, radial_matrix, tile_matrix, *refs):
-    for_tail, (evolved, patches, tail, fine, sems) = refs[: count + 9], refs[count + 9 :]
+    for_tail, (evolved, patches, tail, fine, sems) = refs[: count + 10], refs[count + 10 :]
     lanes = head.shape[2]
     copies = [pltpu.make_async_copy(head, evolved.at[:, :, pl.ds(0, lanes)], sems.at[0])]
     copies[0].start()
@@ -400,6 +422,7 @@
 
     lanes = HEAD_R * BR
     message = jax.ShapeDtypeStruct((rows_z // 4 + 1, cells_t, cells_r), BF16)
+    edge_tiles = jax.ShapeDtypeStruct((4, rows_z, cells_r), F32)
     second_message = jax.ShapeDtypeStruct((rows_z // 2 + 1, 8, cells_r), BF16)
     field = jax.ShapeDtypeStruct(density.shape, F32)
 
@@ -407,15 +430,15 @@
         density, courant_t, courant_z, courant_r, ionization, jnp.transpose(send_block, (0, 2, 1)), recv_slot
     )
     given = tuple(pltpu.with_memory_space_constraint(x, pltpu.HBM) for x in given)
-    *held, sector, even, odd = pl.pallas_call(
+    *held, edges, sector, even, odd = pl.pallas_call(
         functools.partial(first_messages, len(given)),
         out_shape=tuple(
             pltpu.SMEM(x.shape, x.dtype) if x.dtype == jnp.int32 else jax.ShapeDtypeStruct(x.shape, x.dtype)
             for x in given
         )
-        + (message,) * 3,
+        + (edge_tiles,) + (message,) * 3,
         in_specs=[pl.BlockSpec(memory_space=pltpu.HBM)] * len(given),
-        out_specs=tuple(in_vmem(len(given) - 2) + in_smem(2) + in_vmem(3)),
+        out_specs=tuple(in_vmem(len(given) - 2) + in_smem(2) + in_vmem(4)),
         scratch_shapes=[pltpu.SemaphoreType.DMA((len(given),))],
         compiler_params=PARAMS,
         name="first_messages",
@@ -425,34 +448,34 @@
     count = len(sectors)
 
     inner_cost = pl.CostEstimate(flops=40 * density.size, bytes_accessed=16 * density.size, transcendentals=0)
-    partial = pl.pallas_call(
+    partial, faces = pl.pallas_call(
         first_inner,
-        out_shape=field,
-        in_specs=in_vmem(4),
-        out_specs=in_vmem(1)[0],
+        out_shape=(field, jax.ShapeDtypeStruct((3, rows_z, cells_r), F32)),
+        in_specs=in_vmem(5),
+        out_specs=tuple(in_vmem(2)),
         compiler_params=PARAMS,
         cost_estimate=inner_cost,
         name="first_inner",
-    )(density, courant_r, courant_z, ionization)
-    section, sector, even_two, odd_two = pl.pallas_call(
+    )(density, courant_r, courant_t, courant_z, ionization)
+    section, section_edges, sector, even_two, odd_two = pl.pallas_call(
         functools.partial(first_stage, count),
-        out_shape=(field,) + (second_message,) * 3,
-        in_specs=in_vmem(7 + count),
-        out_specs=tuple(in_vmem(4)),
+        out_shape=(field, edge_tiles) + (second_message,) * 3,
+        in_specs=in_vmem(8 + count),
+        out_specs=tuple(in_vmem(5)),
         compiler_params=PARAMS,
         name="first_stage",
-    )(odd, *sectors, even, partial, density, courant_r, courant_t, courant_z)
+    )(odd, *sectors, even, partial, density, edges, faces, courant_r, courant_z)
     sectors_two, even_two, odd_two = exchange(sector, even_two, odd_two, all_steps)
 
     partial = pl.pallas_call(
         second_inner,
         out_shape=field,
-        in_specs=in_vmem(5),
+        in_specs=in_vmem(6),
         out_specs=in_vmem(1)[0],
         compiler_params=PARAMS,
         cost_estimate=inner_cost,
         name="second_inner",
-    )(density, section, courant_r, courant_z, ionization)
+    )(density, section, courant_r, courant_t, courant_z, ionization)
     blocks = rows_z // BZ * (cells_t // BT) * (cells_r // BR)
     head, outgoing = pl.pallas_call(
         functools.partial(second_head, count),
@@ -460,13 +483,13 @@
             jax.ShapeDtypeStruct((rows_z, cells_t, lanes), F32),
             jax.ShapeDtypeStruct((ax_count, CAP * BLOCK_ROWS, BR), BF16),
         ),
-        in_specs=in_smem(1) + in_vmem(10 + count),
+        in_specs=in_smem(1) + in_vmem(11 + count),
         out_specs=tuple(in_vmem(2)),
         scratch_shapes=[pltpu.VMEM((blocks + 1, BLOCK_ROWS, BR), BF16)],
         compiler_params=PARAMS,
         name="second_head",
     )(
-        wanted, odd_two, *sectors_two, even_two, partial, section, courant_r, courant_t, courant_z,
+        wanted, odd_two, *sectors_two, even_two, partial, section, section_edges, faces, courant_r, courant_z,
         sectors[0], even, odd,
     )
 
@@ -479,7 +502,7 @@
     evolved, patches = pl.pallas_call(
         functools.partial(prolong_patches, count),
         out_shape=(field, jax.ShapeDtypeStruct((owned, fine_rows, 2 * BR), F32)),
-        in_specs=in_smem(1) + in_vmem(13 + count),
+        in_specs=in_smem(1) + in_vmem(14 + count),
         out_specs=(pl.BlockSpec(memory_space=pltpu.HBM),) * 2,
         scratch_shapes=[
             pltpu.VMEM((rows_z, cells_t, cells_r - lanes), F32),
@@ -490,7 +513,7 @@
         name="prolong_patches",
     )(
         slots, head, arrived, radial_matrix, tile_matrix,
-        odd_two, *sectors_two, even_two, partial, section, courant_t, courant_z, sectors[0], even, odd,
+        odd_two, *sectors_two, even_two, partial, section, section_edges, faces, courant_z, sectors[0], even, odd,
     )
     return (evolved, patches.reshape(1, owned, 2 * BZ, 2 * BT, 2 * BR))
 

time: 31.6 us -> 31.5 us (level)
  transfers between devices with their start and end apart: 6 -> 6, of which waited for: 3 -> 3; matrix products, arithmetic and copies ran while one was open for 0% -> 0% of each run, Pallas kernels for 4% -> 5%
where the time goes in v7:
time: 31.5 us; the launch traced here: 31.3 us
  blocking collectives  14.5 us (46%)
  starting transfers between devices  6.45 us (20%)
  Pallas kernels  5.61 us (18%)
  waiting for transfers between devices  4.04 us (13%)
  between operations  0.7 us (2%)
    all_to_all x1, blocking collectives, local(): lax.all_to_all(outgoing, 'ax', split_axis=0, concat_axis=0, tiled=True)  14.5 us
    ppermute x2, starting transfers between devices, exchange(): lax.ppermute(odd, ('az', 'ax'), odd_pairs)  4.09 us
    ppermute x2, waiting for transfers between devices, exchange(): sectors = [lax.ppermute(sector, 'az', by(s)) for s in steps]  2.91 us
    pallas_call x1, Pallas kernels, local(): pl.pallas_call(functools.partial(prolong_patches, count), out_shape=(fiel...  2.15 us
    pallas_call x1, Pallas kernels, local(): pl.pallas_call(functools.partial(first_messages, len(given)), out_shape=t...  1.26 us
    ppermute x2, starting transfers between devices, exchange(): lax.ppermute(even, 'ax', even_pairs)  1.25 us
    ppermute x2, waiting for transfers between devices, exchange(): lax.ppermute(odd, ('az', 'ax'), odd_pairs)  1.13 us
    ppermute x2, starting transfers between devices, exchange(): sectors = [lax.ppermute(sector, 'az', by(s)) for s in steps]  1.11 us
  transfers between devices with their start and end apart: 6, of which 3 were waited for; matrix products, arithmetic and copies ran while one was open for 0% of the time, Pallas kernels for 5%

profile of v7, /device:TPU:0, one launch (start us, length us, event | category | flops | bytes accessed | tf_op | source)
XLA Modules:
  0.0 31.3 jit_solution(5761939559651196503)
XLA Ops:
  0.6 0.0 copy-start
  0.6 0.0 copy-start.1
  0.7 1.3 %first_messages.1 = (f32[8,16,512]{2,1,0:T(8,128)S(1)}, bf16[8,16,512]{2,1,0:T(8,128)(2,1)S(1)}, bf16[8,16,512]{2,1,0:T(8,128)(2,1)S(1)}, bf16[8,16,512]{2,1,0:T...) custom-call(f32[8,16,512]{2,1,0:T(8,128)} %refs_0_.1, ...), custom_call_target="tpu_custom_call" | custom-call | tf_op jit(solution)/shard_map/first_messages/pallas_call | solution.py:433
  1.9 3.0 %collective-permute-start = (bf16[3,16,512]{2,1,0:T(8,128)(2,1)S(1)}, bf16[3,16,512]{2,1,0:T(8,128)(2,1)S(1)}, u32[]{:S(2)}, u32[]{:S(2)}) collective-permute-start(bf16[3,16,512]{2,1,0:T(8,128)(2,1)S(1)} %get-tuple-element.26), channel_id=1, source_target_pairs={{1,2},{2,1},{3,4},{4,3},{5,6},{6,5},{7,8},{8,7},{9,10},{10,9},{11,... | collective-permute-start | bytes 147464 | tf_op jit(solution)/shard_map/ppermute | solution.py:421
  5.0 0.1 collective-permute-start.1
  5.0 1.2 %collective-permute-start.2 = (bf16[3,16,512]{2,1,0:T(8,128)(2,1)S(1)}, bf16[3,16,512]{2,1,0:T(8,128)(2,1)S(1)}, u32[]{:S(2)}, u32[]{:S(2)}) collective-permute-start(bf16[3,16,512]{2,1,0:T(8,128)(2,1)S(1)} %get-tuple-element.28), channel_id=1, source_target_pairs={{0,1},{1,0},{2,3},{3,2},{4,5},{5,4},{6,7},{7,6},{8,9},{9,8},{10,11... | collective-permute-start | bytes 147464 | tf_op jit(solution)/shard_map/ppermute | solution.py:421
  6.3 0.8 %first_inner.1 = (f32[8,16,512]{2,1,0:T(8,128)S(1)}, f32[3,8,512]{2,1,0:T(8,128)S(1)}) custom-call(f32[8,16,512]{2,1,0:T(8,128)S(1)} %get-tuple-element.29.density.refs_4_, bf16[8,16,512]{2,1,0:T(8,128)(2,1)S(1)} %get-tuple-element.30.courant_r.refs_7_.refs_8_, bf16[8,16,512]{2,1,0:T(8,128)(2,1)S(1)} %get-tuple-element.31.courant_t, ...), custom_call_target="tpu_custom_call" | custom-call | flops 2621440 | bytes 1048576 | tf_op jit(solution)/shard_map/first_inner/pallas_call | solution.py:451
  7.1 0.0 collective-permute-done.refs_0_.refs_12_.refs_10_
  7.1 1.9 %collective-permute-done.1.refs_1_.refs_10_.refs_8_ = bf16[3,16,512]{2,1,0:T(8,128)(2,1)S(1)} collective-permute-done((bf16[3,16,512]{2,1,0:T(8,128)(2,1)S(1)}, bf16[3,16,512]{2,1,0:T(8,128)(2,1)S(1)}, u32[]{:S(2)}, u32[]{:S(2)}) %collective-permute-start.1) | collective-permute-done | bytes 49184 | tf_op jit(solution)/shard_map/ppermute | solution.py:420
  9.1 0.0 collective-permute-done.2.refs_2_.refs_11_.refs_9_
  9.1 0.3 first_stage.1
  9.3 1.1 %collective-permute-start.3 = (bf16[5,8,512]{2,1,0:T(8,128)(2,1)S(1)}, bf16[5,8,512]{2,1,0:T(8,128)(2,1)S(1)}, u32[]{:S(2)}, u32[]{:S(2)}) collective-permute-start(bf16[5,8,512]{2,1,0:T(8,128)(2,1)S(1)} %get-tuple-element.37), channel_id=1, source_target_pairs={{1,2},{2,1},{3,4},{4,3},{5,6},{6,5},{7,8},{8,7},{9,10},{10,9},{11,... | collective-permute-start | bytes 122888 | tf_op jit(solution)/shard_map/ppermute | solution.py:421
  10.4 1.0 %collective-permute-start.4 = (bf16[5,8,512]{2,1,0:T(8,128)(2,1)S(1)}, bf16[5,8,512]{2,1,0:T(8,128)(2,1)S(1)}, u32[]{:S(2)}, u32[]{:S(2)}) collective-permute-start(bf16[5,8,512]{2,1,0:T(8,128)(2,1)S(1)} %get-tuple-element.38), channel_id=1, source_target_pairs={{0,16},{16,0},{1,17},{17,1},{2,18},{18,2},{3,19},{19,3},{4,20},{20... | collective-permute-start | bytes 122888 | tf_op jit(solution)/shard_map/ppermute | solution.py:420
  11.4 0.0 collective-permute-start.5
  11.4 0.8 %second_inner.1.refs_4_.refs_3_ = f32[8,16,512]{2,1,0:T(8,128)S(1)} custom-call(f32[8,16,512]{2,1,0:T(8,128)S(1)} %get-tuple-element.29.density.refs_4_, f32[8,16,512]{2,1,0:T(8,128)S(1)} %get-tuple-element.40.section.refs_5_.refs_4_, bf16[8,16,512]{2,1,0:T(8,128)(2,1)S(1)} %get-tuple-element.30.courant_r.refs_7_.refs_8_, ...), custom_call_target="tpu_custom_call" | custom-call | flops 2621440 | bytes 1048576 | tf_op jit(solution)/shard_map/second_inner/pallas_call | solution.py:470
  12.3 1.1 %collective-permute-done.3.refs_1_.refs_0_ = bf16[5,8,512]{2,1,0:T(8,128)(2,1)S(1)} collective-permute-done((bf16[5,8,512]{2,1,0:T(8,128)(2,1)S(1)}, bf16[5,8,512]{2,1,0:T(8,128)(2,1)S(1)}, u32[]{:S(2)}, u32[]{:S(2)}) %collective-permute-start.3) | collective-permute-done | bytes 40992 | tf_op jit(solution)/shard_map/ppermute | solution.py:421
  13.4 1.0 %collective-permute-done.4.refs_2_.refs_1_ = bf16[5,8,512]{2,1,0:T(8,128)(2,1)S(1)} collective-permute-done((bf16[5,8,512]{2,1,0:T(8,128)(2,1)S(1)}, bf16[5,8,512]{2,1,0:T(8,128)(2,1)S(1)}, u32[]{:S(2)}, u32[]{:S(2)}) %collective-permute-start.4) | collective-permute-done | bytes 40992 | tf_op jit(solution)/shard_map/ppermute | solution.py:420
  14.4 0.0 collective-permute-done.5.refs_3_.refs_2_
  14.4 0.2 second_head.1
  14.7 14.5 %all_to_all.5.arrived = bf16[16,64,128]{2,1,0:T(8,128)(2,1)S(1)} all-to-all(bf16[16,64,128]{2,1,0:T(8,128)(2,1)S(1)} %get-tuple-element.43), channel_id=1, replica_groups=mesh['az'=2,'ax'=16] {'ax'}, dimensions={0} | all-to-all | bytes 524288 | tf_op jit(solution)/shard_map/all_to_all | solution.py:496
  29.1 0.0 copy-done
  29.1 0.0 copy-done.1
  29.1 2.2 %prolong_patches.1 = (f32[8,16,512]{2,1,0:T(8,128)}, f32[24,128,256]{2,1,0:T(8,128)}) custom-call(s32[1,24]{1,0:T(1,128)S(4)} %get-tuple-element.24.slots, f32[8,16,256]{2,1,0:T(8,128)S(1)} %get-tuple-element.42.head, bf16[16,64,128]{2,1,0:T(8,128)(2,1)S(1)} %all_to_all.5.arrived, bf16[128,256]{1,0:T(8,128)(2,1)S(1)} %copy-done, ...), custom_call_target="tpu_custom_call" | custom-call | tf_op jit(solution)/shard_map/prolong_patches/pallas_call | solution.py:502
Async XLA Ops:
  0.6 28.5 %copy-start = (bf16[128,256]{1,0:T(8,128)(2,1)S(1)}, bf16[128,256]{1,0:T(8,128)(2,1)}, u32[]{:S(2)}) copy-start(bf16[128,256]{1,0:T(8,128)(2,1)} %constant.5.clone.radial_matrix) | copy-start | bytes 196612
  0.6 28.5 %copy-start.1 = (bf16[128,64]{1,0:T(8,128)(2,1)S(1)}, bf16[128,64]{1,0:T(8,128)(2,1)}, u32[]{:S(2)}) copy-start(bf16[128,64]{1,0:T(8,128)(2,1)} %constant.4.clone.tile_matrix) | copy-start | bytes 49156
  1.9 5.2 %collective-permute-start = (bf16[3,16,512]{2,1,0:T(8,128)(2,1)S(1)}, bf16[3,16,512]{2,1,0:T(8,128)(2,1)S(1)}, u32[]{:S(2)}, u32[]{:S(2)}) collective-permute-start(bf16[3,16,512]{2,1,0:T(8,128)(2,1)S(1)} %get-tuple-element.26), channel_id=1, source_target_pairs={{1,2},{2,1},{3,4},{4,3},{5,6},{6,5},{7,8},{8,7},{9,10},{10,9},{11,... | collective-permute-start | bytes 147464 | tf_op jit(solution)/shard_map/ppermute | solution.py:421
  5.0 4.1 %collective-permute-start.1 = (bf16[3,16,512]{2,1,0:T(8,128)(2,1)S(1)}, bf16[3,16,512]{2,1,0:T(8,128)(2,1)S(1)}, u32[]{:S(2)}, u32[]{:S(2)}) collective-permute-start(bf16[3,16,512]{2,1,0:T(8,128)(2,1)S(1)} %get-tuple-element.27), channel_id=1, source_target_pairs={{0,16},{16,0},{1,17},{17,1},{2,18},{18,2},{3,19},{19,3},{4,20},{20... | collective-permute-start | bytes 147464 | tf_op jit(solution)/shard_map/ppermute | solution.py:420
  5.0 4.0 %collective-permute-start.2 = (bf16[3,16,512]{2,1,0:T(8,128)(2,1)S(1)}, bf16[3,16,512]{2,1,0:T(8,128)(2,1)S(1)}, u32[]{:S(2)}, u32[]{:S(2)}) collective-permute-start(bf16[3,16,512]{2,1,0:T(8,128)(2,1)S(1)} %get-tuple-element.28), channel_id=1, source_target_pairs={{0,1},{1,0},{2,3},{3,2},{4,5},{5,4},{6,7},{7,6},{8,9},{9,8},{10,11... | collective-permute-start | bytes 147464 | tf_op jit(solution)/shard_map/ppermute | solution.py:421
  9.3 4.1 %collective-permute-start.3 = (bf16[5,8,512]{2,1,0:T(8,128)(2,1)S(1)}, bf16[5,8,512]{2,1,0:T(8,128)(2,1)S(1)}, u32[]{:S(2)}, u32[]{:S(2)}) collective-permute-start(bf16[5,8,512]{2,1,0:T(8,128)(2,1)S(1)} %get-tuple-element.37), channel_id=1, source_target_pairs={{1,2},{2,1},{3,4},{4,3},{5,6},{6,5},{7,8},{8,7},{9,10},{10,9},{11,... | collective-permute-start | bytes 122888 | tf_op jit(solution)/shard_map/ppermute | solution.py:421
  10.4 4.0 %collective-permute-start.4 = (bf16[5,8,512]{2,1,0:T(8,128)(2,1)S(1)}, bf16[5,8,512]{2,1,0:T(8,128)(2,1)S(1)}, u32[]{:S(2)}, u32[]{:S(2)}) collective-permute-start(bf16[5,8,512]{2,1,0:T(8,128)(2,1)S(1)} %get-tuple-element.38), channel_id=1, source_target_pairs={{0,16},{16,0},{1,17},{17,1},{2,18},{18,2},{3,19},{19,3},{4,20},{20... | collective-permute-start | bytes 122888 | tf_op jit(solution)/shard_map/ppermute | solution.py:420
  11.4 3.0 %collective-permute-start.5 = (bf16[5,8,512]{2,1,0:T(8,128)(2,1)S(1)}, bf16[5,8,512]{2,1,0:T(8,128)(2,1)S(1)}, u32[]{:S(2)}, u32[]{:S(2)}) collective-permute-start(bf16[5,8,512]{2,1,0:T(8,128)(2,1)S(1)} %get-tuple-element.39), channel_id=1, source_target_pairs={{0,1},{1,0},{2,3},{3,2},{4,5},{5,4},{6,7},{7,6},{8,9},{9,8},{10,11... | collective-permute-start | bytes 122888 | tf_op jit(solution)/shard_map/ppermute | solution.py:421

commit v8 on v7

--- a/solution.py
+++ b/solution.py
@@ -47,6 +47,27 @@
     parts = tile_of(msg, index, (0, 512))
     parts = parts[:, 0:256] + parts[:, 256:512]
     return jnp.concatenate([parts[:, 0:128], parts[:, 128:256]], axis=0)
+
+
+class Either:
+    def __init__(self, chosen, one, other):
+        self.chosen, self.one, self.other, self.shape = chosen, one, other, one.shape
+
+    def __getitem__(self, index):
+        return jnp.where(self.chosen, self.one[index], self.other[index])
+
+
+def crosses():
+    me = lax.axis_index("ax")
+    inside = (me > 0) & (me < lax.axis_size("ax") - 1)
+    return inside & ((lax.rem(me, 4) == 3) | (lax.rem(me, 4) == 0))
+
+
+def parted(count, odd, sector):
+    if count == 3:
+        return odd, *sector
+    one = Either(crosses(), sector[0], odd)
+    return Either(crosses(), odd, sector[0]), one, one, one
 
 
 def write_tiles(out_ref, first, tiles):
@@ -85,7 +106,25 @@
             write_tiles(out_ref, parts * r, [row[8 * part : 8 * part + 8, :] for part in range(parts)])
 
 
-def first_messages(count, *refs):
+def pack(count, tiles, values, courant_z, sector_out, even_out, odd_out):
+    def write(sector_out, odd_out):
+        pack_slab(values, courant_z, even_out, odd_out)
+        pack_sector(tiles, values, sector_out)
+
+    if count == 3:
+        write(sector_out, odd_out)
+        return
+
+    @pl.when(crosses())
+    def _():
+        write(sector_out, odd_out)
+
+    @pl.when(jnp.logical_not(crosses()))
+    def _():
+        write(odd_out, sector_out)
+
+
+def first_messages(sectors, count, *refs):
     given, held = refs[:count], refs[count : 2 * count]
     edges, sector_out, even_out, odd_out, sems = refs[2 * count :]
     copies = [pltpu.make_async_copy(given[i], held[i], sems.at[i]) for i in range(count)]
@@ -94,12 +133,13 @@
     density, courant_t, courant_z = held[:3]
     for copy in copies[:3]:
         copy.wait()
-    pack_slab(density, courant_z, even_out, odd_out)
     cells_t = density.shape[1]
     tiles = [gathered(density, j) for j in (0, 1, cells_t - 2, cells_t - 1)]
     for index, tile in enumerate(tiles):
         edges[index] = tile
-    pack_sector(tiles + [gathered(courant_t, cells_t - 1)], density, sector_out)
+    tiles.append(gathered(courant_t, cells_t - 1))
+
+    pack(sectors, tiles, density, courant_z, sector_out, even_out, odd_out)
     for copy in copies[3:]:
         copy.wait()
 
@@ -253,7 +293,7 @@
     odd, sector, refs = refs[0], refs[1 : 1 + count], refs[1:]
     even, partial, density, edges, faces, courant_r, courant_z = refs[count : count + 7]
     section, section_edges, sector_out, even_out, odd_out = refs[count + 7 :]
-    left, right, across = sector if count == 3 else sector * 3
+    odd, left, right, across = parted(count, odd, sector)
     tiles = finish(
         section,
         partial,
@@ -270,8 +310,7 @@
     )
     for index, tile in enumerate(tiles):
         section_edges[index] = tile
-    pack_sector(tiles, section, sector_out)
-    pack_slab(section, None, even_out, odd_out)
+    pack(count, tiles, section, None, sector_out, even_out, odd_out)
 
 
 def second_head(count, *refs):
@@ -280,7 +319,8 @@
     left_faces, even_faces, odd_faces = refs[count + 7 : count + 10]
     evolved, outgoing, table = refs[count + 10 :]
     rows_z, cells_t, lanes = evolved.shape
-    left, right, across = sector if count == 3 else sector * 3
+    odd, left, right, across = parted(count, odd, sector)
+    odd_faces, left_faces = parted(count, odd_faces, [left_faces] * count)[:2]
     finish(
         evolved,
         partial,
@@ -314,7 +354,8 @@
 def second_tail(count, refs, evolved):
     odd, sector, refs = refs[0], refs[1 : 1 + count], refs[1:]
     even, partial, section, edges, faces, courant_z, left_faces, even_faces, odd_faces = refs[count:]
-    left, right, _ = sector if count == 3 else sector * 3
+    odd, left, right, _ = parted(count, odd, sector)
+    odd_faces, left_faces = parted(count, odd_faces, [left_faces] * count)[:2]
     finish(
         evolved,
         partial,
@@ -416,9 +457,23 @@
     beside = (1,) if az_count == 2 else (1, az_count - 1)
     all_steps = beside if az_count == 2 else beside + (az_count // 2,)
 
+    pairs_one, pairs_two = [], []
+    for a in range(az_count):
+        for i in range(ax_count):
+            end = i in (0, ax_count - 1)
+            far = i % 4 in (0, 3) and not end
+            beside_me = flat(a, ((i - 1) ^ 1) + 1)
+            opposite = flat(a ^ 1, i)
+            pairs_one.append((flat(a, i), beside_me if far else opposite))
+            pairs_two.append((flat(a, i), opposite if far or end else beside_me))
+
     def exchange(sector, even, odd, steps):
-        sectors = [lax.ppermute(sector, "az", by(s)) for s in steps]
-        return sectors, lax.ppermute(even, "ax", even_pairs), lax.ppermute(odd, ("az", "ax"), odd_pairs)
+        if len(steps) == 1:
+            sectors = [lax.ppermute(sector, ("az", "ax"), pairs_two)]
+        else:
+            sectors = [lax.ppermute(sector, "az", by(s)) for s in steps]
+        odd = lax.ppermute(odd, ("az", "ax"), pairs_one if len(steps) == 1 else odd_pairs)
+        return sectors, lax.ppermute(even, "ax", even_pairs), odd
 
     lanes = HEAD_R * BR
     message = jax.ShapeDtypeStruct((rows_z // 4 + 1, cells_t, cells_r), BF16)
@@ -431,7 +486,7 @@
     )
     given = tuple(pltpu.with_memory_space_constraint(x, pltpu.HBM) for x in given)
     *held, edges, sector, even, odd = pl.pallas_call(
-        functools.partial(first_messages, len(given)),
+        functools.partial(first_messages, len(all_steps), len(given)),
         out_shape=tuple(
             pltpu.SMEM(x.shape, x.dtype) if x.dtype == jnp.int32 else jax.ShapeDtypeStruct(x.shape, x.dtype)
             for x in given

time: 31.5 us -> 31.2 us (level)
  waiting for transfers between devices: 4.04 us -> 3.26 us
  starting transfers between devices: 6.45 us -> 6.77 us
    ppermute x6, waiting for transfers between devices: 4.04 us -> 3.26 us  [the longest x2 2.16 us: exchange(): sectors = [lax.ppermute(sector, ('az', 'ax'), pairs_two)]]
    ppermute x6, starting transfers between devices: 6.45 us -> 6.77 us  [the longest x2 3.62 us: exchange(): lax.ppermute(odd, ('az', 'ax'), pairs_one if len(steps) == 1 else odd_pairs)]
where the time goes in v8:
time: 31.2 us; the launch traced here: 31.1 us
  blocking collectives  14.7 us (47%)
  starting transfers between devices  6.77 us (22%)
  Pallas kernels  5.67 us (18%)
  waiting for transfers between devices  3.26 us (10%)
  between operations  0.69 us (2%)
    all_to_all x1, blocking collectives, local(): lax.all_to_all(outgoing, 'ax', split_axis=0, concat_axis=0, tiled=True)  14.7 us
    ppermute x2, starting transfers between devices, exchange(): lax.ppermute(odd, ('az', 'ax'), pairs_one if len(steps) == 1 else odd_pairs)  3.62 us
    ppermute x2, waiting for transfers between devices, exchange(): sectors = [lax.ppermute(sector, ('az', 'ax'), pairs_two)]  2.16 us
    pallas_call x1, Pallas kernels, local(): pl.pallas_call(functools.partial(prolong_patches, count), out_shape=(fiel...  2.15 us
    ppermute x2, starting transfers between devices, exchange(): sectors = [lax.ppermute(sector, ('az', 'ax'), pairs_two)]  1.58 us
    ppermute x2, starting transfers between devices, exchange(): return (sectors, lax.ppermute(even, 'ax', even_pairs), odd)  1.57 us
    pallas_call x1, Pallas kernels, local(): pl.pallas_call(functools.partial(first_messages, len(all_steps), len(give...  1.31 us
    ppermute x2, waiting for transfers between devices, exchange(): lax.ppermute(odd, ('az', 'ax'), pairs_one if len(steps) == 1 else odd_pairs)  1.09 us
  transfers between devices with their start and end apart: 6, of which 3 were waited for; matrix products, arithmetic and copies ran while one was open for 0% of the time, Pallas kernels for 5%

profile of v8, /device:TPU:0, one launch (start us, length us, event | category | flops | bytes accessed | tf_op | source)
XLA Modules:
  0.0 31.1 jit_solution(11767745688234776913)
XLA Ops:
  0.6 0.0 copy-start
  0.6 0.0 copy-start.1
  0.7 1.3 %first_messages.1 = (f32[8,16,512]{2,1,0:T(8,128)S(1)}, bf16[8,16,512]{2,1,0:T(8,128)(2,1)S(1)}, bf16[8,16,512]{2,1,0:T(8,128)(2,1)S(1)}, bf16[8,16,512]{2,1,0:T...) custom-call(f32[8,16,512]{2,1,0:T(8,128)} %refs_0_.1, ...), custom_call_target="tpu_custom_call" | custom-call | tf_op jit(solution)/shard_map/first_messages/pallas_call | solution.py:488
  2.0 3.0 %collective-permute-start = (bf16[3,16,512]{2,1,0:T(8,128)(2,1)S(1)}, bf16[3,16,512]{2,1,0:T(8,128)(2,1)S(1)}, u32[]{:S(2)}, u32[]{:S(2)}) collective-permute-start(bf16[3,16,512]{2,1,0:T(8,128)(2,1)S(1)} %get-tuple-element.26), channel_id=1, source_target_pairs={{0,16},{1,17},{2,18},{3,4},{4,3},{5,21},{6,22},{7,8},{8,7},{9,25},... | collective-permute-start | bytes 147464 | tf_op jit(solution)/shard_map/ppermute | solution.py:475
  5.0 0.1 collective-permute-start.1
  5.1 1.5 %collective-permute-start.2 = (bf16[3,16,512]{2,1,0:T(8,128)(2,1)S(1)}, bf16[3,16,512]{2,1,0:T(8,128)(2,1)S(1)}, u32[]{:S(2)}, u32[]{:S(2)}) collective-permute-start(bf16[3,16,512]{2,1,0:T(8,128)(2,1)S(1)} %get-tuple-element.28), channel_id=1, source_target_pairs={{0,1},{1,0},{2,3},{3,2},{4,5},{5,4},{6,7},{7,6},{8,9},{9,8},{10,11... | collective-permute-start | bytes 147464 | tf_op jit(solution)/shard_map/ppermute | solution.py:476
  6.6 0.8 %first_inner.1 = (f32[8,16,512]{2,1,0:T(8,128)S(1)}, f32[3,8,512]{2,1,0:T(8,128)S(1)}) custom-call(f32[8,16,512]{2,1,0:T(8,128)S(1)} %get-tuple-element.29.density.refs_4_, bf16[8,16,512]{2,1,0:T(8,128)(2,1)S(1)} %get-tuple-element.30.courant_r.refs_7_.refs_8_, bf16[8,16,512]{2,1,0:T(8,128)(2,1)S(1)} %get-tuple-element.31.courant_t, ...), custom_call_target="tpu_custom_call" | custom-call | flops 2621440 | bytes 1048576 | tf_op jit(solution)/shard_map/first_inner/pallas_call | solution.py:506
  7.4 0.0 collective-permute-done.refs_0_.refs_12_.refs_10_
  7.5 1.6 %collective-permute-done.1.refs_1_.refs_10_.refs_8_ = bf16[3,16,512]{2,1,0:T(8,128)(2,1)S(1)} collective-permute-done((bf16[3,16,512]{2,1,0:T(8,128)(2,1)S(1)}, bf16[3,16,512]{2,1,0:T(8,128)(2,1)S(1)}, u32[]{:S(2)}, u32[]{:S(2)}) %collective-permute-start.1) | collective-permute-done | bytes 49184 | tf_op jit(solution)/shard_map/ppermute | solution.py:472
  9.1 0.0 collective-permute-done.2.refs_2_.refs_11_.refs_9_
  9.1 0.3 first_stage.1
  9.4 0.6 %collective-permute-start.3 = (bf16[5,8,512]{2,1,0:T(8,128)(2,1)S(1)}, bf16[5,8,512]{2,1,0:T(8,128)(2,1)S(1)}, u32[]{:S(2)}, u32[]{:S(2)}) collective-permute-start(bf16[5,8,512]{2,1,0:T(8,128)(2,1)S(1)} %get-tuple-element.37), channel_id=1, source_target_pairs={{0,16},{1,17},{2,18},{3,4},{4,3},{5,21},{6,22},{7,8},{8,7},{9,25},... | collective-permute-start | bytes 122888 | tf_op jit(solution)/shard_map/ppermute | solution.py:475
  10.0 1.5 %collective-permute-start.4 = (bf16[5,8,512]{2,1,0:T(8,128)(2,1)S(1)}, bf16[5,8,512]{2,1,0:T(8,128)(2,1)S(1)}, u32[]{:S(2)}, u32[]{:S(2)}) collective-permute-start(bf16[5,8,512]{2,1,0:T(8,128)(2,1)S(1)} %get-tuple-element.38), channel_id=1, source_target_pairs={{0,16},{1,2},{2,1},{3,19},{4,20},{5,6},{6,5},{7,23},{8,24},{9,10},... | collective-permute-start | bytes 122888 | tf_op jit(solution)/shard_map/ppermute | solution.py:472
  11.5 0.0 collective-permute-start.5
  11.5 0.8 %second_inner.1.refs_4_.refs_3_ = f32[8,16,512]{2,1,0:T(8,128)S(1)} custom-call(f32[8,16,512]{2,1,0:T(8,128)S(1)} %get-tuple-element.29.density.refs_4_, f32[8,16,512]{2,1,0:T(8,128)S(1)} %get-tuple-element.40.section.refs_5_.refs_4_, bf16[8,16,512]{2,1,0:T(8,128)(2,1)S(1)} %get-tuple-element.30.courant_r.refs_7_.refs_8_, ...), custom_call_target="tpu_custom_call" | custom-call | flops 2621440 | bytes 1048576 | tf_op jit(solution)/shard_map/second_inner/pallas_call | solution.py:525
  12.4 1.1 %collective-permute-done.3.refs_1_.refs_0_ = bf16[5,8,512]{2,1,0:T(8,128)(2,1)S(1)} collective-permute-done((bf16[5,8,512]{2,1,0:T(8,128)(2,1)S(1)}, bf16[5,8,512]{2,1,0:T(8,128)(2,1)S(1)}, u32[]{:S(2)}, u32[]{:S(2)}) %collective-permute-start.3) | collective-permute-done | bytes 40992 | tf_op jit(solution)/shard_map/ppermute | solution.py:475
  13.5 0.5 %collective-permute-done.4.refs_2_.refs_1_ = bf16[5,8,512]{2,1,0:T(8,128)(2,1)S(1)} collective-permute-done((bf16[5,8,512]{2,1,0:T(8,128)(2,1)S(1)}, bf16[5,8,512]{2,1,0:T(8,128)(2,1)S(1)}, u32[]{:S(2)}, u32[]{:S(2)}) %collective-permute-start.4) | collective-permute-done | bytes 40992 | tf_op jit(solution)/shard_map/ppermute | solution.py:472
  14.0 0.0 collective-permute-done.5.refs_3_.refs_2_
  14.0 0.3 second_head.1
  14.3 14.7 %all_to_all.5.arrived = bf16[16,64,128]{2,1,0:T(8,128)(2,1)S(1)} all-to-all(bf16[16,64,128]{2,1,0:T(8,128)(2,1)S(1)} %get-tuple-element.43), channel_id=1, replica_groups=mesh['az'=2,'ax'=16] {'ax'}, dimensions={0} | all-to-all | bytes 524288 | tf_op jit(solution)/shard_map/all_to_all | solution.py:551
  28.9 0.0 copy-done
  28.9 0.0 copy-done.1
  28.9 2.2 %prolong_patches.1 = (f32[8,16,512]{2,1,0:T(8,128)}, f32[24,128,256]{2,1,0:T(8,128)}) custom-call(s32[1,24]{1,0:T(1,128)S(4)} %get-tuple-element.24.slots, f32[8,16,256]{2,1,0:T(8,128)S(1)} %get-tuple-element.42.head, bf16[16,64,128]{2,1,0:T(8,128)(2,1)S(1)} %all_to_all.5.arrived, bf16[128,256]{1,0:T(8,128)(2,1)S(1)} %copy-done, ...), custom_call_target="tpu_custom_call" | custom-call | tf_op jit(solution)/shard_map/prolong_patches/pallas_call | solution.py:557
Async XLA Ops:
  0.6 28.3 %copy-start = (bf16[128,256]{1,0:T(8,128)(2,1)S(1)}, bf16[128,256]{1,0:T(8,128)(2,1)}, u32[]{:S(2)}) copy-start(bf16[128,256]{1,0:T(8,128)(2,1)} %constant.5.clone.radial_matrix) | copy-start | bytes 196612
  0.6 28.3 %copy-start.1 = (bf16[128,64]{1,0:T(8,128)(2,1)S(1)}, bf16[128,64]{1,0:T(8,128)(2,1)}, u32[]{:S(2)}) copy-start(bf16[128,64]{1,0:T(8,128)(2,1)} %constant.4.clone.tile_matrix) | copy-start | bytes 49156
  2.0 5.5 %collective-permute-start = (bf16[3,16,512]{2,1,0:T(8,128)(2,1)S(1)}, bf16[3,16,512]{2,1,0:T(8,128)(2,1)S(1)}, u32[]{:S(2)}, u32[]{:S(2)}) collective-permute-start(bf16[3,16,512]{2,1,0:T(8,128)(2,1)S(1)} %get-tuple-element.26), channel_id=1, source_target_pairs={{0,16},{1,17},{2,18},{3,4},{4,3},{5,21},{6,22},{7,8},{8,7},{9,25},... | collective-permute-start | bytes 147464 | tf_op jit(solution)/shard_map/ppermute | solution.py:475
  5.0 4.1 %collective-permute-start.1 = (bf16[3,16,512]{2,1,0:T(8,128)(2,1)S(1)}, bf16[3,16,512]{2,1,0:T(8,128)(2,1)S(1)}, u32[]{:S(2)}, u32[]{:S(2)}) collective-permute-start(bf16[3,16,512]{2,1,0:T(8,128)(2,1)S(1)} %get-tuple-element.27), channel_id=1, source_target_pairs={{0,16},{1,2},{2,1},{3,19},{4,20},{5,6},{6,5},{7,23},{8,24},{9,10},... | collective-permute-start | bytes 147464 | tf_op jit(solution)/shard_map/ppermute | solution.py:472
  5.1 4.0 %collective-permute-start.2 = (bf16[3,16,512]{2,1,0:T(8,128)(2,1)S(1)}, bf16[3,16,512]{2,1,0:T(8,128)(2,1)S(1)}, u32[]{:S(2)}, u32[]{:S(2)}) collective-permute-start(bf16[3,16,512]{2,1,0:T(8,128)(2,1)S(1)} %get-tuple-element.28), channel_id=1, source_target_pairs={{0,1},{1,0},{2,3},{3,2},{4,5},{5,4},{6,7},{7,6},{8,9},{9,8},{10,11... | collective-permute-start | bytes 147464 | tf_op jit(solution)/shard_map/ppermute | solution.py:476
  9.4 4.1 %collective-permute-start.3 = (bf16[5,8,512]{2,1,0:T(8,128)(2,1)S(1)}, bf16[5,8,512]{2,1,0:T(8,128)(2,1)S(1)}, u32[]{:S(2)}, u32[]{:S(2)}) collective-permute-start(bf16[5,8,512]{2,1,0:T(8,128)(2,1)S(1)} %get-tuple-element.37), channel_id=1, source_target_pairs={{0,16},{1,17},{2,18},{3,4},{4,3},{5,21},{6,22},{7,8},{8,7},{9,25},... | collective-permute-start | bytes 122888 | tf_op jit(solution)/shard_map/ppermute | solution.py:475
  10.0 4.0 %collective-permute-start.4 = (bf16[5,8,512]{2,1,0:T(8,128)(2,1)S(1)}, bf16[5,8,512]{2,1,0:T(8,128)(2,1)S(1)}, u32[]{:S(2)}, u32[]{:S(2)}) collective-permute-start(bf16[5,8,512]{2,1,0:T(8,128)(2,1)S(1)} %get-tuple-element.38), channel_id=1, source_target_pairs={{0,16},{1,2},{2,1},{3,19},{4,20},{5,6},{6,5},{7,23},{8,24},{9,10},... | collective-permute-start | bytes 122888 | tf_op jit(solution)/shard_map/ppermute | solution.py:472
  11.5 2.5 %collective-permute-start.5 = (bf16[5,8,512]{2,1,0:T(8,128)(2,1)S(1)}, bf16[5,8,512]{2,1,0:T(8,128)(2,1)S(1)}, u32[]{:S(2)}, u32[]{:S(2)}) collective-permute-start(bf16[5,8,512]{2,1,0:T(8,128)(2,1)S(1)} %get-tuple-element.39), channel_id=1, source_target_pairs={{0,1},{1,0},{2,3},{3,2},{4,5},{5,4},{6,7},{7,6},{8,9},{9,8},{10,11... | collective-permute-start | bytes 122888 | tf_op jit(solution)/shard_map/ppermute | solution.py:476

commit v9 on v8

--- a/solution.py
+++ b/solution.py
@@ -394,7 +394,8 @@
         firsts = [2 * BLOCK_ROWS * i for i in range(len(blocks))]
         return [halves(spread[f : f + BLOCK_ROWS] + spread[f + BLOCK_ROWS : f + 2 * BLOCK_ROWS]) for f in firsts]
 
-    groups = [range(p, min(p + GROUP, owned)) for p in range(0, owned, GROUP)]
+    starts = [0, *range(GROUP // 2, owned, GROUP), owned]
+    groups = [range(p, q) for p, q in zip(starts, starts[1:])]
     following = radial(groups[0])
     for g, group in enumerate(groups):
         pairs = following
@@ -562,7 +563,7 @@
         scratch_shapes=[
             pltpu.VMEM((rows_z, cells_t, cells_r - lanes), F32),
             pltpu.VMEM((owned, fine_rows, 2 * BR), F32),
-            pltpu.SemaphoreType.DMA((-(-owned // GROUP) + 2,)),
+            pltpu.SemaphoreType.DMA((-(-owned // GROUP) + 3,)),
         ],
         compiler_params=PARAMS,
         name="prolong_patches",

time: 31.2 us -> 31.3 us (level)
  no operation moved by 1% of the time
where the time goes in v9:
time: 31.3 us; the launch traced here: 31.1 us
  blocking collectives  14.7 us (47%)
  starting transfers between devices  6.77 us (22%)
  Pallas kernels  5.68 us (18%)
  waiting for transfers between devices  3.26 us (10%)
  between operations  0.69 us (2%)
    all_to_all x1, blocking collectives, local(): lax.all_to_all(outgoing, 'ax', split_axis=0, concat_axis=0, tiled=True)  14.7 us
    ppermute x2, starting transfers between devices, exchange(): lax.ppermute(odd, ('az', 'ax'), pairs_one if len(steps) == 1 else odd_pairs)  3.62 us
    ppermute x2, waiting for transfers between devices, exchange(): sectors = [lax.ppermute(sector, ('az', 'ax'), pairs_two)]  2.16 us
    pallas_call x1, Pallas kernels, local(): pl.pallas_call(functools.partial(prolong_patches, count), out_shape=(fiel...  2.16 us
    ppermute x2, starting transfers between devices, exchange(): sectors = [lax.ppermute(sector, ('az', 'ax'), pairs_two)]  1.58 us
    ppermute x2, starting transfers between devices, exchange(): return (sectors, lax.ppermute(even, 'ax', even_pairs), odd)  1.57 us
    pallas_call x1, Pallas kernels, local(): pl.pallas_call(functools.partial(first_messages, len(all_steps), len(give...  1.31 us
    ppermute x2, waiting for transfers between devices, exchange(): lax.ppermute(odd, ('az', 'ax'), pairs_one if len(steps) == 1 else odd_pairs)  1.09 us
  transfers between devices with their start and end apart: 6, of which 3 were waited for; matrix products, arithmetic and copies ran while one was open for 0% of the time, Pallas kernels for 5%

profile of v9, /device:TPU:0, one launch (start us, length us, event | category | flops | bytes accessed | tf_op | source)
XLA Modules:
  0.0 31.1 jit_solution(5123288622986009753)
XLA Ops:
  0.6 0.0 copy-start
  0.6 0.0 copy-start.1
  0.7 1.3 %first_messages.1 = (f32[8,16,512]{2,1,0:T(8,128)S(1)}, bf16[8,16,512]{2,1,0:T(8,128)(2,1)S(1)}, bf16[8,16,512]{2,1,0:T(8,128)(2,1)S(1)}, bf16[8,16,512]{2,1,0:T...) custom-call(f32[8,16,512]{2,1,0:T(8,128)} %refs_0_.1, ...), custom_call_target="tpu_custom_call" | custom-call | tf_op jit(solution)/shard_map/first_messages/pallas_call | solution.py:489
  2.0 3.0 %collective-permute-start = (bf16[3,16,512]{2,1,0:T(8,128)(2,1)S(1)}, bf16[3,16,512]{2,1,0:T(8,128)(2,1)S(1)}, u32[]{:S(2)}, u32[]{:S(2)}) collective-permute-start(bf16[3,16,512]{2,1,0:T(8,128)(2,1)S(1)} %get-tuple-element.26), channel_id=1, source_target_pairs={{0,16},{1,17},{2,18},{3,4},{4,3},{5,21},{6,22},{7,8},{8,7},{9,25},... | collective-permute-start | bytes 147464 | tf_op jit(solution)/shard_map/ppermute | solution.py:476
  5.0 0.1 collective-permute-start.1
  5.1 1.5 %collective-permute-start.2 = (bf16[3,16,512]{2,1,0:T(8,128)(2,1)S(1)}, bf16[3,16,512]{2,1,0:T(8,128)(2,1)S(1)}, u32[]{:S(2)}, u32[]{:S(2)}) collective-permute-start(bf16[3,16,512]{2,1,0:T(8,128)(2,1)S(1)} %get-tuple-element.28), channel_id=1, source_target_pairs={{0,1},{1,0},{2,3},{3,2},{4,5},{5,4},{6,7},{7,6},{8,9},{9,8},{10,11... | collective-permute-start | bytes 147464 | tf_op jit(solution)/shard_map/ppermute | solution.py:477
  6.6 0.8 %first_inner.1 = (f32[8,16,512]{2,1,0:T(8,128)S(1)}, f32[3,8,512]{2,1,0:T(8,128)S(1)}) custom-call(f32[8,16,512]{2,1,0:T(8,128)S(1)} %get-tuple-element.29.density.refs_4_, bf16[8,16,512]{2,1,0:T(8,128)(2,1)S(1)} %get-tuple-element.30.courant_r.refs_7_.refs_8_, bf16[8,16,512]{2,1,0:T(8,128)(2,1)S(1)} %get-tuple-element.31.courant_t, ...), custom_call_target="tpu_custom_call" | custom-call | flops 2621440 | bytes 1048576 | tf_op jit(solution)/shard_map/first_inner/pallas_call | solution.py:507
  7.4 0.0 collective-permute-done.refs_0_.refs_12_.refs_10_
  7.5 1.6 %collective-permute-done.1.refs_1_.refs_10_.refs_8_ = bf16[3,16,512]{2,1,0:T(8,128)(2,1)S(1)} collective-permute-done((bf16[3,16,512]{2,1,0:T(8,128)(2,1)S(1)}, bf16[3,16,512]{2,1,0:T(8,128)(2,1)S(1)}, u32[]{:S(2)}, u32[]{:S(2)}) %collective-permute-start.1) | collective-permute-done | bytes 49184 | tf_op jit(solution)/shard_map/ppermute | solution.py:473
  9.1 0.0 collective-permute-done.2.refs_2_.refs_11_.refs_9_
  9.1 0.3 first_stage.1
  9.4 0.6 %collective-permute-start.3 = (bf16[5,8,512]{2,1,0:T(8,128)(2,1)S(1)}, bf16[5,8,512]{2,1,0:T(8,128)(2,1)S(1)}, u32[]{:S(2)}, u32[]{:S(2)}) collective-permute-start(bf16[5,8,512]{2,1,0:T(8,128)(2,1)S(1)} %get-tuple-element.37), channel_id=1, source_target_pairs={{0,16},{1,17},{2,18},{3,4},{4,3},{5,21},{6,22},{7,8},{8,7},{9,25},... | collective-permute-start | bytes 122888 | tf_op jit(solution)/shard_map/ppermute | solution.py:476
  10.0 1.5 %collective-permute-start.4 = (bf16[5,8,512]{2,1,0:T(8,128)(2,1)S(1)}, bf16[5,8,512]{2,1,0:T(8,128)(2,1)S(1)}, u32[]{:S(2)}, u32[]{:S(2)}) collective-permute-start(bf16[5,8,512]{2,1,0:T(8,128)(2,1)S(1)} %get-tuple-element.38), channel_id=1, source_target_pairs={{0,16},{1,2},{2,1},{3,19},{4,20},{5,6},{6,5},{7,23},{8,24},{9,10},... | collective-permute-start | bytes 122888 | tf_op jit(solution)/shard_map/ppermute | solution.py:473
  11.5 0.0 collective-permute-start.5
  11.5 0.8 %second_inner.1.refs_4_.refs_3_ = f32[8,16,512]{2,1,0:T(8,128)S(1)} custom-call(f32[8,16,512]{2,1,0:T(8,128)S(1)} %get-tuple-element.29.density.refs_4_, f32[8,16,512]{2,1,0:T(8,128)S(1)} %get-tuple-element.40.section.refs_5_.refs_4_, bf16[8,16,512]{2,1,0:T(8,128)(2,1)S(1)} %get-tuple-element.30.courant_r.refs_7_.refs_8_, ...), custom_call_target="tpu_custom_call" | custom-call | flops 2621440 | bytes 1048576 | tf_op jit(solution)/shard_map/second_inner/pallas_call | solution.py:526
  12.4 1.1 %collective-permute-done.3.refs_1_.refs_0_ = bf16[5,8,512]{2,1,0:T(8,128)(2,1)S(1)} collective-permute-done((bf16[5,8,512]{2,1,0:T(8,128)(2,1)S(1)}, bf16[5,8,512]{2,1,0:T(8,128)(2,1)S(1)}, u32[]{:S(2)}, u32[]{:S(2)}) %collective-permute-start.3) | collective-permute-done | bytes 40992 | tf_op jit(solution)/shard_map/ppermute | solution.py:476
  13.5 0.5 %collective-permute-done.4.refs_2_.refs_1_ = bf16[5,8,512]{2,1,0:T(8,128)(2,1)S(1)} collective-permute-done((bf16[5,8,512]{2,1,0:T(8,128)(2,1)S(1)}, bf16[5,8,512]{2,1,0:T(8,128)(2,1)S(1)}, u32[]{:S(2)}, u32[]{:S(2)}) %collective-permute-start.4) | collective-permute-done | bytes 40992 | tf_op jit(solution)/shard_map/ppermute | solution.py:473
  14.0 0.0 collective-permute-done.5.refs_3_.refs_2_
  14.0 0.3 second_head.1
  14.3 14.7 %all_to_all.5.arrived = bf16[16,64,128]{2,1,0:T(8,128)(2,1)S(1)} all-to-all(bf16[16,64,128]{2,1,0:T(8,128)(2,1)S(1)} %get-tuple-element.43), channel_id=1, replica_groups=mesh['az'=2,'ax'=16] {'ax'}, dimensions={0} | all-to-all | bytes 524288 | tf_op jit(solution)/shard_map/all_to_all | solution.py:552
  28.9 0.0 copy-done
  28.9 0.0 copy-done.1
  28.9 2.2 %prolong_patches.1 = (f32[8,16,512]{2,1,0:T(8,128)}, f32[24,128,256]{2,1,0:T(8,128)}) custom-call(s32[1,24]{1,0:T(1,128)S(4)} %get-tuple-element.24.slots, f32[8,16,256]{2,1,0:T(8,128)S(1)} %get-tuple-element.42.head, bf16[16,64,128]{2,1,0:T(8,128)(2,1)S(1)} %all_to_all.5.arrived, bf16[128,256]{1,0:T(8,128)(2,1)S(1)} %copy-done, ...), custom_call_target="tpu_custom_call" | custom-call | tf_op jit(solution)/shard_map/prolong_patches/pallas_call | solution.py:558
Async XLA Ops:
  0.6 28.3 %copy-start = (bf16[128,256]{1,0:T(8,128)(2,1)S(1)}, bf16[128,256]{1,0:T(8,128)(2,1)}, u32[]{:S(2)}) copy-start(bf16[128,256]{1,0:T(8,128)(2,1)} %constant.5.clone.radial_matrix) | copy-start | bytes 196612
  0.6 28.3 %copy-start.1 = (bf16[128,64]{1,0:T(8,128)(2,1)S(1)}, bf16[128,64]{1,0:T(8,128)(2,1)}, u32[]{:S(2)}) copy-start(bf16[128,64]{1,0:T(8,128)(2,1)} %constant.4.clone.tile_matrix) | copy-start | bytes 49156
  2.0 5.5 %collective-permute-start = (bf16[3,16,512]{2,1,0:T(8,128)(2,1)S(1)}, bf16[3,16,512]{2,1,0:T(8,128)(2,1)S(1)}, u32[]{:S(2)}, u32[]{:S(2)}) collective-permute-start(bf16[3,16,512]{2,1,0:T(8,128)(2,1)S(1)} %get-tuple-element.26), channel_id=1, source_target_pairs={{0,16},{1,17},{2,18},{3,4},{4,3},{5,21},{6,22},{7,8},{8,7},{9,25},... | collective-permute-start | bytes 147464 | tf_op jit(solution)/shard_map/ppermute | solution.py:476
  5.0 4.1 %collective-permute-start.1 = (bf16[3,16,512]{2,1,0:T(8,128)(2,1)S(1)}, bf16[3,16,512]{2,1,0:T(8,128)(2,1)S(1)}, u32[]{:S(2)}, u32[]{:S(2)}) collective-permute-start(bf16[3,16,512]{2,1,0:T(8,128)(2,1)S(1)} %get-tuple-element.27), channel_id=1, source_target_pairs={{0,16},{1,2},{2,1},{3,19},{4,20},{5,6},{6,5},{7,23},{8,24},{9,10},... | collective-permute-start | bytes 147464 | tf_op jit(solution)/shard_map/ppermute | solution.py:473
  5.1 4.0 %collective-permute-start.2 = (bf16[3,16,512]{2,1,0:T(8,128)(2,1)S(1)}, bf16[3,16,512]{2,1,0:T(8,128)(2,1)S(1)}, u32[]{:S(2)}, u32[]{:S(2)}) collective-permute-start(bf16[3,16,512]{2,1,0:T(8,128)(2,1)S(1)} %get-tuple-element.28), channel_id=1, source_target_pairs={{0,1},{1,0},{2,3},{3,2},{4,5},{5,4},{6,7},{7,6},{8,9},{9,8},{10,11... | collective-permute-start | bytes 147464 | tf_op jit(solution)/shard_map/ppermute | solution.py:477
  9.4 4.1 %collective-permute-start.3 = (bf16[5,8,512]{2,1,0:T(8,128)(2,1)S(1)}, bf16[5,8,512]{2,1,0:T(8,128)(2,1)S(1)}, u32[]{:S(2)}, u32[]{:S(2)}) collective-permute-start(bf16[5,8,512]{2,1,0:T(8,128)(2,1)S(1)} %get-tuple-element.37), channel_id=1, source_target_pairs={{0,16},{1,17},{2,18},{3,4},{4,3},{5,21},{6,22},{7,8},{8,7},{9,25},... | collective-permute-start | bytes 122888 | tf_op jit(solution)/shard_map/ppermute | solution.py:476
  10.0 4.0 %collective-permute-start.4 = (bf16[5,8,512]{2,1,0:T(8,128)(2,1)S(1)}, bf16[5,8,512]{2,1,0:T(8,128)(2,1)S(1)}, u32[]{:S(2)}, u32[]{:S(2)}) collective-permute-start(bf16[5,8,512]{2,1,0:T(8,128)(2,1)S(1)} %get-tuple-element.38), channel_id=1, source_target_pairs={{0,16},{1,2},{2,1},{3,19},{4,20},{5,6},{6,5},{7,23},{8,24},{9,10},... | collective-permute-start | bytes 122888 | tf_op jit(solution)/shard_map/ppermute | solution.py:473
  11.5 2.5 %collective-permute-start.5 = (bf16[5,8,512]{2,1,0:T(8,128)(2,1)S(1)}, bf16[5,8,512]{2,1,0:T(8,128)(2,1)S(1)}, u32[]{:S(2)}, u32[]{:S(2)}) collective-permute-start(bf16[5,8,512]{2,1,0:T(8,128)(2,1)S(1)} %get-tuple-element.39), channel_id=1, source_target_pairs={{0,1},{1,0},{2,3},{3,2},{4,5},{5,4},{6,7},{7,6},{8,9},{9,8},{10,11... | collective-permute-start | bytes 122888 | tf_op jit(solution)/shard_map/ppermute | solution.py:477

commit v10 on v9

--- a/solution.py
+++ b/solution.py
@@ -394,7 +394,7 @@
         firsts = [2 * BLOCK_ROWS * i for i in range(len(blocks))]
         return [halves(spread[f : f + BLOCK_ROWS] + spread[f + BLOCK_ROWS : f + 2 * BLOCK_ROWS]) for f in firsts]
 
-    starts = [0, *range(GROUP // 2, owned, GROUP), owned]
+    starts = [0, 1, *range(GROUP, owned, GROUP), owned]
     groups = [range(p, q) for p, q in zip(starts, starts[1:])]
     following = radial(groups[0])
     for g, group in enumerate(groups):

time: 31.3 us -> 31.3 us (level)
  no operation moved by 1% of the time
where the time goes in v10:
time: 31.3 us; the launch traced here: 31.1 us
  blocking collectives  14.7 us (47%)
  starting transfers between devices  6.77 us (22%)
  Pallas kernels  5.72 us (18%)
  waiting for transfers between devices  3.26 us (10%)
  between operations  0.69 us (2%)
    all_to_all x1, blocking collectives, local(): lax.all_to_all(outgoing, 'ax', split_axis=0, concat_axis=0, tiled=True)  14.7 us
    ppermute x2, starting transfers between devices, exchange(): lax.ppermute(odd, ('az', 'ax'), pairs_one if len(steps) == 1 else odd_pairs)  3.62 us
    pallas_call x1, Pallas kernels, local(): pl.pallas_call(functools.partial(prolong_patches, count), out_shape=(fiel...  2.2 us
    ppermute x2, waiting for transfers between devices, exchange(): sectors = [lax.ppermute(sector, ('az', 'ax'), pairs_two)]  2.16 us
    ppermute x2, starting transfers between devices, exchange(): sectors = [lax.ppermute(sector, ('az', 'ax'), pairs_two)]  1.58 us
    ppermute x2, starting transfers between devices, exchange(): return (sectors, lax.ppermute(even, 'ax', even_pairs), odd)  1.57 us
    pallas_call x1, Pallas kernels, local(): pl.pallas_call(functools.partial(first_messages, len(all_steps), len(give...  1.31 us
    ppermute x2, waiting for transfers between devices, exchange(): lax.ppermute(odd, ('az', 'ax'), pairs_one if len(steps) == 1 else odd_pairs)  1.09 us
  transfers between devices with their start and end apart: 6, of which 3 were waited for; matrix products, arithmetic and copies ran while one was open for 0% of the time, Pallas kernels for 5%

profile of v10, /device:TPU:0, one launch (start us, length us, event | category | flops | bytes accessed | tf_op | source)
XLA Modules:
  0.0 31.1 jit_solution(57066391531808976)
XLA Ops:
  0.6 0.0 copy-start
  0.6 0.0 copy-start.1
  0.7 1.3 %first_messages.1 = (f32[8,16,512]{2,1,0:T(8,128)S(1)}, bf16[8,16,512]{2,1,0:T(8,128)(2,1)S(1)}, bf16[8,16,512]{2,1,0:T(8,128)(2,1)S(1)}, bf16[8,16,512]{2,1,0:T...) custom-call(f32[8,16,512]{2,1,0:T(8,128)} %refs_0_.1, ...), custom_call_target="tpu_custom_call" | custom-call | tf_op jit(solution)/shard_map/first_messages/pallas_call | solution.py:489
  2.0 3.0 %collective-permute-start = (bf16[3,16,512]{2,1,0:T(8,128)(2,1)S(1)}, bf16[3,16,512]{2,1,0:T(8,128)(2,1)S(1)}, u32[]{:S(2)}, u32[]{:S(2)}) collective-permute-start(bf16[3,16,512]{2,1,0:T(8,128)(2,1)S(1)} %get-tuple-element.26), channel_id=1, source_target_pairs={{0,16},{1,17},{2,18},{3,4},{4,3},{5,21},{6,22},{7,8},{8,7},{9,25},... | collective-permute-start | bytes 147464 | tf_op jit(solution)/shard_map/ppermute | solution.py:476
  5.0 0.1 collective-permute-start.1
  5.1 1.5 %collective-permute-start.2 = (bf16[3,16,512]{2,1,0:T(8,128)(2,1)S(1)}, bf16[3,16,512]{2,1,0:T(8,128)(2,1)S(1)}, u32[]{:S(2)}, u32[]{:S(2)}) collective-permute-start(bf16[3,16,512]{2,1,0:T(8,128)(2,1)S(1)} %get-tuple-element.28), channel_id=1, source_target_pairs={{0,1},{1,0},{2,3},{3,2},{4,5},{5,4},{6,7},{7,6},{8,9},{9,8},{10,11... | collective-permute-start | bytes 147464 | tf_op jit(solution)/shard_map/ppermute | solution.py:477
  6.6 0.8 %first_inner.1 = (f32[8,16,512]{2,1,0:T(8,128)S(1)}, f32[3,8,512]{2,1,0:T(8,128)S(1)}) custom-call(f32[8,16,512]{2,1,0:T(8,128)S(1)} %get-tuple-element.29.density.refs_4_, bf16[8,16,512]{2,1,0:T(8,128)(2,1)S(1)} %get-tuple-element.30.courant_r.refs_7_.refs_8_, bf16[8,16,512]{2,1,0:T(8,128)(2,1)S(1)} %get-tuple-element.31.courant_t, ...), custom_call_target="tpu_custom_call" | custom-call | flops 2621440 | bytes 1048576 | tf_op jit(solution)/shard_map/first_inner/pallas_call | solution.py:507
  7.4 0.0 collective-permute-done.refs_0_.refs_12_.refs_10_
  7.5 1.6 %collective-permute-done.1.refs_1_.refs_10_.refs_8_ = bf16[3,16,512]{2,1,0:T(8,128)(2,1)S(1)} collective-permute-done((bf16[3,16,512]{2,1,0:T(8,128)(2,1)S(1)}, bf16[3,16,512]{2,1,0:T(8,128)(2,1)S(1)}, u32[]{:S(2)}, u32[]{:S(2)}) %collective-permute-start.1) | collective-permute-done | bytes 49184 | tf_op jit(solution)/shard_map/ppermute | solution.py:473
  9.1 0.0 collective-permute-done.2.refs_2_.refs_11_.refs_9_
  9.1 0.3 first_stage.1
  9.4 0.6 %collective-permute-start.3 = (bf16[5,8,512]{2,1,0:T(8,128)(2,1)S(1)}, bf16[5,8,512]{2,1,0:T(8,128)(2,1)S(1)}, u32[]{:S(2)}, u32[]{:S(2)}) collective-permute-start(bf16[5,8,512]{2,1,0:T(8,128)(2,1)S(1)} %get-tuple-element.37), channel_id=1, source_target_pairs={{0,16},{1,17},{2,18},{3,4},{4,3},{5,21},{6,22},{7,8},{8,7},{9,25},... | collective-permute-start | bytes 122888 | tf_op jit(solution)/shard_map/ppermute | solution.py:476
  10.0 1.5 %collective-permute-start.4 = (bf16[5,8,512]{2,1,0:T(8,128)(2,1)S(1)}, bf16[5,8,512]{2,1,0:T(8,128)(2,1)S(1)}, u32[]{:S(2)}, u32[]{:S(2)}) collective-permute-start(bf16[5,8,512]{2,1,0:T(8,128)(2,1)S(1)} %get-tuple-element.38), channel_id=1, source_target_pairs={{0,16},{1,2},{2,1},{3,19},{4,20},{5,6},{6,5},{7,23},{8,24},{9,10},... | collective-permute-start | bytes 122888 | tf_op jit(solution)/shard_map/ppermute | solution.py:473
  11.5 0.0 collective-permute-start.5
  11.5 0.8 %second_inner.1.refs_4_.refs_3_ = f32[8,16,512]{2,1,0:T(8,128)S(1)} custom-call(f32[8,16,512]{2,1,0:T(8,128)S(1)} %get-tuple-element.29.density.refs_4_, f32[8,16,512]{2,1,0:T(8,128)S(1)} %get-tuple-element.40.section.refs_5_.refs_4_, bf16[8,16,512]{2,1,0:T(8,128)(2,1)S(1)} %get-tuple-element.30.courant_r.refs_7_.refs_8_, ...), custom_call_target="tpu_custom_call" | custom-call | flops 2621440 | bytes 1048576 | tf_op jit(solution)/shard_map/second_inner/pallas_call | solution.py:526
  12.4 1.1 %collective-permute-done.3.refs_1_.refs_0_ = bf16[5,8,512]{2,1,0:T(8,128)(2,1)S(1)} collective-permute-done((bf16[5,8,512]{2,1,0:T(8,128)(2,1)S(1)}, bf16[5,8,512]{2,1,0:T(8,128)(2,1)S(1)}, u32[]{:S(2)}, u32[]{:S(2)}) %collective-permute-start.3) | collective-permute-done | bytes 40992 | tf_op jit(solution)/shard_map/ppermute | solution.py:476
  13.5 0.5 %collective-permute-done.4.refs_2_.refs_1_ = bf16[5,8,512]{2,1,0:T(8,128)(2,1)S(1)} collective-permute-done((bf16[5,8,512]{2,1,0:T(8,128)(2,1)S(1)}, bf16[5,8,512]{2,1,0:T(8,128)(2,1)S(1)}, u32[]{:S(2)}, u32[]{:S(2)}) %collective-permute-start.4) | collective-permute-done | bytes 40992 | tf_op jit(solution)/shard_map/ppermute | solution.py:473
  14.0 0.0 collective-permute-done.5.refs_3_.refs_2_
  14.0 0.3 second_head.1
  14.3 14.7 %all_to_all.5.arrived = bf16[16,64,128]{2,1,0:T(8,128)(2,1)S(1)} all-to-all(bf16[16,64,128]{2,1,0:T(8,128)(2,1)S(1)} %get-tuple-element.43), channel_id=1, replica_groups=mesh['az'=2,'ax'=16] {'ax'}, dimensions={0} | all-to-all | bytes 524288 | tf_op jit(solution)/shard_map/all_to_all | solution.py:552
  28.9 0.0 copy-done
  28.9 0.0 copy-done.1
  28.9 2.2 %prolong_patches.1 = (f32[8,16,512]{2,1,0:T(8,128)}, f32[24,128,256]{2,1,0:T(8,128)}) custom-call(s32[1,24]{1,0:T(1,128)S(4)} %get-tuple-element.24.slots, f32[8,16,256]{2,1,0:T(8,128)S(1)} %get-tuple-element.42.head, bf16[16,64,128]{2,1,0:T(8,128)(2,1)S(1)} %all_to_all.5.arrived, bf16[128,256]{1,0:T(8,128)(2,1)S(1)} %copy-done, ...), custom_call_target="tpu_custom_call" | custom-call | tf_op jit(solution)/shard_map/prolong_patches/pallas_call | solution.py:558
Async XLA Ops:
  0.6 28.3 %copy-start = (bf16[128,256]{1,0:T(8,128)(2,1)S(1)}, bf16[128,256]{1,0:T(8,128)(2,1)}, u32[]{:S(2)}) copy-start(bf16[128,256]{1,0:T(8,128)(2,1)} %constant.5.clone.radial_matrix) | copy-start | bytes 196612
  0.6 28.3 %copy-start.1 = (bf16[128,64]{1,0:T(8,128)(2,1)S(1)}, bf16[128,64]{1,0:T(8,128)(2,1)}, u32[]{:S(2)}) copy-start(bf16[128,64]{1,0:T(8,128)(2,1)} %constant.4.clone.tile_matrix) | copy-start | bytes 49156
  2.0 5.5 %collective-permute-start = (bf16[3,16,512]{2,1,0:T(8,128)(2,1)S(1)}, bf16[3,16,512]{2,1,0:T(8,128)(2,1)S(1)}, u32[]{:S(2)}, u32[]{:S(2)}) collective-permute-start(bf16[3,16,512]{2,1,0:T(8,128)(2,1)S(1)} %get-tuple-element.26), channel_id=1, source_target_pairs={{0,16},{1,17},{2,18},{3,4},{4,3},{5,21},{6,22},{7,8},{8,7},{9,25},... | collective-permute-start | bytes 147464 | tf_op jit(solution)/shard_map/ppermute | solution.py:476
  5.0 4.1 %collective-permute-start.1 = (bf16[3,16,512]{2,1,0:T(8,128)(2,1)S(1)}, bf16[3,16,512]{2,1,0:T(8,128)(2,1)S(1)}, u32[]{:S(2)}, u32[]{:S(2)}) collective-permute-start(bf16[3,16,512]{2,1,0:T(8,128)(2,1)S(1)} %get-tuple-element.27), channel_id=1, source_target_pairs={{0,16},{1,2},{2,1},{3,19},{4,20},{5,6},{6,5},{7,23},{8,24},{9,10},... | collective-permute-start | bytes 147464 | tf_op jit(solution)/shard_map/ppermute | solution.py:473
  5.1 4.0 %collective-permute-start.2 = (bf16[3,16,512]{2,1,0:T(8,128)(2,1)S(1)}, bf16[3,16,512]{2,1,0:T(8,128)(2,1)S(1)}, u32[]{:S(2)}, u32[]{:S(2)}) collective-permute-start(bf16[3,16,512]{2,1,0:T(8,128)(2,1)S(1)} %get-tuple-element.28), channel_id=1, source_target_pairs={{0,1},{1,0},{2,3},{3,2},{4,5},{5,4},{6,7},{7,6},{8,9},{9,8},{10,11... | collective-permute-start | bytes 147464 | tf_op jit(solution)/shard_map/ppermute | solution.py:477
  9.4 4.1 %collective-permute-start.3 = (bf16[5,8,512]{2,1,0:T(8,128)(2,1)S(1)}, bf16[5,8,512]{2,1,0:T(8,128)(2,1)S(1)}, u32[]{:S(2)}, u32[]{:S(2)}) collective-permute-start(bf16[5,8,512]{2,1,0:T(8,128)(2,1)S(1)} %get-tuple-element.37), channel_id=1, source_target_pairs={{0,16},{1,17},{2,18},{3,4},{4,3},{5,21},{6,22},{7,8},{8,7},{9,25},... | collective-permute-start | bytes 122888 | tf_op jit(solution)/shard_map/ppermute | solution.py:476
  10.0 4.0 %collective-permute-start.4 = (bf16[5,8,512]{2,1,0:T(8,128)(2,1)S(1)}, bf16[5,8,512]{2,1,0:T(8,128)(2,1)S(1)}, u32[]{:S(2)}, u32[]{:S(2)}) collective-permute-start(bf16[5,8,512]{2,1,0:T(8,128)(2,1)S(1)} %get-tuple-element.38), channel_id=1, source_target_pairs={{0,16},{1,2},{2,1},{3,19},{4,20},{5,6},{6,5},{7,23},{8,24},{9,10},... | collective-permute-start | bytes 122888 | tf_op jit(solution)/shard_map/ppermute | solution.py:473
  11.5 2.5 %collective-permute-start.5 = (bf16[5,8,512]{2,1,0:T(8,128)(2,1)S(1)}, bf16[5,8,512]{2,1,0:T(8,128)(2,1)S(1)}, u32[]{:S(2)}, u32[]{:S(2)}) collective-permute-start(bf16[5,8,512]{2,1,0:T(8,128)(2,1)S(1)} %get-tuple-element.39), channel_id=1, source_target_pairs={{0,1},{1,0},{2,3},{3,2},{4,5},{5,4},{6,7},{7,6},{8,9},{9,8},{10,11... | collective-permute-start | bytes 122888 | tf_op jit(solution)/shard_map/ppermute | solution.py:477
